TPU v7x, 32 devices: a whole 2x2x4 slice. The times are simulated.
32 devices in a mesh: dp: 2 (over x), expert: 4 (over y, core), tensor: 4 (over z).
Axes of the slice: x: 2, y: 2, z: 4, core: 2. Of those that a mesh axis runs over, the one named last changes fastest.
Arguments:
- hidden_in: bfloat16 [1024, 1024], P(('dp', 'expert')), may hold values from -6 to 6
- seq_lengths: int32 [8, 3], P(('dp', 'expert')), may hold values from 1 to 96, 128 in all within a row
- expert_routes: int32 [1024, 8], P(('dp', 'expert')), may hold values from 0 to 31, all different within a row; in each aligned block of 128 rows (0 to 127, 128 to 255, ...) at most 48 rows name the same one
- first_gain: bfloat16 [1024], replicated, may hold values from 0.5 to 1.5
- query_weight: bfloat16 [1024, 1024], P(None, 'tensor'), may hold values from -0.1875 to 0.1875
- key_weight: bfloat16 [1024, 512], P(None, 'tensor'), may hold values from -0.1875 to 0.1875
- value_weight: bfloat16 [1024, 512], P(None, 'tensor'), may hold values from -0.1875 to 0.1875
- output_weight: bfloat16 [1024, 1024], P(None, 'tensor'), may hold values from -0.5 to 0.5
- second_gain: bfloat16 [1024], replicated, may hold values from 0.5 to 1.5
- router_weight: bfloat16 [1024, 32], replicated, may hold values from -0.09375 to 0.09375
- gate_weight: bfloat16 [32, 1024, 512], P('expert', None, 'tensor'), may hold values from -0.1875 to 0.1875
- up_weight: bfloat16 [32, 1024, 512], P('expert', None, 'tensor'), may hold values from -0.1875 to 0.1875
- down_weight: bfloat16 [32, 1024, 512], P('expert', None, 'tensor'), may hold values from -1 to 1
- grad_layer_out: bfloat16 [1024, 1024], P(('dp', 'expert')), may hold values from -6 to 6
Outputs:
- layer_out: bfloat16 [1024, 1024], P(('dp', 'expert'))
- grad_input: float32 [1024, 1024], P(('dp', 'expert'))
- grad_first_gain: float32 [1024], P(('dp', 'expert'))
- grad_query: float32 [1024, 1024], P(('dp', 'expert'), 'tensor')
- grad_key: float32 [1024, 512], P(('dp', 'expert'), 'tensor')
- grad_value: float32 [1024, 512], P(('dp', 'expert'), 'tensor')
- grad_outproj: float32 [1024, 1024], P(('dp', 'expert'), 'tensor')
- grad_second_gain: float32 [1024], P(('dp', 'expert'))
- grad_router: float32 [1024, 32], P(('dp', 'expert'))
- grad_gate: float32 [32, 1024, 512], P('expert', 'dp', 'tensor')
- grad_upproj: float32 [32, 1024, 512], P('expert', 'dp', 'tensor')
- grad_down: float32 [32, 1024, 512], P('expert', 'dp', 'tensor')
Inputs may be any that keep to these rules, and one draw needn't show every extreme that they name: `expert_routes`: among the 128 rows of one token group, each expert is named at most 48 times.
All inputs are finite; a program needn't handle non-finite values.
Results may differ from a plain program's by a relative error of at most 0.017.
Values may be sent and summed in bfloat16 or wider, within the bound.
No kernel may reach another device: no remote copies, remote signals or barrier semaphores. Data moves between devices by JAX's collectives and lax.ppermute only.
A program may use at most 128 MiB of HBM per device.

v0:
```python
import math

import jax
import jax.numpy as jnp
from jax import lax
from jax.sharding import PartitionSpec as P

HD = 64
CAP = 48


EPSILON = 1e-06


def rope_tables(positions, head_size):
    inverse = jnp.exp(
        jnp.arange(head_size // 2).astype(jnp.float32) * (-2.0 * math.log(10000.0) / head_size)
    )
    angles = positions.astype(jnp.float32)[:, None] * inverse[None, :]
    return (jnp.cos(angles)[:, None, :], jnp.sin(angles)[:, None, :])


def rotate(values, cosine_table, sine_table):
    half_size = values.shape[-1] // 2
    lower_half = values[..., :half_size]
    upper_half = values[..., half_size:]
    return jnp.concatenate(
        [
            lower_half * cosine_table - upper_half * sine_table,
            upper_half * cosine_table + lower_half * sine_table,
        ],
        -1,
    )


def rotate_back(gradient, cosine_table, sine_table):
    half_size = gradient.shape[-1] // 2
    lower_half = gradient[..., :half_size]
    upper_half = gradient[..., half_size:]
    return jnp.concatenate(
        [
            lower_half * cosine_table + upper_half * sine_table,
            upper_half * cosine_table - lower_half * sine_table,
        ],
        -1,
    )


def positions_of(lengths_row, row_ids):
    ends_at = jnp.cumsum(lengths_row, dtype=jnp.int32)
    segment = jnp.sum((row_ids[:, None] >= ends_at[None, :]).astype(jnp.int32), 1, dtype=jnp.int32)
    starts_at = ends_at - lengths_row
    chosen = segment[:, None] == jnp.arange(lengths_row.shape[0], dtype=jnp.int32)[None, :]
    start_row = jnp.sum(jnp.where(chosen, starts_at[None, :], 0), 1, dtype=jnp.int32)
    return (segment, row_ids - start_row)


def contract_rows(left, right):
    return lax.dot_general(
        left, right, (((0,), (0,)), ((), ())), preferred_element_type=jnp.float32
    )


def contract_cols(left, right):
    return lax.dot_general(
        left, right, (((1,), (1,)), ((), ())), preferred_element_type=jnp.float32
    )


def on_device(
    hidden_in,
    seq_lengths,
    expert_routes,
    first_gain,
    query_weight,
    key_weight,
    value_weight,
    output_weight,
    second_gain,
    router_weight,
    gate_weight,
    up_weight,
    down_weight,
    grad_layer_out,
):
    tokens_here = hidden_in.shape[0]
    model_width = hidden_in.shape[1]
    head_size = HD
    query_heads = query_weight.shape[1] // head_size
    kv_heads = key_weight.shape[1] // head_size
    group_size = query_heads // kv_heads
    expert_count = router_weight.shape[1]
    top_count = expert_routes.shape[1]
    capacity = CAP
    expert_devices = lax.axis_size("expert")
    local_experts = gate_weight.shape[0]
    score_scale = HD ** (-0.5)
    hidden_float = hidden_in.astype(jnp.float32)
    grad_float = grad_layer_out.astype(jnp.float32)
    first_scale = lax.rsqrt(jnp.mean(hidden_float * hidden_float, -1, keepdims=True) + EPSILON)
    first_hat = hidden_float * first_scale
    first_float = first_gain.astype(jnp.float32)
    first_normed = (first_hat * first_float).astype(jnp.bfloat16)
    row_ids = jnp.arange(tokens_here, dtype=jnp.int32)
    segment, positions = positions_of(seq_lengths[0], row_ids)
    cosine_table, sine_table = rope_tables(positions, head_size)
    query_pre = jnp.dot(first_normed, query_weight, preferred_element_type=jnp.float32).reshape(
        tokens_here, query_heads, head_size
    )
    key_pre = jnp.dot(first_normed, key_weight, preferred_element_type=jnp.float32).reshape(
        tokens_here, kv_heads, head_size
    )
    queries = rotate(query_pre, cosine_table, sine_table).astype(jnp.bfloat16)
    keys_rot = rotate(key_pre, cosine_table, sine_table).astype(jnp.bfloat16)
    values_low = (
        jnp.dot(first_normed, value_weight, preferred_element_type=jnp.float32)
        .astype(jnp.bfloat16)
        .reshape(tokens_here, kv_heads, head_size)
    )
    grouped = queries.reshape(tokens_here, kv_heads, group_size, head_size)
    scores = (
        jnp.einsum("tkgd,ukd->kgtu", grouped, keys_rot, preferred_element_type=jnp.float32)
        * score_scale
    )
    allowed = (segment[:, None] == segment[None, :]) & (row_ids[None, :] <= row_ids[:, None])
    masked = jnp.where(allowed, scores, -1e30)
    top_score = jnp.max(masked, -1, keepdims=True)
    exponent = jnp.exp(masked - top_score)
    probabilities = exponent / jnp.sum(exponent, -1, keepdims=True)
    probs_low = probabilities.astype(jnp.bfloat16)
    attended = (
        jnp.einsum("kgtu,ukd->tkgd", probs_low, values_low, preferred_element_type=jnp.float32)
        .astype(jnp.bfloat16)
        .reshape(tokens_here, query_heads * head_size)
    )
    attn_part = contract_cols(attended, output_weight)
    attn_out = lax.psum(attn_part, "tensor")
    residual = hidden_float + attn_out
    second_scale = lax.rsqrt(jnp.mean(residual * residual, -1, keepdims=True) + EPSILON)
    second_hat = residual * second_scale
    second_float = second_gain.astype(jnp.float32)
    second_normed = (second_hat * second_float).astype(jnp.bfloat16)
    logits = jnp.dot(second_normed, router_weight, preferred_element_type=jnp.float32)
    expert_ids = jnp.arange(expert_count, dtype=jnp.int32)
    picked = expert_routes[:, :, None] == expert_ids[None, None, :]
    route_logits = jnp.sum(jnp.where(picked, logits[:, None, :], 0.0), -1)
    route_gates = jax.nn.softmax(route_logits, -1)
    flat_experts = expert_routes.reshape(-1)
    route_count = flat_experts.shape[0]
    onehot_flat = (flat_experts[:, None] == expert_ids[None, :]).astype(jnp.int32)
    before = jnp.cumsum(onehot_flat, 0, dtype=jnp.int32) - onehot_flat
    slot_index = jnp.sum(before * onehot_flat, 1, dtype=jnp.int32)
    destination = flat_experts * capacity + slot_index
    route_token = jnp.arange(route_count, dtype=jnp.int32) // top_count
    slot_token = (
        jnp.full((expert_count * capacity,), -1, jnp.int32).at[destination].set(route_token)
    )
    slot_live = slot_token >= 0

    def send_owners(slot_rows):
        gotten = lax.all_to_all(
            slot_rows.reshape(expert_devices, local_experts * capacity, model_width),
            "expert",
            split_axis=0,
            concat_axis=0,
            tiled=True,
        )
        return gotten.reshape(expert_devices, local_experts, capacity, model_width)

    def send_tokens(expert_terms):
        brought = lax.all_to_all(
            expert_terms.reshape(expert_devices, local_experts * capacity, model_width),
            "expert",
            split_axis=0,
            concat_axis=0,
            tiled=True,
        )
        width_now = brought.shape[2]
        return brought.reshape(expert_count * capacity, width_now)[destination].reshape(
            tokens_here, top_count, width_now
        )

    send_rows = jnp.where(
        slot_live[:, None], second_normed[jnp.maximum(slot_token, 0)], jnp.zeros((), jnp.bfloat16)
    )
    arrived = send_owners(send_rows)
    gate_proj = jnp.einsum(
        "secd,edf->secf", arrived, gate_weight, preferred_element_type=jnp.float32
    )
    up_proj = jnp.einsum("secd,edf->secf", arrived, up_weight, preferred_element_type=jnp.float32)
    sigmoid_gate = jax.nn.sigmoid(gate_proj)
    activated = gate_proj * sigmoid_gate
    hidden_units = (activated * up_proj).astype(jnp.bfloat16)
    expert_part = jnp.einsum(
        "secf,edf->secd", hidden_units, down_weight, preferred_element_type=jnp.float32
    )
    route_out = send_tokens(expert_part)
    mixed_part = jnp.sum(route_out * route_gates[:, :, None], 1)
    expert_mix = lax.psum(mixed_part.astype(jnp.bfloat16), "tensor").astype(jnp.float32)
    layer_out = (residual + expert_mix).astype(jnp.bfloat16)
    grad_routes = (
        (route_gates[:, :, None] * grad_float[:, None, :])
        .astype(jnp.bfloat16)
        .reshape(route_count, model_width)
    )
    grad_slots = (
        jnp.zeros((expert_count * capacity, model_width), jnp.bfloat16)
        .at[destination]
        .set(grad_routes)
    )
    grad_arrived = send_owners(grad_slots)
    grad_hidden = jnp.einsum(
        "secd,edf->secf", grad_arrived, down_weight, preferred_element_type=jnp.float32
    )
    grad_gate_proj = (
        grad_hidden * up_proj * sigmoid_gate * (1.0 + gate_proj * (1.0 - sigmoid_gate))
    ).astype(jnp.bfloat16)
    grad_up_proj = (grad_hidden * activated).astype(jnp.bfloat16)
    grad_down_local = jnp.einsum(
        "secd,secf->edf", grad_arrived, hidden_units, preferred_element_type=jnp.float32
    )
    grad_gate_local = jnp.einsum(
        "secd,secf->edf", arrived, grad_gate_proj, preferred_element_type=jnp.float32
    )
    grad_up_local = jnp.einsum(
        "secd,secf->edf", arrived, grad_up_proj, preferred_element_type=jnp.float32
    )
    grad_arrival = jnp.einsum(
        "secf,edf->secd", grad_gate_proj, gate_weight, preferred_element_type=jnp.float32
    ) + jnp.einsum("secf,edf->secd", grad_up_proj, up_weight, preferred_element_type=jnp.float32)
    grad_routed = jnp.sum(send_tokens(grad_arrival), 1)
    grad_gates = jnp.sum(route_out * grad_float[:, None, :], -1)
    grad_route_logits = route_gates * (
        grad_gates - jnp.sum(route_gates * grad_gates, -1, keepdims=True)
    )
    grad_logits = jnp.sum(jnp.where(picked, grad_route_logits[:, :, None], 0.0), 1)
    grad_router_part = lax.dot_general(
        second_normed.astype(jnp.float32),
        grad_logits,
        (((0,), (0,)), ((), ())),
        precision=lax.Precision.HIGHEST,
        preferred_element_type=jnp.float32,
    )
    grad_second = grad_routed + lax.dot_general(
        grad_logits,
        router_weight.astype(jnp.float32),
        (((1,), (1,)), ((), ())),
        precision=lax.Precision.HIGHEST,
        preferred_element_type=jnp.float32,
    )
    second_gained = grad_second * second_float
    grad_second_part = jnp.sum(grad_second * second_hat, 0)
    grad_resid_part = second_scale * (
        second_gained - second_hat * jnp.mean(second_gained * second_hat, -1, keepdims=True)
    )
    grad_resid_sum, grad_second_gain, grad_router_sum = lax.psum(
        (grad_resid_part, grad_second_part, grad_router_part), "tensor"
    )
    grad_resid = grad_float + grad_resid_sum
    grad_out_low = grad_resid.astype(jnp.bfloat16)
    grad_outproj_local = contract_rows(grad_out_low, attended)
    grad_attended = (
        jnp.dot(grad_out_low, output_weight, preferred_element_type=jnp.float32)
        .astype(jnp.bfloat16)
        .reshape(tokens_here, kv_heads, group_size, head_size)
    )
    grad_probs = jnp.einsum(
        "tkgd,ukd->kgtu", grad_attended, values_low, preferred_element_type=jnp.float32
    )
    grad_values = (
        jnp.einsum("kgtu,tkgd->ukd", probs_low, grad_attended, preferred_element_type=jnp.float32)
        .astype(jnp.bfloat16)
        .reshape(tokens_here, kv_heads * head_size)
    )
    grad_scores = (
        probabilities * (grad_probs - jnp.sum(probabilities * grad_probs, -1, keepdims=True))
    ).astype(jnp.bfloat16)
    grad_queries = (
        jnp.einsum("kgtu,ukd->tkgd", grad_scores, keys_rot, preferred_element_type=jnp.float32)
        * score_scale
    )
    grad_keys = (
        jnp.einsum("kgtu,tkgd->ukd", grad_scores, grouped, preferred_element_type=jnp.float32)
        * score_scale
    )
    grad_query_pre = (
        rotate_back(
            grad_queries.reshape(tokens_here, query_heads, head_size), cosine_table, sine_table
        )
        .astype(jnp.bfloat16)
        .reshape(tokens_here, query_heads * head_size)
    )
    grad_key_pre = (
        rotate_back(grad_keys, cosine_table, sine_table)
        .astype(jnp.bfloat16)
        .reshape(tokens_here, kv_heads * head_size)
    )
    grad_query_local = contract_rows(first_normed, grad_query_pre)
    grad_key_local = contract_rows(first_normed, grad_key_pre)
    grad_value_local = contract_rows(first_normed, grad_values)
    grad_first = (
        contract_cols(grad_query_pre, query_weight)
        + contract_cols(grad_key_pre, key_weight)
        + contract_cols(grad_values, value_weight)
    )
    first_gained = grad_first * first_float
    grad_first_part = jnp.sum(grad_first * first_hat, 0)
    grad_input_part = first_scale * (
        first_gained - first_hat * jnp.mean(first_gained * first_hat, -1, keepdims=True)
    )
    grad_input_sum, grad_first_gain = (
        lax.psum(grad_input_part.astype(jnp.bfloat16), "tensor").astype(jnp.float32),
        lax.psum(grad_first_part.astype(jnp.bfloat16), "tensor").astype(jnp.float32),
    )
    grad_input = grad_resid + grad_input_sum
    grad_query, grad_key, grad_value, grad_outproj, grad_first_out, grad_second_out, grad_router = (
        lax.psum_scatter(grad_query_local, ("dp", "expert"), scatter_dimension=0, tiled=True),
        lax.psum_scatter(grad_key_local, ("dp", "expert"), scatter_dimension=0, tiled=True),
        lax.psum_scatter(grad_value_local, ("dp", "expert"), scatter_dimension=0, tiled=True),
        lax.psum_scatter(grad_outproj_local, ("dp", "expert"), scatter_dimension=0, tiled=True),
        lax.psum_scatter(grad_first_gain, ("dp", "expert"), scatter_dimension=0, tiled=True),
        lax.psum_scatter(grad_second_gain, ("dp", "expert"), scatter_dimension=0, tiled=True),
        lax.psum_scatter(grad_router_sum, ("dp", "expert"), scatter_dimension=0, tiled=True),
    )
    grad_gate, grad_upproj, grad_down = (
        lax.psum_scatter(
            grad_gate_local.astype(jnp.bfloat16), "dp", scatter_dimension=1, tiled=True
        ).astype(jnp.float32),
        lax.psum_scatter(
            grad_up_local.astype(jnp.bfloat16), "dp", scatter_dimension=1, tiled=True
        ).astype(jnp.float32),
        lax.psum_scatter(
            grad_down_local.astype(jnp.bfloat16), "dp", scatter_dimension=1, tiled=True
        ).astype(jnp.float32),
    )
    return (
        layer_out,
        grad_input,
        grad_first_out,
        grad_query,
        grad_key,
        grad_value,
        grad_outproj,
        grad_second_out,
        grad_router,
        grad_gate,
        grad_upproj,
        grad_down,
    )


def solution(mesh):
    return jax.shard_map(
        on_device,
        mesh=mesh,
        in_specs=(
            P(("dp", "expert"), None),
            P(("dp", "expert"), None),
            P(("dp", "expert"), None),
            P(),
            P(None, "tensor"),
            P(None, "tensor"),
            P(None, "tensor"),
            P(None, "tensor"),
            P(),
            P(),
            P("expert", None, "tensor"),
            P("expert", None, "tensor"),
            P("expert", None, "tensor"),
            P(("dp", "expert"), None),
        ),
        out_specs=(
            P(("dp", "expert"), None),
            P(("dp", "expert"), None),
            P(("dp", "expert")),
            P(("dp", "expert"), "tensor"),
            P(("dp", "expert"), "tensor"),
            P(("dp", "expert"), "tensor"),
            P(("dp", "expert"), "tensor"),
            P(("dp", "expert")),
            P(("dp", "expert"), None),
            P("expert", "dp", "tensor"),
            P("expert", "dp", "tensor"),
            P("expert", "dp", "tensor"),
        ),
        check_vma=False,
    )
```

profile of v0, /device:TPU:0, one launch (start us, length us, event | category | flops | bytes accessed | tf_op | source)
XLA Modules:
  0.0 712.7 jit_solution(9090257439051307678)
XLA Ops:
  18.7 9.0 %reduce-window.11 = s32[32,8,128]{2,1,0:T(8,128)S(1)} reduce-window(s32[32,8,128]{2,1,0:T(8,128)S(1)} %fusion.65, s32[]{:T(128)} %constant.25.clone.1), window={size=1x1x128 pad=0_0x0_0x127_0}, to_apply=%region_7.8 | reduce-window | flops 4161536 | bytes 262148 | tf_op jit(solution)/shard_map/reduce-window.1
  32.7 26.6 %all-reduce.9.cloned.1.call-done = f32[128,1024]{1,0:T(8,128)} async-done(((f32[128,1024]{1,0:T(8,128)}), f32[128,1024]{1,0:T(8,128)}) %all-reduce.9.cloned.1.call-update) | async-done | bytes 524304 | tf_op jit(solution)/shard_map/psum | solution.py:137
  60.7 5.8 gather_fusion
  69.8 4.8 all-to-all-start
  78.8 8.5 %scatter_custom_fusion.1 = bf16[1536,1024]{1,0:T(8,128)(2,1)} fusion(s32[1024]{0:T(1024)} %bitcast.236, f32[128,1024]{1,0:T(8,128)} %convert_element_type.154, f32[1024]{0:T(1024)} %div.59, bf16[]{:T(256)} %constant.59.clone.1), kind=kCustom, calls=%fused_computation.25 | custom fusion | flops 2097152 | bytes 3674624 | tf_op jit(solution)/shard_map/scatter | solution.py:209
  87.3 24.3 %all-to-all-done = bf16[4,384,1024]{2,1,0:T(8,128)(2,1)} async-done(((bf16[4,384,1024]{2,1,0:T(8,128)(2,1)}), bf16[4,384,1024]{2,1,0:T(8,128)(2,1)}, u32[]{:S(2)}, u32[]{:S(2)}) %all-to-all-start) | async-done | bytes 3145760 | tf_op jit(solution)/shard_map/all_to_all | solution.py:161
  111.6 4.8 all-to-all-start.2
  116.4 4.5 fusion.27
  124.8 28.5 %all-to-all-done.2 = bf16[4,384,1024]{2,1,0:T(8,128)(2,1)} async-done(((bf16[4,384,1024]{2,1,0:T(8,128)(2,1)}), bf16[4,384,1024]{2,1,0:T(8,128)(2,1)}, u32[]{:S(2)}, u32[]{:S(2)}) %all-to-all-start.2) | async-done | bytes 3145760 | tf_op jit(solution)/shard_map/all_to_all | solution.py:161
  163.5 5.3 all-to-all-start.3
  174.0 65.5 %all-to-all-done.3 = f32[4,384,1024]{2,1,0:T(8,128)} async-done(((f32[4,384,1024]{2,1,0:T(8,128)}), f32[4,384,1024]{2,1,0:T(8,128)}, u32[]{:S(2)}, u32[]{:S(2)}) %all-to-all-start.3) | async-done | bytes 6291488 | tf_op jit(solution)/shard_map/all_to_all | solution.py:171
  239.5 5.4 all-to-all-start.1
  245.2 9.2 %gather_fusion.2 = f32[1024,1024]{1,0:T(8,128)} fusion(f32[1536,1024]{1,0:T(8,128)} %bitcast.43, s32[1024]{0:T(1024)S(1)} %broadcast_clamp_fusion), kind=kCustom, calls=%fused_computation.2 | custom fusion | bytes 8392704 | tf_op jit(solution)/shard_map/gather | solution.py:179
  257.6 57.9 %all-to-all-done.1 = f32[4,384,1024]{2,1,0:T(8,128)} async-done(((f32[4,384,1024]{2,1,0:T(8,128)}), f32[4,384,1024]{2,1,0:T(8,128)}, u32[]{:S(2)}, u32[]{:S(2)}) %all-to-all-start.1) | async-done | bytes 6291488 | tf_op jit(solution)/shard_map/all_to_all | solution.py:171
  315.6 9.3 %gather_fusion.1 = f32[1024,1024]{1,0:T(8,128)} fusion(f32[1536,1024]{1,0:T(8,128)} %bitcast.32, s32[1024]{0:T(1024)S(1)} %broadcast_clamp_fusion), kind=kCustom, calls=%fused_computation.1 | custom fusion | bytes 8392704 | tf_op jit(solution)/shard_map/gather | solution.py:179
  324.9 4.5 fusion.3
  331.2 4.7 bitcast_convert_fusion
  336.1 4.7 bitcast_convert_fusion.1
  340.9 4.8 bitcast_convert_fusion.2
  346.7 22.0 %all-reduce.11.cloned.1.call-done = f32[128,1024]{1,0:T(8,128)} async-done(((f32[128,1024]{1,0:T(8,128)}), f32[128,1024]{1,0:T(8,128)}) %all-reduce.11.cloned.1.call-update) | async-done | bytes 524304 | tf_op jit(solution)/shard_map/psum | solution.py:256
  380.6 22.8 %reduce-scatter.21.cloned.1.call-done = bf16[8,512,128]{2,1,0:T(8,128)(2,1)} async-done(((bf16[8,1024,128]{2,1,0:T(8,128)(2,1)}), bf16[8,512,128]{2,1,0:T(8,128)(2,1)}) %reduce-scatter.21.cloned.1.call-update) | async-done | bytes 1048592 | tf_op jit(solution)/shard_map/reduce_scatter | solution.py:332
  406.1 31.9 %reduce-scatter.19.cloned.1.call-done = bf16[8,512,128]{2,1,0:T(8,128)(2,1)} async-done(((bf16[8,1024,128]{2,1,0:T(8,128)(2,1)}), bf16[8,512,128]{2,1,0:T(8,128)(2,1)}) %reduce-scatter.19.cloned.1.call-update) | async-done | bytes 1048592 | tf_op jit(solution)/shard_map/reduce_scatter | solution.py:329
  440.8 31.7 %reduce-scatter.17.cloned.1.call-done = bf16[8,512,128]{2,1,0:T(8,128)(2,1)} async-done(((bf16[8,1024,128]{2,1,0:T(8,128)(2,1)}), bf16[8,512,128]{2,1,0:T(8,128)(2,1)}) %reduce-scatter.17.cloned.1.call-update) | async-done | bytes 1048592 | tf_op jit(solution)/shard_map/reduce_scatter | solution.py:326
  475.2 11.7 %psum.53 = bf16[1024]{0:T(1024)(128)(2,1)S(1)} all-reduce(bf16[1024]{0:T(1024)(128)(2,1)S(1)} %get-tuple-element.16), channel_id=1, replica_groups=mesh['dp'=2,'expert'=4,'tensor'=4] {'tensor'}, use_global_device_ids=true, to_apply=%region_28.29 | all-reduce | flops 1024 | bytes 4096 | tf_op jit(solution)/shard_map/psum | solution.py:313
  486.9 12.1 %all-reduce.2 = (f32[1024]{0:T(1024)S(1)}, f32[1024]{0:T(1024)S(1)}) all-reduce(bf16[1024]{0:T(1024)(128)(2,1)S(1)} %psum.53, f32[1024]{0:T(1024)S(1)} %get-tuple-element.14), channel_id=2, replica_groups=mesh['dp'=2,'expert'=4,'tensor'=4] {'dp','expert'}, use_global_device_ids=true, to_apply=%region_29.30.clone | all-reduce | flops 2048 | bytes 14336
  499.6 9.5 %reduce-scatter.23.cloned.1.call-done = f32[128,32]{0,1:T(8,128)} async-done(((f32[1024,32]{0,1:T(8,128)}), f32[128,32]{0,1:T(8,128)}) %reduce-scatter.23.cloned.1.call-update) | async-done | bytes 16400 | tf_op jit(solution)/shard_map/reduce_scatter | solution.py:323
  509.1 19.7 %all-reduce.3 = (f32[128]{0:T(128)}, f32[128,32]{0,1:T(8,128)}) all-reduce(f32[128]{0:T(128)S(1)} %dynamic-slice.3, f32[128,32]{0,1:T(8,128)} %reduce-scatter.23.cloned.1.call-done), channel_id=1, replica_groups=mesh['dp'=2,'expert'=4,'tensor'=4] {'tensor'}, use_global_device_ids=true, to_apply=%region_35.36 | all-reduce | flops 4224 | bytes 33792 | tf_op jit(solution)/shard_map/psum | solution.py:256
  528.8 22.0 %all-reduce.13.cloned.1.call-done = (bf16[128,1024]{1,0:T(8,128)(2,1)}, bf16[128,1024]{1,0:T(8,128)(2,1)}) async-done(((bf16[128,1024]{1,0:T(8,128)(2,1)}, bf16[128,1024]{1,0:T(8,128)(2,1)}), (bf16[128,1024]{1,0:T(8,128)(2,1)}, bf16[128,1024]{1,0:T(8,128)(2,1)})) %all-reduce.13.cloned.1.call-update) | async-done | bytes 524304 | tf_op jit(solution)/shard_map/psum | solution.py:199
  552.9 35.7 %reduce-scatter.13.cloned.1.call-done = f32[128,128]{1,0:T(8,128)} async-done(((f32[1024,128]{1,0:T(8,128)}), f32[128,128]{1,0:T(8,128)}) %reduce-scatter.13.cloned.1.call-update) | async-done | bytes 65552 | tf_op jit(solution)/shard_map/reduce_scatter | solution.py:319
  588.5 38.1 %reduce-scatter.11.cloned.1.call-done = f32[128,128]{1,0:T(8,128)} async-done(((f32[1024,128]{1,0:T(8,128)}), f32[128,128]{1,0:T(8,128)}) %reduce-scatter.11.cloned.1.call-update) | async-done | bytes 65552 | tf_op jit(solution)/shard_map/reduce_scatter | solution.py:318
  626.7 39.7 %reduce-scatter.15.cloned.1.call-done = f32[128,256]{1,0:T(8,128)} async-done(((f32[1024,256]{1,0:T(8,128)}), f32[128,256]{1,0:T(8,128)}) %reduce-scatter.15.cloned.1.call-update) | async-done | bytes 131088 | tf_op jit(solution)/shard_map/reduce_scatter | solution.py:320
  666.3 39.8 %reduce-scatter.9.cloned.1.call-done = f32[128,256]{1,0:T(8,128)} async-done(((f32[1024,256]{1,0:T(8,128)}), f32[128,256]{1,0:T(8,128)}) %reduce-scatter.9.cloned.1.call-update) | async-done | bytes 131088 | tf_op jit(solution)/shard_map/reduce_scatter | solution.py:317
  (217 shorter events, 72.5 us)
Async XLA Ops:
  7.2 146.1 %copy-start = (bf16[8,1024,128]{2,1,0:T(8,128)(2,1)S(1)}, bf16[8,1024,128]{2,1,0:T(8,128)(2,1)}, u32[]{:S(2)}) copy-start(bf16[8,1024,128]{2,1,0:T(8,128)(2,1)} %param.26) | copy-start | bytes 6291460
  7.2 9.8 %copy-start.8 = (bf16[1024,256]{1,0:T(8,128)(2,1)S(1)}, bf16[1024,256]{1,0:T(8,128)(2,1)}, u32[]{:S(2)}) copy-start(bf16[1024,256]{1,0:T(8,128)(2,1)} %param.21) | copy-start | bytes 1572868
  7.2 52.1 %all-reduce.9.cloned.1.call-start = ((), (), s32[]{:S(2)}) async-start(), calls=%async_computation.12 | async-start | bytes 1048576 | tf_op jit(solution)/shard_map/psum | solution.py:137
  9.1 9.0 %copy-start.36 = (pred[128,128]{0,1:T(8,128)(4,1)}, pred[128,128]{0,1:T(8,128)(4,1)S(1)}, u32[]{:S(2)}) copy-start(pred[128,128]{0,1:T(8,128)(4,1)S(1)} %fusion.68) | copy-start | bytes 49156
  9.2 8.9 %copy-start.27 = (s32[128,8]{0,1:T(8,128)S(1)}, s32[128,8]{0,1:T(8,128)}, u32[]{:S(2)}) copy-start(s32[128,8]{0,1:T(8,128)} %param.16) | copy-start | bytes 12292
  13.8 45.6 %copy-start.2 = (bf16[128,1024]{1,0:T(8,128)(2,1)S(1)}, bf16[128,1024]{1,0:T(8,128)(2,1)}, u32[]{:S(2)}) copy-start(bf16[128,1024]{1,0:T(8,128)(2,1)} %param.14) | copy-start | bytes 786436
  69.8 41.8 %all-to-all-start = ((bf16[4,384,1024]{2,1,0:T(8,128)(2,1)}), bf16[4,384,1024]{2,1,0:T(8,128)(2,1)}, u32[]{:S(2)}, u32[]{:S(2)}) async-start(bf16[4,384,1024]{2,1,0:T(8,128)(2,1)} %broadcast_select_fusion), calls=%async_computation | async-start | bytes 6291456 | tf_op jit(solution)/shard_map/all_to_all | solution.py:161
  111.6 41.6 %all-to-all-start.2 = ((bf16[4,384,1024]{2,1,0:T(8,128)(2,1)}), bf16[4,384,1024]{2,1,0:T(8,128)(2,1)}, u32[]{:S(2)}, u32[]{:S(2)}) async-start(bf16[4,384,1024]{2,1,0:T(8,128)(2,1)} %bitcast.209), calls=%async_computation.2 | async-start | bytes 6291456 | tf_op jit(solution)/shard_map/all_to_all | solution.py:161
  163.5 76.0 %all-to-all-start.3 = ((f32[4,384,1024]{2,1,0:T(8,128)}), f32[4,384,1024]{2,1,0:T(8,128)}, u32[]{:S(2)}, u32[]{:S(2)}) async-start(f32[4,384,1024]{2,1,0:T(8,128)} %bitcast.208), calls=%async_computation.3 | async-start | bytes 12582912 | tf_op jit(solution)/shard_map/all_to_all | solution.py:171
  239.5 76.1 %all-to-all-start.1 = ((f32[4,384,1024]{2,1,0:T(8,128)}), f32[4,384,1024]{2,1,0:T(8,128)}, u32[]{:S(2)}, u32[]{:S(2)}) async-start(f32[4,384,1024]{2,1,0:T(8,128)} %bitcast.207), calls=%async_computation.1 | async-start | bytes 12582912 | tf_op jit(solution)/shard_map/all_to_all | solution.py:171
  244.9 123.8 %all-reduce.11.cloned.1.call-start = ((), (), s32[]{:S(2)}) async-start(), calls=%async_computation.13 | async-start | bytes 1048576 | tf_op jit(solution)/shard_map/psum | solution.py:256
  315.6 9.3 %copy-start.3 = (f32[128,1024]{1,0:T(8,128)S(1)}, f32[128,1024]{1,0:T(8,128)}, u32[]{:S(2)}) copy-start(f32[128,1024]{1,0:T(8,128)} %convert_element_type.154) | copy-start | bytes 1572868
  331.2 72.2 %reduce-scatter.21.cloned.1.call-start = ((), (), s32[]{:S(2)}) async-start(), calls=%async_computation.20 | async-start | bytes 3145728 | tf_op jit(solution)/shard_map/reduce_scatter | solution.py:332
  336.0 102.0 %reduce-scatter.19.cloned.1.call-start = ((), (), s32[]{:S(2)}) async-start(), calls=%async_computation.19 | async-start | bytes 3145728 | tf_op jit(solution)/shard_map/reduce_scatter | solution.py:329
  340.8 27.9 %copy-start.9 = (bf16[1024,256]{1,0:T(8,128)(2,1)S(1)}, bf16[1024,256]{1,0:T(8,128)(2,1)}, u32[]{:S(2)}) copy-start(bf16[1024,256]{1,0:T(8,128)(2,1)} %param.21) | copy-start | bytes 1572868
  340.8 131.7 %reduce-scatter.17.cloned.1.call-start = ((), (), s32[]{:S(2)}) async-start(), calls=%async_computation.18 | async-start | bytes 3145728 | tf_op jit(solution)/shard_map/reduce_scatter | solution.py:326
  345.7 24.4 %copy-start.26 = (bf16[128,4,32]{0,2,1:T(8,128)(2,1)S(1)}, bf16[128,4,32]{0,2,1:T(8,128)(2,1)}, u32[]{:S(2)}) copy-start(bf16[128,4,32]{0,2,1:T(8,128)(2,1)} %copy-done.25) | copy-start | bytes 98308
  345.7 24.5 %copy-start.29 = (bf16[128,2,32]{0,2,1:T(8,128)(2,1)S(1)}, bf16[128,2,32]{0,2,1:T(8,128)(2,1)}, u32[]{:S(2)}) copy-start(bf16[128,2,32]{0,2,1:T(8,128)(2,1)} %copy-done.28) | copy-start | bytes 49156
  345.7 24.5 %copy-start.31 = (bf16[128,2,32]{0,2,1:T(8,128)(2,1)S(1)}, bf16[128,2,32]{0,2,1:T(8,128)(2,1)}, u32[]{:S(2)}) copy-start(bf16[128,2,32]{0,2,1:T(8,128)(2,1)} %copy-done.30) | copy-start | bytes 49156
  345.7 24.5 %copy-start.44 = (f32[2,2,128]{2,1,0:T(2,128)S(1)}, f32[2,2,128]{2,1,0:T(2,128)}, u32[]{:S(2)}) copy-start(f32[2,2,128]{2,1,0:T(2,128)} %copy-done.43) | copy-start | bytes 6148
  345.7 25.7 %copy-start.18 = (f32[2,2,128,128]{2,3,1,0:T(8,128)S(1)}, f32[2,2,128,128]{2,3,1,0:T(8,128)}, u32[]{:S(2)}) copy-start(f32[2,2,128,128]{2,3,1,0:T(8,128)} %get-tuple-element.40) | copy-start | bytes 786436
  345.7 25.7 %copy-start.47 = (bf16[128,128]{0,1:T(8,128)(2,1)S(1)}, bf16[128,128]{0,1:T(8,128)(2,1)}, u32[]{:S(2)}) copy-start(bf16[128,128]{0,1:T(8,128)(2,1)} %copy-done.46) | copy-start | bytes 98308
  345.7 26.3 %copy-start.10 = (bf16[1024,256]{1,0:T(8,128)(2,1)S(1)}, bf16[1024,256]{1,0:T(8,128)(2,1)}, u32[]{:S(2)}) copy-start(bf16[1024,256]{1,0:T(8,128)(2,1)} %param.18) | copy-start | bytes 1572868
  345.7 163.3 %reduce-scatter.23.cloned.1.call-start = ((), (), s32[]{:S(2)}) async-start(), calls=%async_computation.21 | async-start | bytes 147456 | tf_op jit(solution)/shard_map/reduce_scatter | solution.py:323
  346.7 25.7 %copy-start.21 = (bf16[1024,128]{1,0:T(8,128)(2,1)S(1)}, bf16[1024,128]{1,0:T(8,128)(2,1)}, u32[]{:S(2)}) copy-start(bf16[1024,128]{1,0:T(8,128)(2,1)} %param.19) | copy-start | bytes 786436
  346.7 204.1 %all-reduce.13.cloned.1.call-start = ((), (), s32[]{:S(2)}) async-start(), calls=%async_computation.22 | async-start | bytes 1048576 | tf_op jit(solution)/shard_map/psum | solution.py:199
  374.1 214.5 %reduce-scatter.13.cloned.1.call-start = ((), (), s32[]{:S(2)}) async-start(), calls=%async_computation.16 | async-start | bytes 589824 | tf_op jit(solution)/shard_map/reduce_scatter | solution.py:319
  375.3 251.4 %reduce-scatter.11.cloned.1.call-start = ((), (), s32[]{:S(2)}) async-start(), calls=%async_computation.15 | async-start | bytes 589824 | tf_op jit(solution)/shard_map/reduce_scatter | solution.py:318
  376.5 289.8 %reduce-scatter.15.cloned.1.call-start = ((), (), s32[]{:S(2)}) async-start(), calls=%async_computation.17 | async-start | bytes 1179648 | tf_op jit(solution)/shard_map/reduce_scatter | solution.py:320
  377.9 328.2 %reduce-scatter.9.cloned.1.call-start = ((), (), s32[]{:S(2)}) async-start(), calls=%async_computation.14 | async-start | bytes 1179648 | tf_op jit(solution)/shard_map/reduce_scatter | solution.py:317
  406.1 144.7 %copy-start.5 = (f32[128,1024]{1,0:T(8,128)S(1)}, f32[128,1024]{1,0:T(8,128)}, u32[]{:S(2)}) copy-start(f32[128,1024]{1,0:T(8,128)} %all-reduce.11.cloned.1.call-done) | copy-start | bytes 1572868
  438.0 268.1 %copy-start.1 = (bf16[8,1024,128]{2,1,0:T(8,128)(2,1)S(1)}, bf16[8,1024,128]{2,1,0:T(8,128)(2,1)}, u32[]{:S(2)}) copy-start(bf16[8,1024,128]{2,1,0:T(8,128)(2,1)} %param.26) | copy-start | bytes 6291460
  (32 other events, 120.2 us)
Sparse Core Ops, SparseCore 0:
  18.2 41.0 all-reduce.8
  331.3 37.3 all-reduce.10
  371.5 31.8 reduce-scatter.20
  406.1 31.8 reduce-scatter.18
  440.6 31.8 reduce-scatter.16
  475.7 33.3 reduce-scatter.22
  512.0 38.6 all-reduce.12
  554.4 34.0 reduce-scatter.12
  592.5 34.1 reduce-scatter.10
  630.3 36.0 reduce-scatter.14
  670.1 35.9 reduce-scatter.8
where the time goes:
time: 714 us; the launch traced here: 713 us
  waiting for transfers between devices  496 us (69%)
  matrix products  48 us (7%)
  other arithmetic  47.9 us (7%)
  blocking collectives  43.4 us (6%)
  local copies, waits for them, and re-layouts  40.9 us (6%)
  starting transfers between devices  20.9 us (3%)
  between operations  15.4 us (2%)
    all_to_all x2, waiting for transfers between devices, send_tokens(): lax.all_to_all(expert_terms.reshape(expert_devices, local_experts * capac...  123 us
    all_to_all x2, waiting for transfers between devices, send_owners(): lax.all_to_all(slot_rows.reshape(expert_devices, local_experts * capacity...  52.8 us
    reduce_scatter x1, waiting for transfers between devices, on_device(): lax.psum_scatter(grad_query_local, ('dp', 'expert'), scatter_dimension=0,...  39.8 us
    reduce_scatter x1, waiting for transfers between devices, on_device(): lax.psum_scatter(grad_outproj_local, ('dp', 'expert'), scatter_dimension=...  39.7 us
    reduce_scatter x1, waiting for transfers between devices, on_device(): lax.psum_scatter(grad_key_local, ('dp', 'expert'), scatter_dimension=0, t...  38.1 us
    reduce_scatter x1, waiting for transfers between devices, on_device(): lax.psum_scatter(grad_value_local, ('dp', 'expert'), scatter_dimension=0,...  35.7 us
    reduce_scatter x1, waiting for transfers between devices, on_device(): lax.psum_scatter(grad_up_local.astype(jnp.bfloat16), 'dp', scatter_dimens...  31.9 us
    reduce_scatter x1, waiting for transfers between devices, on_device(): lax.psum_scatter(grad_gate_local.astype(jnp.bfloat16), 'dp', scatter_dime...  31.7 us
  transfers between devices with their start and end apart: 15, of which 15 were waited for; matrix products, arithmetic and copies ran while one was open for 12% of the time, Pallas kernels for 0%

commit v1 on v0

v1 whole, which is shorter than its diff:
```python
import math

import jax
import jax.numpy as jnp
from jax import lax
from jax.sharding import PartitionSpec as P

HD = 64
EPSILON = 1e-06
F32 = jnp.float32
BF16 = jnp.bfloat16
HIGH = lax.Precision.HIGHEST


def rope_tables(positions, head_size):
    inverse = jnp.exp(
        jnp.arange(head_size // 2).astype(F32) * (-2.0 * math.log(10000.0) / head_size)
    )
    angles = positions.astype(F32)[:, None] * inverse[None, :]
    return (jnp.cos(angles)[:, None, :], jnp.sin(angles)[:, None, :])


def rotate(values, cosine_table, sine_table):
    half_size = values.shape[-1] // 2
    lower_half = values[..., :half_size]
    upper_half = values[..., half_size:]
    return jnp.concatenate(
        [
            lower_half * cosine_table - upper_half * sine_table,
            upper_half * cosine_table + lower_half * sine_table,
        ],
        -1,
    )


def positions_of(lengths_row, row_ids):
    ends_at = [lengths_row[0]]
    for i in range(1, lengths_row.shape[0]):
        ends_at.append(ends_at[-1] + lengths_row[i])
    ends_at = jnp.stack(ends_at)
    segment = jnp.sum((row_ids[:, None] >= ends_at[None, :]).astype(jnp.int32), 1, dtype=jnp.int32)
    starts_at = ends_at - lengths_row
    chosen = segment[:, None] == jnp.arange(lengths_row.shape[0], dtype=jnp.int32)[None, :]
    start_row = jnp.sum(jnp.where(chosen, starts_at[None, :], 0), 1, dtype=jnp.int32)
    return (segment, row_ids - start_row)


def dot(left, right, dims, **kw):
    return lax.dot_general(left, right, (dims, ((), ())), preferred_element_type=F32, **kw)


def swap(x, axis, k):
    n = lax.axis_size(axis)
    return lax.ppermute(x, axis, [(i, i ^ k) for i in range(n)])


def bits_of(n):
    k, out = n // 2, []
    while k >= 1:
        out.append(k)
        k //= 2
    return out


def gather_expert(x, axis=0):
    for k in bits_of(lax.axis_size("expert")):
        x = jnp.concatenate([x, swap(x, "expert", k)], axis)
    return x


def reduce_expert(x, dtype, axis=0):
    for k in reversed(bits_of(lax.axis_size("expert"))):
        half = x.shape[axis] // 2
        keep = lax.slice_in_dim(x, 0, half, axis=axis)
        sent = lax.slice_in_dim(x, half, 2 * half, axis=axis).astype(dtype)
        x = keep.astype(F32) + swap(sent, "expert", k).astype(F32)
        x = x.astype(dtype)
    return x


def reduce_tensor(x, dtype, axis=0):
    n = lax.axis_size("tensor")
    rows = x.shape[axis] // n
    blocks = [lax.slice_in_dim(x, k * rows, (k + 1) * rows, axis=axis) for k in range(n)]
    total = blocks[0].astype(F32)
    for k in range(1, n):
        total = total + swap(blocks[k].astype(dtype), "tensor", k).astype(F32)
    return total


def gather_tensor(x):
    n = lax.axis_size("tensor")
    return [x] + [swap(x, "tensor", k) for k in range(1, n)]


def by_distance(x, me, n):
    blocks = x.reshape((n, x.shape[0] // n) + x.shape[1:])
    return jnp.concatenate(
        [lax.dynamic_index_in_dim(blocks, me ^ k, 0, keepdims=False) for k in range(n)], 0
    )


def reduce_plane(x):
    places = lax.axis_size("dp"), lax.axis_size("expert")
    width = x.shape[1]
    rows = x.shape[0] // (places[0] * places[1])
    expert_bits = bits_of(places[1])
    me = lax.axis_index("expert")
    x = x.reshape((places[0],) + (2,) * len(expert_bits) + (rows, width))
    for k in reversed(expert_bits):
        at = x.ndim - 3
        bit = (me // k) % 2
        keep = lax.dynamic_index_in_dim(x, bit, at, keepdims=False)
        sent = lax.dynamic_index_in_dim(x, 1 - bit, at, keepdims=False)
        shape = keep.shape
        got = swap(sent.astype(BF16).reshape(-1, width), "expert", k).reshape(shape)
        x = keep + got.astype(F32)
    mine = lax.axis_index("dp")
    total = lax.dynamic_index_in_dim(x, mine, 0, keepdims=False)
    for k in range(1, places[0]):
        sent = lax.dynamic_index_in_dim(x, mine ^ k, 0, keepdims=False)
        total = total + swap(sent.astype(BF16), "dp", k).astype(F32)
    return total


def on_device(
    hidden_in,
    seq_lengths,
    expert_routes,
    first_gain,
    query_weight,
    key_weight,
    value_weight,
    output_weight,
    second_gain,
    router_weight,
    gate_weight,
    up_weight,
    down_weight,
    grad_layer_out,
):
    tokens_here, model_width = hidden_in.shape
    query_heads = query_weight.shape[1] // HD
    kv_heads = key_weight.shape[1] // HD
    group_size = query_heads // kv_heads
    expert_count = router_weight.shape[1]
    local_experts, _, units = gate_weight.shape
    tensor_n = lax.axis_size("tensor")
    expert_n = lax.axis_size("expert")
    dp_n = lax.axis_size("dp")
    me_t, me_e, me_d = (lax.axis_index(a) for a in ("tensor", "expert", "dp"))
    block = tokens_here // tensor_n
    score_scale = HD ** (-0.5)

    hidden_rel = by_distance(hidden_in, me_t, tensor_n)
    grad_rel = by_distance(grad_layer_out, me_t, tensor_n)
    routes_rel = by_distance(expert_routes, me_t, tensor_n)
    row_ids = (
        ((jnp.arange(tensor_n, dtype=jnp.int32) ^ me_t) * block)[:, None]
        + jnp.arange(block, dtype=jnp.int32)[None, :]
    ).reshape(-1)

    expert_ids = jnp.arange(expert_count, dtype=jnp.int32)
    routed = jnp.sum((routes_rel[:, :, None] == expert_ids).astype(F32), 1).astype(BF16)
    grad_far = [swap(grad_rel, "dp", k) for k in range(1, dp_n)]
    routed_far = [swap(routed, "dp", k) for k in range(1, dp_n)]
    grad_sets = [gather_expert(g) for g in [grad_rel] + grad_far]
    routed_sets = [gather_expert(g) for g in [routed] + routed_far]

    hidden_float = hidden_rel.astype(F32)
    first_scale = lax.rsqrt(jnp.mean(hidden_float * hidden_float, -1, keepdims=True) + EPSILON)
    first_hat = hidden_float * first_scale
    first_float = first_gain.astype(F32)
    first_normed = (first_hat * first_float).astype(BF16)
    segment, positions = positions_of(seq_lengths[0], row_ids)
    cosine_table, sine_table = rope_tables(positions, HD)
    query_pre = dot(first_normed, query_weight, ((1,), (0,))).reshape(tokens_here, query_heads, HD)
    key_pre = dot(first_normed, key_weight, ((1,), (0,))).reshape(tokens_here, kv_heads, HD)
    queries = rotate(query_pre, cosine_table, sine_table).astype(BF16)
    keys_rot = rotate(key_pre, cosine_table, sine_table).astype(BF16)
    values_low = (
        dot(first_normed, value_weight, ((1,), (0,)))
        .astype(BF16)
        .reshape(tokens_here, kv_heads, HD)
    )
    grouped = queries.reshape(tokens_here, kv_heads, group_size, HD)
    scores = (
        jnp.einsum("tkgd,ukd->kgtu", grouped, keys_rot, preferred_element_type=F32) * score_scale
    )
    allowed = (segment[:, None] == segment[None, :]) & (row_ids[None, :] <= row_ids[:, None])
    masked = jnp.where(allowed, scores, -1e30)
    top_score = jnp.max(masked, -1, keepdims=True)
    exponent = jnp.exp(masked - top_score)
    probabilities = exponent / jnp.sum(exponent, -1, keepdims=True)
    probs_low = probabilities.astype(BF16)
    attended = (
        jnp.einsum("kgtu,ukd->tkgd", probs_low, values_low, preferred_element_type=F32)
        .astype(BF16)
        .reshape(tokens_here, query_heads * HD)
    )
    attn_part = dot(attended, output_weight, ((1,), (1,)))
    attn_out = reduce_tensor(attn_part, BF16)

    residual = hidden_float[:block] + attn_out
    second_scale = lax.rsqrt(jnp.mean(residual * residual, -1, keepdims=True) + EPSILON)
    second_hat = residual * second_scale
    second_float = second_gain.astype(F32)
    second_block = (second_hat * second_float).astype(BF16)
    second_group = jnp.concatenate(gather_tensor(second_block), 0)
    second_sets = [gather_expert(second_group)] + [
        gather_expert(swap(second_group, "dp", k)) for k in range(1, dp_n)
    ]

    def gates_of(normed, routed_here):
        logits = dot(normed, router_weight, ((1,), (0,)))
        logits = jnp.where(routed_here > 0, logits, -1e30)
        weights = jnp.exp(logits - jnp.max(logits, -1, keepdims=True))
        return weights / jnp.sum(weights, -1, keepdims=True)

    def expert_side(normed, routed_here, grad_here):
        gates = gates_of(normed, routed_here)
        mine = lax.dynamic_slice_in_dim(gates, me_e * local_experts, local_experts, 1)
        raw = jnp.einsum("td,edf->tef", grad_here, down_weight, preferred_element_type=F32)
        gate_proj = jnp.einsum("td,edf->tef", normed, gate_weight, preferred_element_type=F32)
        up_proj = jnp.einsum("td,edf->tef", normed, up_weight, preferred_element_type=F32)
        sigmoid_gate = jax.nn.sigmoid(gate_proj)
        activated = gate_proj * sigmoid_gate
        hidden = activated * up_proj
        grad_hidden = raw * mine[:, :, None]
        grad_gate_proj = (
            grad_hidden * up_proj * sigmoid_gate * (1.0 + gate_proj * (1.0 - sigmoid_gate))
        ).astype(BF16)
        grad_up_proj = (grad_hidden * activated).astype(BF16)
        gated = (hidden * mine[:, :, None]).astype(BF16)
        return gates, mine, raw, hidden, gated, grad_gate_proj, grad_up_proj

    sides = [
        expert_side(second_sets[i], routed_sets[i], grad_sets[i]) for i in range(dp_n)
    ]
    gates, mine, raw, hidden, gated, grad_gate_proj, grad_up_proj = sides[0]
    grad_arrival = jnp.einsum(
        "tef,edf->td", grad_gate_proj, gate_weight, preferred_element_type=F32
    ) + jnp.einsum("tef,edf->td", grad_up_proj, up_weight, preferred_element_type=F32)
    grad_arrival = grad_arrival.astype(BF16)
    grad_gates_mine = jnp.sum(raw * hidden, -1).T
    grad_gates = lax.dynamic_update_slice_in_dim(
        jnp.zeros((expert_count, grad_gates_mine.shape[1]), F32),
        grad_gates_mine,
        me_e * local_experts,
        0,
    )
    grad_routed = reduce_tensor(reduce_expert(grad_arrival, BF16), BF16)
    grad_gates = reduce_tensor(reduce_expert(grad_gates, F32, 1), F32, 1).T
    if tokens_here * expert_n > 1024:
        gated, grad_routed = lax.optimization_barrier((gated, grad_routed))
    mixed = jnp.einsum("tef,edf->td", gated, down_weight, preferred_element_type=F32)
    mixed = mixed.astype(BF16)
    mixed = reduce_tensor(reduce_expert(mixed, BF16), BF16)
    layer_block = (residual + mixed).astype(BF16)

    half = model_width // dp_n

    def weight_grad(lefts, rights):
        return sum(
            jnp.einsum(
                "td,tef->edf",
                lax.dynamic_slice_in_dim(left, me_d * half, half, 1),
                right,
                preferred_element_type=F32,
            )
            for left, right in zip(lefts, rights)
        )

    grad_gate = weight_grad(second_sets, [s[5] for s in sides])
    grad_upproj = weight_grad(second_sets, [s[6] for s in sides])
    grad_down = weight_grad(grad_sets, [s[4] for s in sides])

    gates_block = gates[:block]
    grad_logits = gates_block * (
        grad_gates - jnp.sum(gates_block * grad_gates, -1, keepdims=True)
    )
    grad_second = grad_routed + dot(
        grad_logits, router_weight.astype(F32), ((1,), (1,)), precision=HIGH
    )
    second_gained = grad_second * second_float
    grad_resid = grad_rel[:block].astype(F32) + second_scale * (
        second_gained - second_hat * jnp.mean(second_gained * second_hat, -1, keepdims=True)
    )
    grad_out_low = jnp.concatenate(gather_tensor(grad_resid.astype(BF16)), 0)
    grad_logits_all = jnp.concatenate(gather_tensor(grad_logits), 0)
    grad_second_gain = sum(gather_tensor(jnp.sum(grad_second * second_hat, 0)))
    grad_router = dot(second_group.astype(F32), grad_logits_all, ((0,), (0,)), precision=HIGH)

    grad_outproj = reduce_plane(dot(grad_out_low, attended, ((0,), (0,))))
    grad_attended = (
        dot(grad_out_low, output_weight, ((1,), (0,)))
        .astype(BF16)
        .reshape(tokens_here, kv_heads, group_size, HD)
    )
    grad_probs = jnp.einsum(
        "tkgd,ukd->kgtu", grad_attended, values_low, preferred_element_type=F32
    )
    grad_values = (
        jnp.einsum("kgtu,tkgd->ukd", probs_low, grad_attended, preferred_element_type=F32)
        .astype(BF16)
        .reshape(tokens_here, kv_heads * HD)
    )
    grad_scores = (
        probabilities * (grad_probs - jnp.sum(probabilities * grad_probs, -1, keepdims=True))
    ).astype(BF16)
    grad_queries = (
        jnp.einsum("kgtu,ukd->tkgd", grad_scores, keys_rot, preferred_element_type=F32)
        * score_scale
    )
    grad_keys = (
        jnp.einsum("kgtu,tkgd->ukd", grad_scores, grouped, preferred_element_type=F32)
        * score_scale
    )
    grad_query_pre = (
        rotate(grad_queries.reshape(tokens_here, query_heads, HD), cosine_table, -sine_table)
        .astype(BF16)
        .reshape(tokens_here, query_heads * HD)
    )
    grad_key_pre = (
        rotate(grad_keys, cosine_table, -sine_table)
        .astype(BF16)
        .reshape(tokens_here, kv_heads * HD)
    )
    grad_first = (
        dot(grad_query_pre, query_weight, ((1,), (1,)))
        + dot(grad_key_pre, key_weight, ((1,), (1,)))
        + dot(grad_values, value_weight, ((1,), (1,)))
    )
    grad_first_part = jnp.sum(grad_first * first_hat, 0)
    grad_first = reduce_tensor(grad_first, BF16)
    first_gained = grad_first * first_float
    hat_block = first_hat[:block]
    grad_input = grad_resid + first_scale[:block] * (
        first_gained - hat_block * jnp.mean(first_gained * hat_block, -1, keepdims=True)
    )
    last = jnp.concatenate(
        [
            dot(first_normed, grad_query_pre, ((0,), (0,))),
            dot(first_normed, grad_key_pre, ((0,), (0,))),
            dot(first_normed, grad_values, ((0,), (0,))),
            grad_router,
            grad_second_gain[:, None],
            grad_first_part[:, None],
        ],
        1,
    )
    last = reduce_plane(last)
    marks = [0]
    for w in (query_heads * HD, kv_heads * HD, kv_heads * HD, expert_count, 1, 1):
        marks.append(marks[-1] + w)
    grad_query, grad_key, grad_value, grad_router, grad_second_out, grad_first_out = (
        last[:, marks[i] : marks[i + 1]] for i in range(6)
    )
    grad_first_out = sum(gather_tensor(grad_first_out[:, 0]))

    layer_out = by_distance(jnp.concatenate(gather_tensor(layer_block), 0), me_t, tensor_n)
    grad_input = by_distance(
        jnp.concatenate(gather_tensor(grad_input.astype(BF16)), 0), me_t, tensor_n
    ).astype(F32)
    return (
        layer_out,
        grad_input,
        grad_first_out,
        grad_query,
        grad_key,
        grad_value,
        grad_outproj,
        grad_second_out[:, 0],
        grad_router,
        grad_gate,
        grad_upproj,
        grad_down,
    )


def solution(mesh):
    tokens = P(("dp", "expert"), None)
    columns = P(None, "tensor")
    experts = P("expert", None, "tensor")
    rows = P(("dp", "expert"))
    both = P(("dp", "expert"), "tensor")
    expert_grads = P("expert", "dp", "tensor")
    return jax.shard_map(
        on_device,
        mesh=mesh,
        in_specs=(tokens, tokens, tokens, P())
        + (columns,) * 4
        + (P(), P())
        + (experts,) * 3
        + (tokens,),
        out_specs=(tokens, tokens, rows)
        + (both,) * 4
        + (rows, tokens)
        + (expert_grads,) * 3,
        check_vma=False,
    )
```

time: 714 us -> 248 us (0.35)
  waiting for transfers between devices: 496 us -> 46.9 us
  starting transfers between devices: 20.9 us -> 72.7 us
  blocking collectives: 43.4 us -> 0 us
  other arithmetic: 47.9 us -> 25.8 us
  local copies, waits for them, and re-layouts: 40.9 us -> 55.1 us
  between operations: 15.4 us -> 4.09 us
    reduce_scatter x8 -> x0, waiting for transfers between devices: 249 us -> none  [the longest x1 39.8 us: on_device(): lax.psum_scatter(grad_query_local, ('dp', 'expert'), scatter_dimension=0,...]
    all_to_all x4 -> x0, waiting for transfers between devices: 176 us -> none  [the longest x2 123 us: send_tokens(): lax.all_to_all(expert_terms.reshape(expert_devices, local_experts * capac...]
    ppermute x0 -> x63, starting transfers between devices: none -> 72.7 us  [swap(): return lax.ppermute(x, axis, [(i, i ^ k) for i in range(n)])]
    psum x3 -> x0, waiting for transfers between devices: 70.6 us -> none  [the longest x1 26.6 us: on_device(): attn_out = lax.psum(attn_part, 'tensor')]
    ppermute x0 -> x63, waiting for transfers between devices: none -> 46.9 us  [swap(): return lax.ppermute(x, axis, [(i, i ^ k) for i in range(n)])]
    psum x2 -> x0, blocking collectives: 31.4 us -> none  [the longest x1 19.7 us: on_device(): lax.psum((grad_resid_part, grad_second_part, grad_router_part), 'tensor')]
    unnamed x102 -> x164, local copies, waits for them, and re-layouts: 3.45 us -> 28.7 us
    gather x3 -> x0, local copies, waits for them, and re-layouts: 24.4 us -> none  [the longest x2 18.5 us: send_tokens(): brought.reshape(expert_count * capacity, width_now)[destination]]
  transfers between devices with their start and end apart: 15 -> 63, of which waited for: 15 -> 25; matrix products, arithmetic and copies ran while one was open for 12% -> 47% of each run, Pallas kernels for 0% -> 0%
where the time goes in v1:
time: 248 us; the launch traced here: 247 us
  starting transfers between devices  72.7 us (29%)
  local copies, waits for them, and re-layouts  55.1 us (22%)
  waiting for transfers between devices  46.9 us (19%)
  matrix products  42.4 us (17%)
  other arithmetic  25.8 us (10%)
  between operations  4.09 us (2%)
    ppermute x63, starting transfers between devices, swap(): return lax.ppermute(x, axis, [(i, i ^ k) for i in range(n)])  72.7 us
    ppermute x63, waiting for transfers between devices, swap(): return lax.ppermute(x, axis, [(i, i ^ k) for i in range(n)])  46.9 us
    unnamed x164, local copies, waits for them, and re-layouts  28.7 us
    dot_general x16, matrix products, dot(): lax.dot_general(left, right, (dims, ((), ())), preferred_element_type=F32...  14.2 us
    dot_general x6, matrix products, weight_grad(): jnp.einsum('td,tef->edf', lax.dynamic_slice_in_dim(left, me_d * half, hal...  9.51 us
    unnamed x3, matrix products  5.21 us
    concatenate x3, local copies, waits for them, and re-layouts, on_device(): jnp.concatenate([dot(first_normed, grad_query_pre, ((0,), (0,))), dot(fir...  5.05 us
  transfers between devices with their start and end apart: 63, of which 25 were waited for; matrix products, arithmetic and copies ran while one was open for 47% of the time, Pallas kernels for 0%

profile of v1, /device:TPU:0, one launch (start us, length us, event | category | flops | bytes accessed | tf_op | source)
XLA Modules:
  0.0 247.0 jit_solution(11224662896104140373)
XLA Ops:
  5.1 3.0 %collective-permute-start.18 = (bf16[128,1024]{1,0:T(8,128)(2,1)}, bf16[128,1024]{1,0:T(8,128)(2,1)}, u32[]{:S(2)}, u32[]{:S(2)}) collective-permute-start(bf16[128,1024]{1,0:T(8,128)(2,1)} %pad_maximum_fusion.5), channel_id=1, source_target_pairs={{0,8},{4,12},{8,0},{12,4},{1,9},{5,13},{9,1},{13,5},{2,10},{6,14},... | collective-permute-start | bytes 786440 | tf_op jit(solution)/shard_map/ppermute | solution.py:54
  25.0 4.1 %collective-permute-start.2 = (bf16[32,1024]{1,0:T(8,128)(2,1)}, bf16[32,1024]{1,0:T(8,128)(2,1)}, u32[]{:S(2)}, u32[]{:S(2)}) collective-permute-start(bf16[32,1024]{1,0:T(8,128)(2,1)} %get-tuple-element.136), channel_id=1, source_target_pairs={{0,3},{1,2},{2,1},{3,0},{4,7},{5,6},{6,5},{7,4},{8,11},{9,10},{10,... | collective-permute-start | bytes 196616 | tf_op jit(solution)/shard_map/ppermute | solution.py:54
  33.7 2.6 %copy.228 = bf16[8,1024,128]{1,2,0:T(8,128)(2,1)} copy(bf16[8,1024,128]{2,1,0:T(8,128)(2,1)S(1)} %copy-done.6) | data formatting | bytes 4194304 | tf_op args[12]
  36.3 3.9 %copy.225 = bf16[8,1024,128]{1,2,0:T(8,128)(2,1)} copy(bf16[8,1024,128]{2,1,0:T(8,128)(2,1)} %param.24) | data formatting | bytes 4194304 | tf_op args[10]
  40.2 4.0 %copy.226 = bf16[8,1024,128]{1,2,0:T(8,128)(2,1)} copy(bf16[8,1024,128]{2,1,0:T(8,128)(2,1)} %param.25) | data formatting | bytes 4194304 | tf_op args[11]
  49.7 3.0 %collective-permute-done = bf16[32,1024]{1,0:T(8,128)(2,1)S(1)} collective-permute-done((bf16[32,1024]{1,0:T(8,128)(2,1)S(1)}, bf16[32,1024]{1,0:T(8,128)(2,1)S(1)}, u32[]{:S(2)}, u32[]{:S(2)}) %collective-permute-start) | collective-permute-done | bytes 65568 | tf_op jit(solution)/shard_map/ppermute | solution.py:54
  55.1 2.4 collective-permute-start.4
  60.3 3.4 %collective-permute-done.5 = bf16[32,1024]{1,0:T(8,128)(2,1)S(1)} collective-permute-done((bf16[32,1024]{1,0:T(8,128)(2,1)S(1)}, bf16[32,1024]{1,0:T(8,128)(2,1)S(1)}, u32[]{:S(2)}, u32[]{:S(2)}) %collective-permute-start.5) | collective-permute-done | bytes 65568 | tf_op jit(solution)/shard_map/ppermute | solution.py:54
  72.7 3.7 %collective-permute-done.55 = bf16[128,1024]{1,0:T(8,128)(2,1)S(1)} collective-permute-done((bf16[128,1024]{1,0:T(8,128)(2,1)}, bf16[128,1024]{1,0:T(8,128)(2,1)S(1)}, u32[]{:S(2)}, u32[]{:S(2)}) %collective-permute-start.55) | collective-permute-done | bytes 262176 | tf_op jit(solution)/shard_map/ppermute | solution.py:54
  77.4 4.1 %collective-permute-done.61 = bf16[128,1024]{1,0:T(8,128)(2,1)S(1)} collective-permute-done((bf16[128,1024]{1,0:T(8,128)(2,1)S(1)}, bf16[128,1024]{1,0:T(8,128)(2,1)S(1)}, u32[]{:S(2)}, u32[]{:S(2)}) %collective-permute-start.61) | collective-permute-done | bytes 262176 | tf_op jit(solution)/shard_map/ppermute | solution.py:54
  82.4 2.7 %fusion.101 = f32[512,1024]{0,1:S(1)} fusion(bf16[512,1024]{1,0:T(8,128)(2,1)} %constant_dynamic-update-slice_fusion.16, bf16[1024,1024]{0,1:T(8,128)(2,1)S(1)} %bitcast.310), kind=kOutput, calls=%fused_computation.264 | convolution fusion | flops 1073741824 | bytes 5242880
  100.2 2.2 collective-permute-start.27
  104.3 2.3 collective-permute-start.41
  122.0 2.1 fusion.12
  124.8 2.1 add_bitcast_fusion.1
  128.7 2.9 %copy.262 = f32[8,512,128]{2,1,0:T(8,128)} copy(f32[8,512,128]{1,2,0:T(8,128)} %add_bitcast_fusion.1) | data formatting | bytes 4194304
  131.6 2.8 %add_bitcast_fusion = f32[8,512,128]{1,2,0:T(8,128)S(1)} fusion(f32[8,128,512]{2,1,0:T(8,128)} %fusion.12, bf16[512,8,128]{0,2,1:T(8,128)(2,1)} %copy-done.2, bf16[512,1024]{1,0:T(8,128)(2,1)} %constant_dynamic-update-slice_fusion.16, s32[]{:T(128)S(6)} %select_n.127), kind=kOutput, calls=%fused_computation.4 | convolution fusion | flops 537395200 | bytes 5767172 | tf_op jit(solution)/shard_map/td,tef->edf/dot_general | solution.py:265
  141.2 5.7 %collective-permute-done.21 = bf16[128,1024]{1,0:T(8,128)(2,1)S(1)} collective-permute-done((bf16[128,1024]{1,0:T(8,128)(2,1)S(1)}, bf16[128,1024]{1,0:T(8,128)(2,1)S(1)}, u32[]{:S(2)}, u32[]{:S(2)}) %collective-permute-start.21) | collective-permute-done | bytes 262176 | tf_op jit(solution)/shard_map/ppermute | solution.py:54
  147.0 2.2 collective-permute-start.24
  152.9 2.2 collective-permute-start.14
  178.0 2.4 collective-permute-start.33
  184.8 3.0 %concatenate.129 = f32[2,2,2,128,546]{4,3,2,1,0:T(8,128)S(1)} concatenate(f32[2,2,2,128,256]{4,3,2,1,0:T(8,128)} %fusion.104, f32[2,2,2,128,128]{4,3,2,1,0:T(8,128)} %fusion.105, f32[2,2,2,128,128]{4,3,2,1,0:T(8,128)} %fusion.106, f32[2,2,2,128,32]{4,3,2,1,0:T(8,128)} %bitcast.317, f32[2,2,2,128,1]{4,3,2,1,0:T(8,128)} %copy.242, f32[2,2,2,128,1]{4,3,2,1,0:T(8,128)} %copy.243), dimensions={4} | concatenate | bytes 4472832 | tf_op jit(solution)/shard_map/concatenate | solution.py:341
  189.0 2.4 copy.246
  194.8 2.3 fusion.107
  197.9 2.2 copy.245
  201.5 3.1 %collective-permute-done.12 = bf16[32,1024]{1,0:T(8,128)(2,1)S(1)} collective-permute-done((bf16[32,1024]{1,0:T(8,128)(2,1)}, bf16[32,1024]{1,0:T(8,128)(2,1)S(1)}, u32[]{:S(2)}, u32[]{:S(2)}) %collective-permute-start.12) | collective-permute-done | bytes 65568 | tf_op jit(solution)/shard_map/ppermute | solution.py:54
  207.9 2.4 collective-permute-start.36
  214.0 2.4 collective-permute-start.15
  216.4 2.4 collective-permute-done.17
  228.7 4.4 %collective-permute-done.46 = bf16[256,546]{0,1:T(8,128)(2,1)S(1)} collective-permute-done((bf16[256,546]{0,1:T(8,128)(2,1)S(1)}, bf16[256,546]{0,1:T(8,128)(2,1)S(1)}, u32[]{:S(2)}, u32[]{:S(2)}) %collective-permute-start.46) | collective-permute-done | bytes 279584 | tf_op jit(solution)/shard_map/ppermute | solution.py:54
  235.8 2.9 %collective-permute-done.47 = bf16[128,546]{0,1:T(8,128)(2,1)S(1)} collective-permute-done((bf16[128,546]{0,1:T(8,128)(2,1)S(1)}, bf16[128,546]{0,1:T(8,128)(2,1)S(1)}, u32[]{:S(2)}, u32[]{:S(2)}) %collective-permute-start.47) | collective-permute-done | bytes 139808 | tf_op jit(solution)/shard_map/ppermute | solution.py:54
  241.3 2.3 collective-permute-start.48
  (407 shorter events, 149.4 us)
Async XLA Ops:
  5.1 61.8 %collective-permute-start.18 = (bf16[128,1024]{1,0:T(8,128)(2,1)}, bf16[128,1024]{1,0:T(8,128)(2,1)}, u32[]{:S(2)}, u32[]{:S(2)}) collective-permute-start(bf16[128,1024]{1,0:T(8,128)(2,1)} %pad_maximum_fusion.5), channel_id=1, source_target_pairs={{0,8},{4,12},{8,0},{12,4},{1,9},{5,13},{9,1},{13,5},{2,10},{6,14},... | collective-permute-start | bytes 786440 | tf_op jit(solution)/shard_map/ppermute | solution.py:54
  8.1 58.9 %collective-permute-start.54 = (bf16[128,1024]{1,0:T(8,128)(2,1)}, bf16[128,1024]{1,0:T(8,128)(2,1)}, u32[]{:S(2)}, u32[]{:S(2)}) collective-permute-start(bf16[128,1024]{1,0:T(8,128)(2,1)} %pad_maximum_fusion.5), channel_id=1, source_target_pairs={{0,16},{16,0},{1,17},{17,1},{2,18},{18,2},{3,19},{19,3},{4,20},{20... | collective-permute-start | bytes 786440 | tf_op jit(solution)/shard_map/ppermute | solution.py:54
  11.0 33.3 %collective-permute-start.8 = (bf16[128,32]{0,1:T(8,128)(2,1)}, bf16[128,32]{0,1:T(8,128)(2,1)}, u32[]{:S(2)}, u32[]{:S(2)}) collective-permute-start(bf16[128,32]{0,1:T(8,128)(2,1)} %convert_reduce_fusion), channel_id=1, source_target_pairs={{0,8},{4,12},{8,0},{12,4},{1,9},{5,13},{9,1},{13,5},{2,10},{6,14},... | collective-permute-start | bytes 24584 | tf_op jit(solution)/shard_map/ppermute | solution.py:54
  11.6 32.9 %collective-permute-start.57 = (bf16[128,32]{0,1:T(8,128)(2,1)}, bf16[128,32]{0,1:T(8,128)(2,1)}, u32[]{:S(2)}, u32[]{:S(2)}) collective-permute-start(bf16[128,32]{0,1:T(8,128)(2,1)} %convert_reduce_fusion), channel_id=1, source_target_pairs={{0,16},{16,0},{1,17},{17,1},{2,18},{18,2},{3,19},{19,3},{4,20},{20... | collective-permute-start | bytes 24584 | tf_op jit(solution)/shard_map/ppermute | solution.py:54
  25.0 24.6 %collective-permute-start.2 = (bf16[32,1024]{1,0:T(8,128)(2,1)}, bf16[32,1024]{1,0:T(8,128)(2,1)}, u32[]{:S(2)}, u32[]{:S(2)}) collective-permute-start(bf16[32,1024]{1,0:T(8,128)(2,1)} %get-tuple-element.136), channel_id=1, source_target_pairs={{0,3},{1,2},{2,1},{3,0},{4,7},{5,6},{6,5},{7,4},{8,11},{9,10},{10,... | collective-permute-start | bytes 196616 | tf_op jit(solution)/shard_map/ppermute | solution.py:54
  59.1 29.0 %collective-permute-start.9 = (bf16[256,32]{0,1:T(8,128)(2,1)S(1)}, bf16[256,32]{0,1:T(8,128)(2,1)S(1)}, u32[]{:S(2)}, u32[]{:S(2)}) collective-permute-start(bf16[256,32]{0,1:T(8,128)(2,1)S(1)} %pad_maximum_fusion.15), channel_id=1, source_target_pairs={{0,4},{4,0},{8,12},{12,8},{1,5},{5,1},{9,13},{13,9},{2,6},{6,2},{1... | collective-permute-start | bytes 49160 | tf_op jit(solution)/shard_map/ppermute | solution.py:54
  63.8 6.5 %collective-permute-start.6 = (bf16[128,1024]{1,0:T(8,128)(2,1)S(1)}, bf16[128,1024]{1,0:T(8,128)(2,1)S(1)}, u32[]{:S(2)}, u32[]{:S(2)}) collective-permute-start(bf16[128,1024]{1,0:T(8,128)(2,1)S(1)} %pad_maximum_fusion.2), channel_id=1, source_target_pairs={{0,8},{4,12},{8,0},{12,4},{1,9},{5,13},{9,1},{13,5},{2,10},{6,14},... | collective-permute-start | bytes 786440 | tf_op jit(solution)/shard_map/ppermute | solution.py:54
  65.3 6.4 %collective-permute-start.60 = (bf16[128,1024]{1,0:T(8,128)(2,1)S(1)}, bf16[128,1024]{1,0:T(8,128)(2,1)S(1)}, u32[]{:S(2)}, u32[]{:S(2)}) collective-permute-start(bf16[128,1024]{1,0:T(8,128)(2,1)S(1)} %pad_maximum_fusion.2), channel_id=1, source_target_pairs={{0,16},{16,0},{1,17},{17,1},{2,18},{18,2},{3,19},{19,3},{4,20},{20... | collective-permute-start | bytes 786440 | tf_op jit(solution)/shard_map/ppermute | solution.py:54
  66.9 51.3 %collective-permute-start.59 = (bf16[256,32]{0,1:T(8,128)(2,1)S(1)}, bf16[256,32]{0,1:T(8,128)(2,1)S(1)}, u32[]{:S(2)}, u32[]{:S(2)}) collective-permute-start(bf16[256,32]{0,1:T(8,128)(2,1)S(1)} %pad_maximum_fusion.16), channel_id=1, source_target_pairs={{0,4},{4,0},{8,12},{12,8},{1,5},{5,1},{9,13},{13,9},{2,6},{6,2},{1... | collective-permute-start | bytes 49160 | tf_op jit(solution)/shard_map/ppermute | solution.py:54
  67.0 9.4 %collective-permute-start.55 = (bf16[128,1024]{1,0:T(8,128)(2,1)}, bf16[128,1024]{1,0:T(8,128)(2,1)S(1)}, u32[]{:S(2)}, u32[]{:S(2)}) collective-permute-start(bf16[128,1024]{1,0:T(8,128)(2,1)} %collective-permute-done.54), channel_id=1, source_target_pairs={{0,8},{4,12},{8,0},{12,4},{1,9},{5,13},{9,1},{13,5},{2,10},{6,14},... | collective-permute-start | bytes 786440 | tf_op jit(solution)/shard_map/ppermute | solution.py:54
  70.3 11.3 %collective-permute-start.19 = (bf16[256,1024]{1,0:T(8,128)(2,1)S(1)}, bf16[256,1024]{1,0:T(8,128)(2,1)S(1)}, u32[]{:S(2)}, u32[]{:S(2)}) collective-permute-start(bf16[256,1024]{1,0:T(8,128)(2,1)S(1)} %get-tuple-element.124), channel_id=1, source_target_pairs={{0,4},{4,0},{8,12},{12,8},{1,5},{5,1},{9,13},{13,9},{2,6},{6,2},{1... | collective-permute-start | bytes 1572872 | tf_op jit(solution)/shard_map/ppermute | solution.py:54
  71.7 9.8 %collective-permute-start.61 = (bf16[128,1024]{1,0:T(8,128)(2,1)S(1)}, bf16[128,1024]{1,0:T(8,128)(2,1)S(1)}, u32[]{:S(2)}, u32[]{:S(2)}) collective-permute-start(bf16[128,1024]{1,0:T(8,128)(2,1)S(1)} %collective-permute-done.60), channel_id=1, source_target_pairs={{0,8},{4,12},{8,0},{12,4},{1,9},{5,13},{9,1},{13,5},{2,10},{6,14},... | collective-permute-start | bytes 786440 | tf_op jit(solution)/shard_map/ppermute | solution.py:54
  76.4 8.7 %collective-permute-start.7 = (bf16[256,1024]{1,0:T(8,128)(2,1)S(1)}, bf16[256,1024]{1,0:T(8,128)(2,1)S(1)}, u32[]{:S(2)}, u32[]{:S(2)}) collective-permute-start(bf16[256,1024]{1,0:T(8,128)(2,1)S(1)} %get-tuple-element.133), channel_id=1, source_target_pairs={{0,4},{4,0},{8,12},{12,8},{1,5},{5,1},{9,13},{13,9},{2,6},{6,2},{1... | collective-permute-start | bytes 1572872 | tf_op jit(solution)/shard_map/ppermute | solution.py:54
  81.5 32.7 %collective-permute-start.56 = (bf16[256,1024]{1,0:T(8,128)(2,1)S(1)}, bf16[256,1024]{1,0:T(8,128)(2,1)S(1)}, u32[]{:S(2)}, u32[]{:S(2)}) collective-permute-start(bf16[256,1024]{1,0:T(8,128)(2,1)S(1)} %pad_maximum_fusion), channel_id=1, source_target_pairs={{0,4},{4,0},{8,12},{12,8},{1,5},{5,1},{9,13},{13,9},{2,6},{6,2},{1... | collective-permute-start | bytes 1572872 | tf_op jit(solution)/shard_map/ppermute | solution.py:54
  104.3 8.0 %collective-permute-start.41 = (f32[32,32]{0,1:T(8,128)S(1)}, f32[32,32]{0,1:T(8,128)S(1)}, u32[]{:S(2)}, u32[]{:S(2)}) collective-permute-start(f32[32,32]{0,1:T(8,128)S(1)} %subtract_multiply_fusion), channel_id=1, source_target_pairs={{0,3},{1,2},{2,1},{3,0},{4,7},{5,6},{6,5},{7,4},{8,11},{9,10},{10,... | collective-permute-start | bytes 12296 | tf_op jit(solution)/shard_map/ppermute | solution.py:54
  112.3 23.8 %collective-permute-start.20 = (bf16[256,1024]{1,0:T(8,128)(2,1)}, bf16[256,1024]{1,0:T(8,128)(2,1)}, u32[]{:S(2)}, u32[]{:S(2)}) collective-permute-start(bf16[256,1024]{1,0:T(8,128)(2,1)} %slice.243), channel_id=1, source_target_pairs={{0,4},{4,0},{8,12},{12,8},{1,5},{5,1},{9,13},{13,9},{2,6},{6,2},{1... | collective-permute-start | bytes 1572872 | tf_op jit(solution)/shard_map/ppermute | solution.py:54
  112.8 26.4 %collective-permute-start.10 = (bf16[256,1024]{1,0:T(8,128)(2,1)}, bf16[256,1024]{1,0:T(8,128)(2,1)}, u32[]{:S(2)}, u32[]{:S(2)}) collective-permute-start(bf16[256,1024]{1,0:T(8,128)(2,1)} %slice.235), channel_id=1, source_target_pairs={{0,4},{4,0},{8,12},{12,8},{1,5},{5,1},{9,13},{13,9},{2,6},{6,2},{1... | collective-permute-start | bytes 1572872 | tf_op jit(solution)/shard_map/ppermute | solution.py:54
  137.7 9.2 %collective-permute-start.21 = (bf16[128,1024]{1,0:T(8,128)(2,1)S(1)}, bf16[128,1024]{1,0:T(8,128)(2,1)S(1)}, u32[]{:S(2)}, u32[]{:S(2)}) collective-permute-start(bf16[128,1024]{1,0:T(8,128)(2,1)S(1)} %slice.245), channel_id=1, source_target_pairs={{0,8},{4,12},{8,0},{12,4},{1,9},{5,13},{9,1},{13,5},{2,10},{6,14},... | collective-permute-start | bytes 786440 | tf_op jit(solution)/shard_map/ppermute | solution.py:54
  140.5 11.6 %collective-permute-start.11 = (bf16[128,1024]{1,0:T(8,128)(2,1)S(1)}, bf16[128,1024]{1,0:T(8,128)(2,1)S(1)}, u32[]{:S(2)}, u32[]{:S(2)}) collective-permute-start(bf16[128,1024]{1,0:T(8,128)(2,1)S(1)} %slice.237), channel_id=1, source_target_pairs={{0,8},{4,12},{8,0},{12,4},{1,9},{5,13},{9,1},{13,5},{2,10},{6,14},... | collective-permute-start | bytes 786440 | tf_op jit(solution)/shard_map/ppermute | solution.py:54
  147.0 8.3 %collective-permute-start.24 = (bf16[32,1024]{1,0:T(8,128)(2,1)S(1)}, bf16[32,1024]{1,0:T(8,128)(2,1)S(1)}, u32[]{:S(2)}, u32[]{:S(2)}) collective-permute-start(bf16[32,1024]{1,0:T(8,128)(2,1)S(1)} %get-tuple-element.122), channel_id=1, source_target_pairs={{0,3},{1,2},{2,1},{3,0},{4,7},{5,6},{6,5},{7,4},{8,11},{9,10},{10,... | collective-permute-start | bytes 196616 | tf_op jit(solution)/shard_map/ppermute | solution.py:54
  152.9 48.6 %collective-permute-start.14 = (bf16[32,1024]{1,0:T(8,128)(2,1)}, bf16[32,1024]{1,0:T(8,128)(2,1)}, u32[]{:S(2)}, u32[]{:S(2)}) collective-permute-start(bf16[32,1024]{1,0:T(8,128)(2,1)} %get-tuple-element.131), channel_id=1, source_target_pairs={{0,3},{1,2},{2,1},{3,0},{4,7},{5,6},{6,5},{7,4},{8,11},{9,10},{10,... | collective-permute-start | bytes 196616 | tf_op jit(solution)/shard_map/ppermute | solution.py:54
  155.1 46.4 %collective-permute-start.13 = (bf16[32,1024]{1,0:T(8,128)(2,1)}, bf16[32,1024]{1,0:T(8,128)(2,1)}, u32[]{:S(2)}, u32[]{:S(2)}) collective-permute-start(bf16[32,1024]{1,0:T(8,128)(2,1)} %get-tuple-element.132), channel_id=1, source_target_pairs={{0,2},{1,3},{2,0},{3,1},{4,6},{5,7},{6,4},{7,5},{8,10},{9,11},{10,... | collective-permute-start | bytes 196616 | tf_op jit(solution)/shard_map/ppermute | solution.py:54
  161.6 6.6 %collective-permute-start.32 = (bf16[32,1024]{1,0:T(8,128)(2,1)S(1)}, bf16[32,1024]{1,0:T(8,128)(2,1)S(1)}, u32[]{:S(2)}, u32[]{:S(2)}) collective-permute-start(bf16[32,1024]{1,0:T(8,128)(2,1)S(1)} %fusion.84), channel_id=1, source_target_pairs={{0,3},{1,2},{2,1},{3,0},{4,7},{5,6},{6,5},{7,4},{8,11},{9,10},{10,... | collective-permute-start | bytes 196616 | tf_op jit(solution)/shard_map/ppermute | solution.py:54
  176.0 24.1 %collective-permute-start.35 = (bf16[32,1024]{1,0:T(8,128)(2,1)}, bf16[32,1024]{1,0:T(8,128)(2,1)S(1)}, u32[]{:S(2)}, u32[]{:S(2)}) collective-permute-start(bf16[32,1024]{1,0:T(8,128)(2,1)} %get-tuple-element.119), channel_id=1, source_target_pairs={{0,3},{1,2},{2,1},{3,0},{4,7},{5,6},{6,5},{7,4},{8,11},{9,10},{10,... | collective-permute-start | bytes 196616 | tf_op jit(solution)/shard_map/ppermute | solution.py:54
  178.0 22.1 %collective-permute-start.34 = (bf16[32,1024]{1,0:T(8,128)(2,1)}, bf16[32,1024]{1,0:T(8,128)(2,1)}, u32[]{:S(2)}, u32[]{:S(2)}) collective-permute-start(bf16[32,1024]{1,0:T(8,128)(2,1)} %get-tuple-element.120), channel_id=1, source_target_pairs={{0,2},{1,3},{2,0},{3,1},{4,6},{5,7},{6,4},{7,5},{8,10},{9,11},{10,... | collective-permute-start | bytes 196616 | tf_op jit(solution)/shard_map/ppermute | solution.py:54
  178.0 22.2 %collective-permute-start.33 = (bf16[32,1024]{1,0:T(8,128)(2,1)}, bf16[32,1024]{1,0:T(8,128)(2,1)}, u32[]{:S(2)}, u32[]{:S(2)}) collective-permute-start(bf16[32,1024]{1,0:T(8,128)(2,1)} %get-tuple-element.118), channel_id=1, source_target_pairs={{0,1},{1,0},{2,3},{3,2},{4,5},{5,4},{6,7},{7,6},{8,9},{9,8},{10,11... | collective-permute-start | bytes 196616 | tf_op jit(solution)/shard_map/ppermute | solution.py:54
  200.2 23.1 %collective-permute-start.45 = (bf16[512,546]{0,1:T(8,128)(2,1)}, bf16[512,546]{0,1:T(8,128)(2,1)}, u32[]{:S(2)}, u32[]{:S(2)}) collective-permute-start(bf16[512,546]{0,1:T(8,128)(2,1)} %copy.245), channel_id=1, source_target_pairs={{0,4},{4,0},{8,12},{12,8},{1,5},{5,1},{9,13},{13,9},{2,6},{6,2},{1... | collective-permute-start | bytes 1677320 | tf_op jit(solution)/shard_map/ppermute | solution.py:54
  210.4 11.3 %collective-permute-start.51 = (bf16[512,256]{1,0:T(8,128)(2,1)S(1)}, bf16[512,256]{1,0:T(8,128)(2,1)S(1)}, u32[]{:S(2)}, u32[]{:S(2)}) collective-permute-start(bf16[512,256]{1,0:T(8,128)(2,1)S(1)} %bitcast.328), channel_id=1, source_target_pairs={{0,4},{4,0},{8,12},{12,8},{1,5},{5,1},{9,13},{13,9},{2,6},{6,2},{1... | collective-permute-start | bytes 786440 | tf_op jit(solution)/shard_map/ppermute | solution.py:54
  212.0 6.9 %collective-permute-start.17 = (bf16[32,1024]{1,0:T(8,128)(2,1)S(1)}, bf16[32,1024]{1,0:T(8,128)(2,1)S(1)}, u32[]{:S(2)}, u32[]{:S(2)}) collective-permute-start(bf16[32,1024]{1,0:T(8,128)(2,1)S(1)} %get-tuple-element.147), channel_id=1, source_target_pairs={{0,3},{1,2},{2,1},{3,0},{4,7},{5,6},{6,5},{7,4},{8,11},{9,10},{10,... | collective-permute-start | bytes 196616 | tf_op jit(solution)/shard_map/ppermute | solution.py:54
  226.4 6.7 %collective-permute-start.46 = (bf16[256,546]{0,1:T(8,128)(2,1)S(1)}, bf16[256,546]{0,1:T(8,128)(2,1)S(1)}, u32[]{:S(2)}, u32[]{:S(2)}) collective-permute-start(bf16[256,546]{0,1:T(8,128)(2,1)S(1)} %bitcast.322), channel_id=1, source_target_pairs={{0,8},{4,12},{8,0},{12,4},{1,9},{5,13},{9,1},{13,5},{2,10},{6,14},... | collective-permute-start | bytes 838664 | tf_op jit(solution)/shard_map/ppermute | solution.py:54
  227.3 7.8 %collective-permute-start.53 = (bf16[128,256]{1,0:T(8,128)(2,1)S(1)}, bf16[128,256]{1,0:T(8,128)(2,1)S(1)}, u32[]{:S(2)}, u32[]{:S(2)}) collective-permute-start(bf16[128,256]{1,0:T(8,128)(2,1)S(1)} %fusion.44), channel_id=1, source_target_pairs={{0,16},{16,0},{1,17},{17,1},{2,18},{18,2},{3,19},{19,3},{4,20},{20... | collective-permute-start | bytes 196616 | tf_op jit(solution)/shard_map/ppermute | solution.py:54
  239.2 7.2 %collective-permute-start.50 = (f32[128]{0:T(128)S(1)}, f32[128]{0:T(128)S(1)}, u32[]{:S(2)}, u32[]{:S(2)}) collective-permute-start(f32[128]{0:T(128)S(1)} %get-tuple-element.110), channel_id=1, source_target_pairs={{0,3},{1,2},{2,1},{3,0},{4,7},{5,6},{6,5},{7,4},{8,11},{9,10},{10,... | collective-permute-start | bytes 1544 | tf_op jit(solution)/shard_map/ppermute | solution.py:54
  (99 other events, 796.4 us)

commit v2 on v1

--- a/solution.py
+++ b/solution.py
@@ -1,8 +1,11 @@
+import functools
 import math
 
 import jax
 import jax.numpy as jnp
 from jax import lax
+from jax.experimental import pallas as pl
+from jax.experimental.pallas import tpu as pltpu
 from jax.sharding import PartitionSpec as P
 
 HD = 64
@@ -121,6 +124,253 @@
         sent = lax.dynamic_index_in_dim(x, mine ^ k, 0, keepdims=False)
         total = total + swap(sent.astype(BF16), "dp", k).astype(F32)
     return total
+
+
+def pair_of(local_experts):
+    return 2 if local_experts % 2 == 0 else 1
+
+
+def kernel_params(tokens):
+    return pltpu.CompilerParams(vmem_limit_bytes=(40 if tokens <= 512 else 60) * 2**20)
+
+
+def side_by_side(ref, first, count):
+    parts = [ref[first + i] for i in range(count)]
+    return parts[0] if count == 1 else jnp.concatenate(parts, 1)
+
+
+def split_rows(chunk, chunks, value, near_ref, far_ref):
+    if chunks == 1:
+        half = value.shape[0] // 2
+        near_ref[...] = value[:half]
+        far_ref[...] = value[half:]
+        return
+    rows = value.shape[0]
+
+    @pl.when(chunk < chunks // 2)
+    def _():
+        near_ref[pl.ds(pl.multiple_of(chunk * rows, rows), rows), :] = value
+
+    @pl.when(chunk >= chunks // 2)
+    def _():
+        at = (chunk - chunks // 2) * rows
+        far_ref[pl.ds(pl.multiple_of(at, rows), rows), :] = value
+
+
+def expert_kernel(own, chunks, steps, pair, experts, *refs):
+    base_ref, x_ref, dy_ref, gate_ref, up_ref, down_ref, router_ref = refs[:7]
+    both_ref, gated_ref = refs[7:9]
+    if own:
+        near_ref, far_ref = refs[9:11]
+        gates_scr, total_scr, dg_scr = refs[11:]
+    else:
+        (gates_scr,) = refs[9:]
+    chunk, step = pl.program_id(0), pl.program_id(1)
+    width = x_ref.shape[1]
+    lanes = gates_scr.shape[1]
+
+    @pl.when(step == 0)
+    def _():
+        logits = dot(x_ref[...], router_ref[...], ((1,), (0,)))
+        routed = dy_ref[:, width : width + experts].astype(F32) > 0.5
+        logits = jnp.where(routed, logits, -1e30)
+        weights = jnp.exp(logits - jnp.max(logits, -1, keepdims=True))
+        gates_scr[...] = jnp.zeros_like(gates_scr)
+        gates_scr[:, :experts] = weights / jnp.sum(weights, -1, keepdims=True)
+        if own:
+            total_scr[...] = jnp.zeros_like(total_scr)
+            dg_scr[...] = jnp.zeros_like(dg_scr)
+
+    first = base_ref[0] + step * pair
+    gates = pltpu.roll(gates_scr[...], lax.rem(lanes - first, lanes), 1)
+    raw_all = dot(dy_ref[:, :width], side_by_side(down_ref, 0, pair), ((1,), (0,)))
+    units = gate_ref.shape[2]
+    column = lax.broadcasted_iota(jnp.int32, gates.shape, 1)
+    for i in range(pair):
+        weight = jnp.concatenate([gate_ref[i], up_ref[i]], 1)
+        both = dot(x_ref[...], weight, ((1,), (0,)))
+        gate_proj, up_proj = both[:, :units], both[:, units:]
+        raw = raw_all[:, i * units : (i + 1) * units]
+        mine = gates[:, i : i + 1]
+        sigmoid_gate = 0.5 * jnp.tanh(0.5 * gate_proj) + 0.5
+        activated = gate_proj * sigmoid_gate
+        hidden = activated * up_proj
+        grad_hidden = raw * mine
+        grad_gate = grad_hidden * up_proj * (sigmoid_gate + activated * (1.0 - sigmoid_gate))
+        grads = jnp.concatenate([grad_gate, grad_hidden * activated], 1).astype(BF16)
+        both_ref[:, i * 2 * units : (i + 1) * 2 * units] = grads
+        gated_ref[:, i * units : (i + 1) * units] = (hidden * mine).astype(BF16)
+        if own:
+            total_scr[...] += dot(grads, weight, ((1,), (1,)))
+            dg = jnp.sum(raw * hidden, 1, keepdims=True)
+            dg_scr[...] += jnp.where(column == first + i, dg, 0.0)
+
+    if own:
+
+        @pl.when(step == steps - 1)
+        def _():
+            dg = dg_scr[...]
+            high = dg.astype(BF16).astype(F32)
+            low = pltpu.roll(dg - high, experts, 1)
+            message = jnp.concatenate([total_scr[...], high + low], 1).astype(BF16)
+            split_rows(chunk, chunks, message, near_ref, far_ref)
+
+
+def expert_call(own, base, x, dy, gate_weight, up_weight, down_weight, router_weight):
+    tokens, width = x.shape
+    local, _, units = gate_weight.shape
+    experts = router_weight.shape[1]
+    pair = pair_of(local)
+    rows = min(tokens, 512)
+    chunks, steps = tokens // rows, local // pair
+    grid_spec = dict(
+        grid=(chunks, steps),
+        in_specs=[
+            pl.BlockSpec(memory_space=pltpu.SMEM),
+            pl.BlockSpec((rows, width), lambda c, s: (c, 0)),
+            pl.BlockSpec((rows, dy.shape[1]), lambda c, s: (c, 0)),
+        ]
+        + [pl.BlockSpec((pair, width, units), lambda c, s: (s, 0, 0))] * 3
+        + [pl.BlockSpec(router_weight.shape, lambda c, s: (0, 0))],
+        out_specs=[
+            pl.BlockSpec((rows, pair * 2 * units), lambda c, s: (c, s)),
+            pl.BlockSpec((rows, pair * units), lambda c, s: (c, s)),
+        ],
+        scratch_shapes=[pltpu.VMEM((rows, 128), F32)],
+    )
+    out_shape = [
+        jax.ShapeDtypeStruct((tokens, local * 2 * units), BF16),
+        jax.ShapeDtypeStruct((tokens, local * units), BF16),
+    ]
+    if own:
+        half = (tokens // 2, width + 128)
+        grid_spec["out_specs"] += [pl.BlockSpec(half, lambda c, s: (0, 0))] * 2
+        out_shape += [jax.ShapeDtypeStruct(half, BF16)] * 2
+        grid_spec["scratch_shapes"] += [
+            pltpu.VMEM((rows, width), F32),
+            pltpu.VMEM((rows, 128), F32),
+        ]
+    products = 5 if own else 3
+    return pl.pallas_call(
+        functools.partial(expert_kernel, own, chunks, steps, pair, experts),
+        out_shape=out_shape,
+        compiler_params=kernel_params(tokens),
+        cost_estimate=pl.CostEstimate(
+            flops=2 * products * tokens * width * local * units,
+            bytes_accessed=2 * (3 * local * width * units + 3 * tokens * width),
+            transcendentals=tokens * local * units,
+        ),
+        name="experts_own" if own else "experts_far",
+        **grid_spec,
+    )(base, x, dy, gate_weight, up_weight, down_weight, router_weight)
+
+
+def mixed_kernel(chunks, steps, pair, gated_ref, down_ref, near_ref, far_ref, total_scr):
+    chunk, step = pl.program_id(0), pl.program_id(1)
+
+    @pl.when(step == 0)
+    def _():
+        total_scr[...] = jnp.zeros_like(total_scr)
+
+    total_scr[...] += dot(gated_ref[...], side_by_side(down_ref, 0, pair), ((1,), (1,)))
+
+    @pl.when(step == steps - 1)
+    def _():
+        split_rows(chunk, chunks, total_scr[...].astype(BF16), near_ref, far_ref)
+
+
+def mixed_call(gated, down_weight):
+    tokens = gated.shape[0]
+    local, width, units = down_weight.shape
+    pair = pair_of(local)
+    rows = min(tokens, 512)
+    chunks, steps = tokens // rows, local // pair
+    half = (tokens // 2, width)
+    return pl.pallas_call(
+        functools.partial(mixed_kernel, chunks, steps, pair),
+        grid=(chunks, steps),
+        in_specs=[
+            pl.BlockSpec((rows, pair * units), lambda c, s: (c, s)),
+            pl.BlockSpec((pair, width, units), lambda c, s: (s, 0, 0)),
+        ],
+        out_specs=[pl.BlockSpec(half, lambda c, s: (0, 0))] * 2,
+        out_shape=[jax.ShapeDtypeStruct(half, BF16)] * 2,
+        scratch_shapes=[pltpu.VMEM((rows, width), F32)],
+        compiler_params=kernel_params(tokens),
+        cost_estimate=pl.CostEstimate(
+            flops=2 * tokens * width * local * units,
+            bytes_accessed=2 * (local * width * units + 2 * tokens * width),
+            transcendentals=0,
+        ),
+        name="experts_mixed",
+    )(gated, down_weight)
+
+
+def weight_grad_kernel(sets, pair, units, place_ref, *refs):
+    xs, dys, boths, gateds = (refs[i * sets : (i + 1) * sets] for i in range(4))
+    grad_gate_ref, grad_up_ref, grad_down_ref, x_scr, dy_scr = refs[4 * sets :]
+
+    @pl.when(pl.program_id(0) == 0)
+    def _():
+        for n in range(sets):
+            rows = xs[n].shape[0]
+            x_scr[:, n * rows : (n + 1) * rows] = xs[n][...].T
+            dy_scr[:, n * rows : (n + 1) * rows] = dys[n][...].T
+
+    rows = xs[0].shape[0]
+    totals = [None] * pair
+    down = None
+    for n in range(sets):
+        left = x_scr[:, n * rows : (n + 1) * rows]
+        for i in range(pair):
+            part = dot(left, boths[n][:, i * 2 * units : (i + 1) * 2 * units], ((1,), (0,)))
+            totals[i] = part if totals[i] is None else totals[i] + part
+        part = dot(dy_scr[:, n * rows : (n + 1) * rows], gateds[n][...], ((1,), (0,)))
+        down = part if down is None else down + part
+    for i in range(pair):
+        grad_gate_ref[i] = totals[i][:, :units]
+        grad_up_ref[i] = totals[i][:, units:]
+        grad_down_ref[i] = down[:, i * units : (i + 1) * units]
+
+
+def weight_grad_call(place, xs, dys, boths, gateds, local, units):
+    sets = len(xs)
+    tokens, width = xs[0].shape
+    half = width // sets
+    pair = pair_of(local)
+    once = pl.Buffered(1)
+    grads = jax.ShapeDtypeStruct((local, half, units), F32)
+    columns = pl.BlockSpec((tokens, half), lambda s, place: (0, place[0]), pipeline_mode=once)
+    return pl.pallas_call(
+        functools.partial(weight_grad_kernel, sets, pair, units),
+        grid_spec=pltpu.PrefetchScalarGridSpec(
+            num_scalar_prefetch=1,
+            grid=(local // pair,),
+            in_specs=[columns] * (2 * sets)
+            + [pl.BlockSpec((tokens, pair * 2 * units), lambda s, place: (0, s))] * sets
+            + [pl.BlockSpec((tokens, pair * units), lambda s, place: (0, s))] * sets,
+            out_specs=[pl.BlockSpec((pair, half, units), lambda s, place: (s, 0, 0))] * 3,
+            scratch_shapes=[pltpu.VMEM((half, sets * tokens), BF16)] * 2,
+        ),
+        out_shape=[grads] * 3,
+        compiler_params=kernel_params(tokens),
+        cost_estimate=pl.CostEstimate(
+            flops=6 * sets * tokens * half * local * units,
+            bytes_accessed=4 * 3 * local * half * units + 8 * sets * tokens * width,
+            transcendentals=0,
+        ),
+        name="experts_weight_grads",
+    )(place, *xs, *dys, *boths, *gateds)
+
+
+def reduce_halves(near, far, dtype):
+    bits = list(reversed(bits_of(lax.axis_size("expert"))))
+    for k in bits[:-1]:
+        got = swap(far, "expert", k)
+        half = near.shape[0] // 2
+        far = (near[half:].astype(F32) + got[half:].astype(F32)).astype(dtype)
+        near = (near[:half].astype(F32) + got[:half].astype(F32)).astype(dtype)
+    return near.astype(F32) + swap(far, "expert", bits[-1]).astype(F32)
 
 
 def on_device(
@@ -160,12 +410,12 @@
         + jnp.arange(block, dtype=jnp.int32)[None, :]
     ).reshape(-1)
 
-    expert_ids = jnp.arange(expert_count, dtype=jnp.int32)
+    expert_ids = jnp.arange(128, dtype=jnp.int32)
     routed = jnp.sum((routes_rel[:, :, None] == expert_ids).astype(F32), 1).astype(BF16)
-    grad_far = [swap(grad_rel, "dp", k) for k in range(1, dp_n)]
-    routed_far = [swap(routed, "dp", k) for k in range(1, dp_n)]
-    grad_sets = [gather_expert(g) for g in [grad_rel] + grad_far]
-    routed_sets = [gather_expert(g) for g in [routed] + routed_far]
+    grad_own = jnp.concatenate([grad_rel, routed], 1)
+    grad_sets = [gather_expert(grad_own)] + [
+        gather_expert(swap(grad_own, "dp", k)) for k in range(1, dp_n)
+    ]
 
     hidden_float = hidden_rel.astype(F32)
     first_scale = lax.rsqrt(jnp.mean(hidden_float * hidden_float, -1, keepdims=True) + EPSILON)
@@ -211,71 +461,35 @@
         gather_expert(swap(second_group, "dp", k)) for k in range(1, dp_n)
     ]
 
-    def gates_of(normed, routed_here):
-        logits = dot(normed, router_weight, ((1,), (0,)))
-        logits = jnp.where(routed_here > 0, logits, -1e30)
-        weights = jnp.exp(logits - jnp.max(logits, -1, keepdims=True))
-        return weights / jnp.sum(weights, -1, keepdims=True)
-
-    def expert_side(normed, routed_here, grad_here):
-        gates = gates_of(normed, routed_here)
-        mine = lax.dynamic_slice_in_dim(gates, me_e * local_experts, local_experts, 1)
-        raw = jnp.einsum("td,edf->tef", grad_here, down_weight, preferred_element_type=F32)
-        gate_proj = jnp.einsum("td,edf->tef", normed, gate_weight, preferred_element_type=F32)
-        up_proj = jnp.einsum("td,edf->tef", normed, up_weight, preferred_element_type=F32)
-        sigmoid_gate = jax.nn.sigmoid(gate_proj)
-        activated = gate_proj * sigmoid_gate
-        hidden = activated * up_proj
-        grad_hidden = raw * mine[:, :, None]
-        grad_gate_proj = (
-            grad_hidden * up_proj * sigmoid_gate * (1.0 + gate_proj * (1.0 - sigmoid_gate))
-        ).astype(BF16)
-        grad_up_proj = (grad_hidden * activated).astype(BF16)
-        gated = (hidden * mine[:, :, None]).astype(BF16)
-        return gates, mine, raw, hidden, gated, grad_gate_proj, grad_up_proj
-
+    base = jnp.reshape(me_e * local_experts, (1,)).astype(jnp.int32)
+    weights = (gate_weight, up_weight, down_weight, router_weight)
     sides = [
-        expert_side(second_sets[i], routed_sets[i], grad_sets[i]) for i in range(dp_n)
+        expert_call(i == 0, base, second_sets[i], grad_sets[i], *weights) for i in range(dp_n)
     ]
-    gates, mine, raw, hidden, gated, grad_gate_proj, grad_up_proj = sides[0]
-    grad_arrival = jnp.einsum(
-        "tef,edf->td", grad_gate_proj, gate_weight, preferred_element_type=F32
-    ) + jnp.einsum("tef,edf->td", grad_up_proj, up_weight, preferred_element_type=F32)
-    grad_arrival = grad_arrival.astype(BF16)
-    grad_gates_mine = jnp.sum(raw * hidden, -1).T
-    grad_gates = lax.dynamic_update_slice_in_dim(
-        jnp.zeros((expert_count, grad_gates_mine.shape[1]), F32),
-        grad_gates_mine,
-        me_e * local_experts,
-        0,
-    )
-    grad_routed = reduce_tensor(reduce_expert(grad_arrival, BF16), BF16)
-    grad_gates = reduce_tensor(reduce_expert(grad_gates, F32, 1), F32, 1).T
-    if tokens_here * expert_n > 1024:
-        gated, grad_routed = lax.optimization_barrier((gated, grad_routed))
-    mixed = jnp.einsum("tef,edf->td", gated, down_weight, preferred_element_type=F32)
-    mixed = mixed.astype(BF16)
-    mixed = reduce_tensor(reduce_expert(mixed, BF16), BF16)
+    arrival = reduce_tensor(reduce_halves(sides[0][2], sides[0][3], BF16), BF16)
+    mixed = mixed_call(sides[0][1], down_weight)
+    mixed = reduce_tensor(reduce_halves(mixed[0], mixed[1], BF16), BF16)
     layer_block = (residual + mixed).astype(BF16)
-
-    half = model_width // dp_n
-
-    def weight_grad(lefts, rights):
-        return sum(
-            jnp.einsum(
-                "td,tef->edf",
-                lax.dynamic_slice_in_dim(left, me_d * half, half, 1),
-                right,
-                preferred_element_type=F32,
-            )
-            for left, right in zip(lefts, rights)
-        )
-
-    grad_gate = weight_grad(second_sets, [s[5] for s in sides])
-    grad_upproj = weight_grad(second_sets, [s[6] for s in sides])
-    grad_down = weight_grad(grad_sets, [s[4] for s in sides])
-
-    gates_block = gates[:block]
+    place = jnp.reshape(me_d, (1,)).astype(jnp.int32)
+    grad_gate, grad_upproj, grad_down = weight_grad_call(
+        place,
+        second_sets,
+        grad_sets,
+        [s[0] for s in sides],
+        [s[1] for s in sides],
+        local_experts,
+        units,
+    )
+
+    logits = dot(second_block, router_weight, ((1,), (0,)))
+    logits = jnp.where(grad_own[:block, model_width : model_width + expert_count] > 0, logits, -1e30)
+    gates_block = jnp.exp(logits - jnp.max(logits, -1, keepdims=True))
+    gates_block = gates_block / jnp.sum(gates_block, -1, keepdims=True)
+    grad_routed = arrival[:, :model_width]
+    grad_gates = (
+        arrival[:, model_width : model_width + expert_count]
+        + arrival[:, model_width + expert_count : model_width + 2 * expert_count]
+    )
     grad_logits = gates_block * (
         grad_gates - jnp.sum(gates_block * grad_gates, -1, keepdims=True)
     )

time: 248 us -> 187 us (0.75)
  local copies, waits for them, and re-layouts: 55.1 us -> 25.9 us
  matrix products: 42.4 us -> 13.3 us
  Pallas kernels: 0 us -> 24.3 us
  other arithmetic: 25.8 us -> 12.8 us
  starting transfers between devices: 72.7 us -> 61.3 us
    pallas_call x0 -> x4, Pallas kernels: none -> 24.3 us  [the longest x2 15.3 us: expert_call(): pl.pallas_call(functools.partial(expert_kernel, own, chunks, steps, pair,...]
    unnamed x164 -> x129, local copies, waits for them, and re-layouts: 28.7 us -> 6.57 us
    dot_general x12 -> x0, matrix products: 17.6 us -> none  [the longest x6 9.51 us: weight_grad(): jnp.einsum('td,tef->edf', lax.dynamic_slice_in_dim(left, me_d * half, hal...]
    ppermute x63 -> x53, starting transfers between devices: 72.7 us -> 61.3 us  [swap(): return lax.ppermute(x, axis, [(i, i ^ k) for i in range(n)])]
    unnamed x3 -> x0, matrix products: 5.21 us -> none
    convert_element_type x5 -> x2, other arithmetic: 4.69 us -> 0.14 us  [reduce_halves(): far = (near[half:].astype(F32) + got[half:].astype(F32)).astype(dtype)]
    dot_general x16 -> x15, matrix products: 14.2 us -> 10.2 us  [dot(): lax.dot_general(left, right, (dims, ((), ())), preferred_element_type=F32...]
    concatenate x6 -> x4, local copies, waits for them, and re-layouts: 2.7 us -> 0.2 us  [gather_expert(): x = jnp.concatenate([x, swap(x, 'expert', k)], axis)]
  transfers between devices with their start and end apart: 63 -> 53, of which waited for: 25 -> 17; matrix products, arithmetic and copies ran while one was open for 47% -> 24% of each run, Pallas kernels for 0% -> 13%
where the time goes in v2:
time: 187 us; the launch traced here: 186 us
  starting transfers between devices  61.3 us (33%)
  waiting for transfers between devices  44.5 us (24%)
  local copies, waits for them, and re-layouts  25.9 us (14%)
  Pallas kernels  24.3 us (13%)
  matrix products  13.3 us (7%)
  other arithmetic  12.8 us (7%)
  between operations  4.01 us (2%)
    ppermute x53, starting transfers between devices, swap(): return lax.ppermute(x, axis, [(i, i ^ k) for i in range(n)])  61.3 us
    ppermute x53, waiting for transfers between devices, swap(): return lax.ppermute(x, axis, [(i, i ^ k) for i in range(n)])  44.5 us
    pallas_call x2, Pallas kernels, expert_call(): pl.pallas_call(functools.partial(expert_kernel, own, chunks, steps, pair,...  15.3 us
    dot_general x15, matrix products, dot(): lax.dot_general(left, right, (dims, ((), ())), preferred_element_type=F32...  10.2 us
    pallas_call x1, Pallas kernels, weight_grad_call(): pl.pallas_call(functools.partial(weight_grad_kernel, sets, pair, units),...  6.66 us
    unnamed x129, local copies, waits for them, and re-layouts  6.57 us
    concatenate x3, local copies, waits for them, and re-layouts, on_device(): jnp.concatenate([dot(first_normed, grad_query_pre, ((0,), (0,))), dot(fir...  5.07 us
  transfers between devices with their start and end apart: 53, of which 17 were waited for; matrix products, arithmetic and copies ran while one was open for 24% of the time, Pallas kernels for 13%

profile of v2, /device:TPU:0, one launch (start us, length us, event | category | flops | bytes accessed | tf_op | source)
XLA Modules:
  0.0 186.1 jit_solution(8595347201575439082)
XLA Ops:
  3.8 3.0 %collective-permute-start.8 = (bf16[128,1152]{1,0:T(8,128)(2,1)}, bf16[128,1152]{1,0:T(8,128)(2,1)S(1)}, u32[]{:S(2)}, u32[]{:S(2)}) collective-permute-start(bf16[128,1152]{1,0:T(8,128)(2,1)} %pad_maximum_fusion.4), channel_id=1, source_target_pairs={{0,8},{4,12},{8,0},{12,4},{1,9},{5,13},{9,1},{13,5},{2,10},{6,14},... | collective-permute-start | bytes 884744 | tf_op jit(solution)/shard_map/ppermute | solution.py:57
  18.7 3.6 %collective-permute-start.2 = (bf16[32,1024]{1,0:T(8,128)(2,1)}, bf16[32,1024]{1,0:T(8,128)(2,1)}, u32[]{:S(2)}, u32[]{:S(2)}) collective-permute-start(bf16[32,1024]{1,0:T(8,128)(2,1)} %get-tuple-element.161), channel_id=1, source_target_pairs={{0,3},{1,2},{2,1},{3,0},{4,7},{5,6},{6,5},{7,4},{8,11},{9,10},{10,... | collective-permute-start | bytes 196616 | tf_op jit(solution)/shard_map/ppermute | solution.py:57
  25.6 2.3 %collective-permute-done.1 = bf16[32,1024]{1,0:T(8,128)(2,1)} collective-permute-done((bf16[32,1024]{1,0:T(8,128)(2,1)}, bf16[32,1024]{1,0:T(8,128)(2,1)}, u32[]{:S(2)}, u32[]{:S(2)}) %collective-permute-start.1) | collective-permute-done | bytes 65568 | tf_op jit(solution)/shard_map/ppermute | solution.py:57
  30.1 2.1 %collective-permute-start.4 = (bf16[32,1024]{1,0:T(8,128)(2,1)S(1)}, bf16[32,1024]{1,0:T(8,128)(2,1)S(1)}, u32[]{:S(2)}, u32[]{:S(2)}) collective-permute-start(bf16[32,1024]{1,0:T(8,128)(2,1)S(1)} %get-tuple-element.127), channel_id=1, source_target_pairs={{0,2},{1,3},{2,0},{3,1},{4,6},{5,7},{6,4},{7,5},{8,10},{9,11},{10,... | collective-permute-start | bytes 196616 | tf_op jit(solution)/shard_map/ppermute | solution.py:57
  36.2 2.1 %collective-permute-done.5 = bf16[32,1024]{1,0:T(8,128)(2,1)S(1)} collective-permute-done((bf16[32,1024]{1,0:T(8,128)(2,1)S(1)}, bf16[32,1024]{1,0:T(8,128)(2,1)S(1)}, u32[]{:S(2)}, u32[]{:S(2)}) %collective-permute-start.5) | collective-permute-done | bytes 65568 | tf_op jit(solution)/shard_map/ppermute | solution.py:57
  39.7 1.6 collective-permute-start.51
  41.3 5.5 %collective-permute-done.6 = bf16[128,1024]{1,0:T(8,128)(2,1)S(1)} collective-permute-done((bf16[128,1024]{1,0:T(8,128)(2,1)S(1)}, bf16[128,1024]{1,0:T(8,128)(2,1)S(1)}, u32[]{:S(2)}, u32[]{:S(2)}) %collective-permute-start.6) | collective-permute-done | bytes 262176 | tf_op jit(solution)/shard_map/ppermute | solution.py:57
  47.0 5.0 %collective-permute-done.51 = bf16[128,1152]{1,0:T(8,128)(2,1)S(1)} collective-permute-done((bf16[128,1152]{1,0:T(8,128)(2,1)S(1)}, bf16[128,1152]{1,0:T(8,128)(2,1)S(1)}, u32[]{:S(2)}, u32[]{:S(2)}) %collective-permute-start.51) | collective-permute-done | bytes 294944 | tf_op jit(solution)/shard_map/ppermute | solution.py:57
  52.2 4.5 %collective-permute-done.48 = bf16[128,1024]{1,0:T(8,128)(2,1)S(1)} collective-permute-done((bf16[128,1024]{1,0:T(8,128)(2,1)S(1)}, bf16[128,1024]{1,0:T(8,128)(2,1)S(1)}, u32[]{:S(2)}, u32[]{:S(2)}) %collective-permute-start.48) | collective-permute-done | bytes 262176 | tf_op jit(solution)/shard_map/ppermute | solution.py:57
  59.0 9.8 %experts_own.1 = (bf16[512,2048]{1,0:T(8,128)(2,1)S(1)}, bf16[512,1024]{1,0:T(8,128)(2,1)S(1)}, bf16[256,1152]{1,0:T(8,128)(2,1)S(1)}, bf16[256,1152]{1,0:T(8,128)(2,1)S(1)}) custom-call(s32[1]{0:T(128)} %bitcast.21.refs_0_, bf16[512,1024]{1,0:T(8,128)(2,1)S(1)} %constant_dynamic-update-slice_fusion.5.refs_1_.refs_0_, ...), custom_call_target="tpu_custom_call" | custom-call | flops 5368709120 | bytes 9437184 | tf_op jit(solution)/shard_map/experts_own/pallas_call | solution.py:254
  68.8 2.3 %experts_mixed.1 = (bf16[256,1024]{1,0:T(8,128)(2,1)S(1)}, bf16[256,1024]{1,0:T(8,128)(2,1)S(1)}) custom-call(bf16[512,1024]{1,0:T(8,128)(2,1)S(1)} %get-tuple-element.23.gated_ref.refs_6_, bf16[8,1024,128]{2,1,0:T(8,128)(2,1)S(1)} %copy-done.3), custom_call_target="tpu_custom_call" | custom-call | flops 1073741824 | bytes 4194304 | tf_op jit(solution)/shard_map/experts_mixed/pallas_call | solution.py:289
  71.9 5.5 %experts_far.1 = (bf16[512,2048]{1,0:T(8,128)(2,1)S(1)}, bf16[512,1024]{1,0:T(8,128)(2,1)S(1)}) custom-call(s32[1]{0:T(128)} %bitcast.21.refs_0_, bf16[512,1024]{1,0:T(8,128)(2,1)S(1)} %constant_dynamic-update-slice_fusion.11.refs_1_, bf16[512,1152]{1,0:T(8,128)(2,1)S(1)} %constant_dynamic-update-slice_fusion.14.refs_2_.refs_3_, ...), custom_call_target="tpu_custom_call" | custom-call | flops 3221225472 | bytes 9437184 | tf_op jit(solution)/shard_map/experts_far/pallas_call | solution.py:254
  79.7 6.7 %experts_weight_grads.1 = (f32[8,512,128]{2,1,0:T(8,128)}, f32[8,512,128]{2,1,0:T(8,128)}, f32[8,512,128]{2,1,0:T(8,128)}) custom-call(s32[1]{0:T(128)} %bitcast.87.place_ref, bf16[512,1024]{1,0:T(8,128)(2,1)S(1)} %constant_dynamic-update-slice_fusion.5.refs_1_.refs_0_, bf16[512,1024]{1,0:T(8,128)(2,1)S(1)} %constant_dynamic-update-slice_fusion.11.refs_1_, ...), custom_call_target="tpu_custom_call" | custom-call | flops 3221225472 | bytes 14680064 | tf_op jit(solution)/shard_map/experts_weight_grads/pallas_call | solution.py:344
  86.8 5.3 %collective-permute-done.19 = bf16[128,1152]{1,0:T(8,128)(2,1)S(1)} collective-permute-done((bf16[128,1152]{1,0:T(8,128)(2,1)S(1)}, bf16[128,1152]{1,0:T(8,128)(2,1)S(1)}, u32[]{:S(2)}, u32[]{:S(2)}) %collective-permute-start.19) | collective-permute-done | bytes 294944 | tf_op jit(solution)/shard_map/ppermute | solution.py:57
  92.3 1.6 collective-permute-start.22
  93.8 2.9 %collective-permute-start.20 = (bf16[32,1152]{1,0:T(8,128)(2,1)S(1)}, bf16[32,1152]{1,0:T(8,128)(2,1)S(1)}, u32[]{:S(2)}, u32[]{:S(2)}) collective-permute-start(bf16[32,1152]{1,0:T(8,128)(2,1)S(1)} %get-tuple-element.132), channel_id=1, source_target_pairs={{0,1},{1,0},{2,3},{3,2},{4,5},{5,4},{6,7},{7,6},{8,9},{9,8},{10,11... | collective-permute-start | bytes 221192 | tf_op jit(solution)/shard_map/ppermute | solution.py:57
  96.7 1.6 collective-permute-start.14
  99.1 2.1 %collective-permute-start.12 = (bf16[32,1024]{1,0:T(8,128)(2,1)S(1)}, bf16[32,1024]{1,0:T(8,128)(2,1)S(1)}, u32[]{:S(2)}, u32[]{:S(2)}) collective-permute-start(bf16[32,1024]{1,0:T(8,128)(2,1)S(1)} %get-tuple-element.151), channel_id=1, source_target_pairs={{0,1},{1,0},{2,3},{3,2},{4,5},{5,4},{6,7},{7,6},{8,9},{9,8},{10,11... | collective-permute-start | bytes 196616 | tf_op jit(solution)/shard_map/ppermute | solution.py:57
  101.2 1.9 %collective-permute-done.21 = bf16[32,1152]{1,0:T(8,128)(2,1)S(1)} collective-permute-done((bf16[32,1152]{1,0:T(8,128)(2,1)S(1)}, bf16[32,1152]{1,0:T(8,128)(2,1)S(1)}, u32[]{:S(2)}, u32[]{:S(2)}) %collective-permute-start.21) | collective-permute-done | bytes 73760 | tf_op jit(solution)/shard_map/ppermute | solution.py:57
  103.8 3.4 %collective-permute-start.37 = (f32[1024]{0:T(1024)S(1)}, f32[1024]{0:T(1024)S(1)}, u32[]{:S(2)}, u32[]{:S(2)}) collective-permute-start(f32[1024]{0:T(1024)S(1)} %get-tuple-element.118), channel_id=1, source_target_pairs={{0,3},{1,2},{2,1},{3,0},{4,7},{5,6},{6,5},{7,4},{8,11},{9,10},{10,... | collective-permute-start | bytes 12296 | tf_op jit(solution)/shard_map/ppermute | solution.py:57
  109.0 3.3 %collective-permute-start.25 = (bf16[32,1024]{1,0:T(8,128)(2,1)S(1)}, bf16[32,1024]{1,0:T(8,128)(2,1)S(1)}, u32[]{:S(2)}, u32[]{:S(2)}) collective-permute-start(bf16[32,1024]{1,0:T(8,128)(2,1)S(1)} %get-tuple-element.120), channel_id=1, source_target_pairs={{0,3},{1,2},{2,1},{3,0},{4,7},{5,6},{6,5},{7,4},{8,11},{9,10},{10,... | collective-permute-start | bytes 196616 | tf_op jit(solution)/shard_map/ppermute | solution.py:57
  118.9 3.6 %collective-permute-start.17 = (bf16[32,1024]{1,0:T(8,128)(2,1)}, bf16[32,1024]{1,0:T(8,128)(2,1)}, u32[]{:S(2)}, u32[]{:S(2)}) collective-permute-start(bf16[32,1024]{1,0:T(8,128)(2,1)} %get-tuple-element.171), channel_id=1, source_target_pairs={{0,3},{1,2},{2,1},{3,0},{4,7},{5,6},{6,5},{7,4},{8,11},{9,10},{10,... | collective-permute-start | bytes 196616 | tf_op jit(solution)/shard_map/ppermute | solution.py:57
  130.6 1.9 %collective-permute-start.27 = (bf16[32,1024]{1,0:T(8,128)(2,1)}, bf16[32,1024]{1,0:T(8,128)(2,1)S(1)}, u32[]{:S(2)}, u32[]{:S(2)}) collective-permute-start(bf16[32,1024]{1,0:T(8,128)(2,1)} %get-tuple-element.146), channel_id=1, source_target_pairs={{0,2},{1,3},{2,0},{3,1},{4,6},{5,7},{6,4},{7,5},{8,10},{9,11},{10,... | collective-permute-start | bytes 196616 | tf_op jit(solution)/shard_map/ppermute | solution.py:57
  138.3 3.0 %concatenate.116 = f32[2,2,2,128,546]{4,3,2,1,0:T(8,128)S(1)} concatenate(f32[2,2,2,128,256]{4,3,2,1,0:T(8,128)} %fusion.64, f32[2,2,2,128,128]{4,3,2,1,0:T(8,128)} %fusion.65, f32[2,2,2,128,128]{4,3,2,1,0:T(8,128)} %fusion.66, f32[2,2,2,128,32]{4,3,2,1,0:T(8,128)} %bitcast.229, f32[2,2,2,128,1]{4,3,2,1,0:T(8,128)} %copy.221, f32[2,2,2,128,1]{4,3,2,1,0:T(8,128)} %copy.222), dimensions={4} | concatenate | bytes 4472832 | tf_op jit(solution)/shard_map/concatenate | solution.py:555
  142.5 2.4 %copy.225 = f32[2,2,128,546]{2,0,3,1:T(2,128)} copy(f32[2,2,128,546]{3,2,1,0:T(8,128)} %dynamic-slice_bitcast_fusion) | data formatting | bytes 2236416 | tf_op jit(solution)/shard_map/jit(dynamic_index_in_dim)/squeeze | solution.py:116
  149.2 3.0 %collective-permute-start.31 = (bf16[32,1024]{1,0:T(8,128)(2,1)S(1)}, bf16[32,1024]{1,0:T(8,128)(2,1)S(1)}, u32[]{:S(2)}, u32[]{:S(2)}) collective-permute-start(bf16[32,1024]{1,0:T(8,128)(2,1)S(1)} %add_convert_fusion.4), channel_id=1, source_target_pairs={{0,3},{1,2},{2,1},{3,0},{4,7},{5,6},{6,5},{7,4},{8,11},{9,10},{10,... | collective-permute-start | bytes 196616 | tf_op jit(solution)/shard_map/ppermute | solution.py:57
  156.0 2.7 %collective-permute-done.30 = bf16[32,1024]{1,0:T(8,128)(2,1)S(1)} collective-permute-done((bf16[32,1024]{1,0:T(8,128)(2,1)S(1)}, bf16[32,1024]{1,0:T(8,128)(2,1)S(1)}, u32[]{:S(2)}, u32[]{:S(2)}) %collective-permute-start.30) | collective-permute-done | bytes 65568 | tf_op jit(solution)/shard_map/ppermute | solution.py:57
  161.1 1.9 %reshape.332 = f32[2,2,128,546]{2,1,0,3:T(2,128)S(1)} reshape(bf16[512,546]{0,1:T(8,128)(2,1)} %collective-permute-done.38) | data formatting | bytes 1677312 | tf_op jit(solution)/shard_map/convert_element_type | solution.py:120
  166.5 5.7 %collective-permute-done.39 = bf16[256,546]{0,1:T(8,128)(2,1)S(1)} collective-permute-done((bf16[256,546]{0,1:T(8,128)(2,1)S(1)}, bf16[256,546]{0,1:T(8,128)(2,1)S(1)}, u32[]{:S(2)}, u32[]{:S(2)}) %collective-permute-start.39) | collective-permute-done | bytes 279584 | tf_op jit(solution)/shard_map/ppermute | solution.py:57
  173.7 4.0 %collective-permute-done.40 = bf16[128,546]{0,1:T(8,128)(2,1)S(1)} collective-permute-done((bf16[128,546]{0,1:T(8,128)(2,1)S(1)}, bf16[128,546]{0,1:T(8,128)(2,1)S(1)}, u32[]{:S(2)}, u32[]{:S(2)}) %collective-permute-start.40) | collective-permute-done | bytes 139808 | tf_op jit(solution)/shard_map/ppermute | solution.py:57
  178.3 2.0 %collective-permute-start.43 = (f32[128]{0:T(128)S(1)}, f32[128]{0:T(128)S(1)}, u32[]{:S(2)}, u32[]{:S(2)}) collective-permute-start(f32[128]{0:T(128)S(1)} %get-tuple-element.136), channel_id=1, source_target_pairs={{0,3},{1,2},{2,1},{3,0},{4,7},{5,6},{6,5},{7,4},{8,11},{9,10},{10,... | collective-permute-start | bytes 1544 | tf_op jit(solution)/shard_map/ppermute | solution.py:57
  180.3 2.4 %collective-permute-start.41 = (f32[128]{0:T(128)S(1)}, f32[128]{0:T(128)S(1)}, u32[]{:S(2)}, u32[]{:S(2)}) collective-permute-start(f32[128]{0:T(128)S(1)} %get-tuple-element.136), channel_id=1, source_target_pairs={{0,1},{1,0},{2,3},{3,2},{4,5},{5,4},{6,7},{7,6},{8,9},{9,8},{10,11... | collective-permute-start | bytes 1544 | tf_op jit(solution)/shard_map/ppermute | solution.py:57
  (329 shorter events, 73.7 us)
Async XLA Ops:
  3.8 35.7 %collective-permute-start.8 = (bf16[128,1152]{1,0:T(8,128)(2,1)}, bf16[128,1152]{1,0:T(8,128)(2,1)S(1)}, u32[]{:S(2)}, u32[]{:S(2)}) collective-permute-start(bf16[128,1152]{1,0:T(8,128)(2,1)} %pad_maximum_fusion.4), channel_id=1, source_target_pairs={{0,8},{4,12},{8,0},{12,4},{1,9},{5,13},{9,1},{13,5},{2,10},{6,14},... | collective-permute-start | bytes 884744 | tf_op jit(solution)/shard_map/ppermute | solution.py:57
  6.7 32.9 %collective-permute-start.50 = (bf16[128,1152]{1,0:T(8,128)(2,1)}, bf16[128,1152]{1,0:T(8,128)(2,1)S(1)}, u32[]{:S(2)}, u32[]{:S(2)}) collective-permute-start(bf16[128,1152]{1,0:T(8,128)(2,1)} %pad_maximum_fusion.4), channel_id=1, source_target_pairs={{0,16},{16,0},{1,17},{17,1},{2,18},{18,2},{3,19},{19,3},{4,20},{20... | collective-permute-start | bytes 884744 | tf_op jit(solution)/shard_map/ppermute | solution.py:57
  38.3 8.5 %collective-permute-start.6 = (bf16[128,1024]{1,0:T(8,128)(2,1)S(1)}, bf16[128,1024]{1,0:T(8,128)(2,1)S(1)}, u32[]{:S(2)}, u32[]{:S(2)}) collective-permute-start(bf16[128,1024]{1,0:T(8,128)(2,1)S(1)} %pad_maximum_fusion.5), channel_id=1, source_target_pairs={{0,8},{4,12},{8,0},{12,4},{1,9},{5,13},{9,1},{13,5},{2,10},{6,14},... | collective-permute-start | bytes 786440 | tf_op jit(solution)/shard_map/ppermute | solution.py:57
  38.9 8.0 %collective-permute-start.47 = (bf16[128,1024]{1,0:T(8,128)(2,1)S(1)}, bf16[128,1024]{1,0:T(8,128)(2,1)S(1)}, u32[]{:S(2)}, u32[]{:S(2)}) collective-permute-start(bf16[128,1024]{1,0:T(8,128)(2,1)S(1)} %pad_maximum_fusion.5), channel_id=1, source_target_pairs={{0,16},{16,0},{1,17},{17,1},{2,18},{18,2},{3,19},{19,3},{4,20},{20... | collective-permute-start | bytes 786440 | tf_op jit(solution)/shard_map/ppermute | solution.py:57
  39.6 17.3 %collective-permute-start.9 = (bf16[256,1152]{1,0:T(8,128)(2,1)S(1)}, bf16[256,1152]{1,0:T(8,128)(2,1)S(1)}, u32[]{:S(2)}, u32[]{:S(2)}) collective-permute-start(bf16[256,1152]{1,0:T(8,128)(2,1)S(1)} %pad_maximum_fusion.1), channel_id=1, source_target_pairs={{0,4},{4,0},{8,12},{12,8},{1,5},{5,1},{9,13},{13,9},{2,6},{6,2},{1... | collective-permute-start | bytes 1769480 | tf_op jit(solution)/shard_map/ppermute | solution.py:57
  39.7 12.4 %collective-permute-start.51 = (bf16[128,1152]{1,0:T(8,128)(2,1)S(1)}, bf16[128,1152]{1,0:T(8,128)(2,1)S(1)}, u32[]{:S(2)}, u32[]{:S(2)}) collective-permute-start(bf16[128,1152]{1,0:T(8,128)(2,1)S(1)} %collective-permute-done.50), channel_id=1, source_target_pairs={{0,8},{4,12},{8,0},{12,4},{1,9},{5,13},{9,1},{13,5},{2,10},{6,14},... | collective-permute-start | bytes 884744 | tf_op jit(solution)/shard_map/ppermute | solution.py:57
  46.9 10.1 %collective-permute-start.7 = (bf16[256,1024]{1,0:T(8,128)(2,1)S(1)}, bf16[256,1024]{1,0:T(8,128)(2,1)S(1)}, u32[]{:S(2)}, u32[]{:S(2)}) collective-permute-start(bf16[256,1024]{1,0:T(8,128)(2,1)S(1)} %get-tuple-element.158), channel_id=1, source_target_pairs={{0,4},{4,0},{8,12},{12,8},{1,5},{5,1},{9,13},{13,9},{2,6},{6,2},{1... | collective-permute-start | bytes 1572872 | tf_op jit(solution)/shard_map/ppermute | solution.py:57
  46.9 9.8 %collective-permute-start.48 = (bf16[128,1024]{1,0:T(8,128)(2,1)S(1)}, bf16[128,1024]{1,0:T(8,128)(2,1)S(1)}, u32[]{:S(2)}, u32[]{:S(2)}) collective-permute-start(bf16[128,1024]{1,0:T(8,128)(2,1)S(1)} %collective-permute-done.47), channel_id=1, source_target_pairs={{0,8},{4,12},{8,0},{12,4},{1,9},{5,13},{9,1},{13,5},{2,10},{6,14},... | collective-permute-start | bytes 786440 | tf_op jit(solution)/shard_map/ppermute | solution.py:57
  52.1 19.7 %collective-permute-start.52 = (bf16[256,1152]{1,0:T(8,128)(2,1)S(1)}, bf16[256,1152]{1,0:T(8,128)(2,1)S(1)}, u32[]{:S(2)}, u32[]{:S(2)}) collective-permute-start(bf16[256,1152]{1,0:T(8,128)(2,1)S(1)} %pad_maximum_fusion.2), channel_id=1, source_target_pairs={{0,4},{4,0},{8,12},{12,8},{1,5},{5,1},{9,13},{13,9},{2,6},{6,2},{1... | collective-permute-start | bytes 1769480 | tf_op jit(solution)/shard_map/ppermute | solution.py:57
  56.7 15.0 %collective-permute-start.49 = (bf16[256,1024]{1,0:T(8,128)(2,1)S(1)}, bf16[256,1024]{1,0:T(8,128)(2,1)S(1)}, u32[]{:S(2)}, u32[]{:S(2)}) collective-permute-start(bf16[256,1024]{1,0:T(8,128)(2,1)S(1)} %pad_maximum_fusion.3), channel_id=1, source_target_pairs={{0,4},{4,0},{8,12},{12,8},{1,5},{5,1},{9,13},{13,9},{2,6},{6,2},{1... | collective-permute-start | bytes 1572872 | tf_op jit(solution)/shard_map/ppermute | solution.py:57
  68.7 9.3 %collective-permute-start.18 = (bf16[256,1152]{1,0:T(8,128)(2,1)S(1)}, bf16[256,1152]{1,0:T(8,128)(2,1)S(1)}, u32[]{:S(2)}, u32[]{:S(2)}) collective-permute-start(bf16[256,1152]{1,0:T(8,128)(2,1)S(1)} %get-tuple-element.27), channel_id=1, source_target_pairs={{0,4},{4,0},{8,12},{12,8},{1,5},{5,1},{9,13},{13,9},{2,6},{6,2},{1... | collective-permute-start | bytes 1769480 | tf_op jit(solution)/shard_map/ppermute | solution.py:57
  77.5 9.2 %collective-permute-start.11 = (bf16[128,1024]{1,0:T(8,128)(2,1)S(1)}, bf16[128,1024]{1,0:T(8,128)(2,1)S(1)}, u32[]{:S(2)}, u32[]{:S(2)}) collective-permute-start(bf16[128,1024]{1,0:T(8,128)(2,1)S(1)} %add_convert_fusion.2), channel_id=1, source_target_pairs={{0,8},{4,12},{8,0},{12,4},{1,9},{5,13},{9,1},{13,5},{2,10},{6,14},... | collective-permute-start | bytes 786440 | tf_op jit(solution)/shard_map/ppermute | solution.py:57
  78.1 13.9 %collective-permute-start.19 = (bf16[128,1152]{1,0:T(8,128)(2,1)S(1)}, bf16[128,1152]{1,0:T(8,128)(2,1)S(1)}, u32[]{:S(2)}, u32[]{:S(2)}) collective-permute-start(bf16[128,1152]{1,0:T(8,128)(2,1)S(1)} %add_convert_fusion), channel_id=1, source_target_pairs={{0,8},{4,12},{8,0},{12,4},{1,9},{5,13},{9,1},{13,5},{2,10},{6,14},... | collective-permute-start | bytes 884744 | tf_op jit(solution)/shard_map/ppermute | solution.py:57
  93.8 9.2 %collective-permute-start.21 = (bf16[32,1152]{1,0:T(8,128)(2,1)S(1)}, bf16[32,1152]{1,0:T(8,128)(2,1)S(1)}, u32[]{:S(2)}, u32[]{:S(2)}) collective-permute-start(bf16[32,1152]{1,0:T(8,128)(2,1)S(1)} %get-tuple-element.134), channel_id=1, source_target_pairs={{0,2},{1,3},{2,0},{3,1},{4,6},{5,7},{6,4},{7,5},{8,10},{9,11},{10,... | collective-permute-start | bytes 221192 | tf_op jit(solution)/shard_map/ppermute | solution.py:57
  93.8 9.2 %collective-permute-start.20 = (bf16[32,1152]{1,0:T(8,128)(2,1)S(1)}, bf16[32,1152]{1,0:T(8,128)(2,1)S(1)}, u32[]{:S(2)}, u32[]{:S(2)}) collective-permute-start(bf16[32,1152]{1,0:T(8,128)(2,1)S(1)} %get-tuple-element.132), channel_id=1, source_target_pairs={{0,1},{1,0},{2,3},{3,2},{4,5},{5,4},{6,7},{7,6},{8,9},{9,8},{10,11... | collective-permute-start | bytes 221192 | tf_op jit(solution)/shard_map/ppermute | solution.py:57
  96.7 10.5 %collective-permute-start.14 = (bf16[32,1024]{1,0:T(8,128)(2,1)S(1)}, bf16[32,1024]{1,0:T(8,128)(2,1)S(1)}, u32[]{:S(2)}, u32[]{:S(2)}) collective-permute-start(bf16[32,1024]{1,0:T(8,128)(2,1)S(1)} %get-tuple-element.152), channel_id=1, source_target_pairs={{0,3},{1,2},{2,1},{3,0},{4,7},{5,6},{6,5},{7,4},{8,11},{9,10},{10,... | collective-permute-start | bytes 196616 | tf_op jit(solution)/shard_map/ppermute | solution.py:57
  98.3 9.9 %collective-permute-start.13 = (bf16[32,1024]{1,0:T(8,128)(2,1)S(1)}, bf16[32,1024]{1,0:T(8,128)(2,1)S(1)}, u32[]{:S(2)}, u32[]{:S(2)}) collective-permute-start(bf16[32,1024]{1,0:T(8,128)(2,1)S(1)} %get-tuple-element.153), channel_id=1, source_target_pairs={{0,2},{1,3},{2,0},{3,1},{4,6},{5,7},{6,4},{7,5},{8,10},{9,11},{10,... | collective-permute-start | bytes 196616 | tf_op jit(solution)/shard_map/ppermute | solution.py:57
  99.1 9.1 %collective-permute-start.12 = (bf16[32,1024]{1,0:T(8,128)(2,1)S(1)}, bf16[32,1024]{1,0:T(8,128)(2,1)S(1)}, u32[]{:S(2)}, u32[]{:S(2)}) collective-permute-start(bf16[32,1024]{1,0:T(8,128)(2,1)S(1)} %get-tuple-element.151), channel_id=1, source_target_pairs={{0,1},{1,0},{2,3},{3,2},{4,5},{5,4},{6,7},{7,6},{8,9},{9,8},{10,11... | collective-permute-start | bytes 196616 | tf_op jit(solution)/shard_map/ppermute | solution.py:57
  103.8 8.6 %collective-permute-start.37 = (f32[1024]{0:T(1024)S(1)}, f32[1024]{0:T(1024)S(1)}, u32[]{:S(2)}, u32[]{:S(2)}) collective-permute-start(f32[1024]{0:T(1024)S(1)} %get-tuple-element.118), channel_id=1, source_target_pairs={{0,3},{1,2},{2,1},{3,0},{4,7},{5,6},{6,5},{7,4},{8,11},{9,10},{10,... | collective-permute-start | bytes 12296 | tf_op jit(solution)/shard_map/ppermute | solution.py:57
  107.2 8.2 %collective-permute-start.35 = (f32[1024]{0:T(1024)S(1)}, f32[1024]{0:T(1024)S(1)}, u32[]{:S(2)}, u32[]{:S(2)}) collective-permute-start(f32[1024]{0:T(1024)S(1)} %get-tuple-element.118), channel_id=1, source_target_pairs={{0,1},{1,0},{2,3},{3,2},{4,5},{5,4},{6,7},{7,6},{8,9},{9,8},{10,11... | collective-permute-start | bytes 12296 | tf_op jit(solution)/shard_map/ppermute | solution.py:57
  109.0 15.0 %collective-permute-start.25 = (bf16[32,1024]{1,0:T(8,128)(2,1)S(1)}, bf16[32,1024]{1,0:T(8,128)(2,1)S(1)}, u32[]{:S(2)}, u32[]{:S(2)}) collective-permute-start(bf16[32,1024]{1,0:T(8,128)(2,1)S(1)} %get-tuple-element.120), channel_id=1, source_target_pairs={{0,3},{1,2},{2,1},{3,0},{4,7},{5,6},{6,5},{7,4},{8,11},{9,10},{10,... | collective-permute-start | bytes 196616 | tf_op jit(solution)/shard_map/ppermute | solution.py:57
  112.3 11.7 %collective-permute-start.24 = (bf16[32,1024]{1,0:T(8,128)(2,1)S(1)}, bf16[32,1024]{1,0:T(8,128)(2,1)S(1)}, u32[]{:S(2)}, u32[]{:S(2)}) collective-permute-start(bf16[32,1024]{1,0:T(8,128)(2,1)S(1)} %get-tuple-element.120), channel_id=1, source_target_pairs={{0,2},{1,3},{2,0},{3,1},{4,6},{5,7},{6,4},{7,5},{8,10},{9,11},{10,... | collective-permute-start | bytes 196616 | tf_op jit(solution)/shard_map/ppermute | solution.py:57
  118.9 30.3 %collective-permute-start.17 = (bf16[32,1024]{1,0:T(8,128)(2,1)}, bf16[32,1024]{1,0:T(8,128)(2,1)}, u32[]{:S(2)}, u32[]{:S(2)}) collective-permute-start(bf16[32,1024]{1,0:T(8,128)(2,1)} %get-tuple-element.171), channel_id=1, source_target_pairs={{0,3},{1,2},{2,1},{3,0},{4,7},{5,6},{6,5},{7,4},{8,11},{9,10},{10,... | collective-permute-start | bytes 196616 | tf_op jit(solution)/shard_map/ppermute | solution.py:57
  122.6 29.6 %collective-permute-start.16 = (bf16[32,1024]{1,0:T(8,128)(2,1)}, bf16[32,1024]{1,0:T(8,128)(2,1)}, u32[]{:S(2)}, u32[]{:S(2)}) collective-permute-start(bf16[32,1024]{1,0:T(8,128)(2,1)} %get-tuple-element.171), channel_id=1, source_target_pairs={{0,2},{1,3},{2,0},{3,1},{4,6},{5,7},{6,4},{7,5},{8,10},{9,11},{10,... | collective-permute-start | bytes 196616 | tf_op jit(solution)/shard_map/ppermute | solution.py:57
  129.6 18.2 %collective-permute-start.28 = (bf16[32,1024]{1,0:T(8,128)(2,1)}, bf16[32,1024]{1,0:T(8,128)(2,1)S(1)}, u32[]{:S(2)}, u32[]{:S(2)}) collective-permute-start(bf16[32,1024]{1,0:T(8,128)(2,1)} %get-tuple-element.145), channel_id=1, source_target_pairs={{0,3},{1,2},{2,1},{3,0},{4,7},{5,6},{6,5},{7,4},{8,11},{9,10},{10,... | collective-permute-start | bytes 196616 | tf_op jit(solution)/shard_map/ppermute | solution.py:57
  130.6 17.9 %collective-permute-start.27 = (bf16[32,1024]{1,0:T(8,128)(2,1)}, bf16[32,1024]{1,0:T(8,128)(2,1)S(1)}, u32[]{:S(2)}, u32[]{:S(2)}) collective-permute-start(bf16[32,1024]{1,0:T(8,128)(2,1)} %get-tuple-element.146), channel_id=1, source_target_pairs={{0,2},{1,3},{2,0},{3,1},{4,6},{5,7},{6,4},{7,5},{8,10},{9,11},{10,... | collective-permute-start | bytes 196616 | tf_op jit(solution)/shard_map/ppermute | solution.py:57
  132.5 15.9 %collective-permute-start.26 = (bf16[32,1024]{1,0:T(8,128)(2,1)S(1)}, bf16[32,1024]{1,0:T(8,128)(2,1)S(1)}, u32[]{:S(2)}, u32[]{:S(2)}) collective-permute-start(bf16[32,1024]{1,0:T(8,128)(2,1)S(1)} %get-tuple-element.144), channel_id=1, source_target_pairs={{0,1},{1,0},{2,3},{3,2},{4,5},{5,4},{6,7},{7,6},{8,9},{9,8},{10,11... | collective-permute-start | bytes 196616 | tf_op jit(solution)/shard_map/ppermute | solution.py:57
  148.4 12.6 %collective-permute-start.38 = (bf16[512,546]{0,1:T(8,128)(2,1)S(1)}, bf16[512,546]{0,1:T(8,128)(2,1)}, u32[]{:S(2)}, u32[]{:S(2)}) collective-permute-start(bf16[512,546]{0,1:T(8,128)(2,1)S(1)} %copy.224), channel_id=1, source_target_pairs={{0,4},{4,0},{8,12},{12,8},{1,5},{5,1},{9,13},{13,9},{2,6},{6,2},{1... | collective-permute-start | bytes 1677320 | tf_op jit(solution)/shard_map/ppermute | solution.py:57
  148.4 11.9 %collective-permute-start.44 = (bf16[512,256]{1,0:T(8,128)(2,1)S(1)}, bf16[512,256]{1,0:T(8,128)(2,1)S(1)}, u32[]{:S(2)}, u32[]{:S(2)}) collective-permute-start(bf16[512,256]{1,0:T(8,128)(2,1)S(1)} %bitcast.236), channel_id=1, source_target_pairs={{0,4},{4,0},{8,12},{12,8},{1,5},{5,1},{9,13},{13,9},{2,6},{6,2},{1... | collective-permute-start | bytes 786440 | tf_op jit(solution)/shard_map/ppermute | solution.py:57
  164.3 7.9 %collective-permute-start.39 = (bf16[256,546]{0,1:T(8,128)(2,1)S(1)}, bf16[256,546]{0,1:T(8,128)(2,1)S(1)}, u32[]{:S(2)}, u32[]{:S(2)}) collective-permute-start(bf16[256,546]{0,1:T(8,128)(2,1)S(1)} %bitcast.234), channel_id=1, source_target_pairs={{0,8},{4,12},{8,0},{12,4},{1,9},{5,13},{9,1},{13,5},{2,10},{6,14},... | collective-permute-start | bytes 838664 | tf_op jit(solution)/shard_map/ppermute | solution.py:57
  165.8 7.2 %collective-permute-start.46 = (bf16[128,256]{1,0:T(8,128)(2,1)S(1)}, bf16[128,256]{1,0:T(8,128)(2,1)S(1)}, u32[]{:S(2)}, u32[]{:S(2)}) collective-permute-start(bf16[128,256]{1,0:T(8,128)(2,1)S(1)} %fusion.22), channel_id=1, source_target_pairs={{0,16},{16,0},{1,17},{17,1},{2,18},{18,2},{3,19},{19,3},{4,20},{20... | collective-permute-start | bytes 196616 | tf_op jit(solution)/shard_map/ppermute | solution.py:57
  178.3 7.2 %collective-permute-start.43 = (f32[128]{0:T(128)S(1)}, f32[128]{0:T(128)S(1)}, u32[]{:S(2)}, u32[]{:S(2)}) collective-permute-start(f32[128]{0:T(128)S(1)} %get-tuple-element.136), channel_id=1, source_target_pairs={{0,3},{1,2},{2,1},{3,0},{4,7},{5,6},{6,5},{7,4},{8,11},{9,10},{10,... | collective-permute-start | bytes 1544 | tf_op jit(solution)/shard_map/ppermute | solution.py:57
  (78 other events, 416.7 us)

commit v3 on v2

v3 whole, which is shorter than its diff:
```python
import functools
import math

import jax
import jax.numpy as jnp
import numpy as np
from jax import lax
from jax.experimental import pallas as pl
from jax.experimental.pallas import tpu as pltpu
from jax.sharding import PartitionSpec as P

HD = 64
EPSILON = 1e-06
F32 = jnp.float32
BF16 = jnp.bfloat16
EXTRA = 128


def dot(left, right, dims):
    return lax.dot_general(left, right, (dims, ((), ())), preferred_element_type=F32)


def rope_tables(rows):
    inverse = np.exp(np.arange(HD // 2).astype(np.float32) * np.float32(-2.0 * math.log(1e4) / HD))
    angles = np.arange(rows, dtype=np.float32)[:, None] * inverse.astype(np.float32)[None, :]
    cosine, sine = np.cos(angles), np.sin(angles)
    return (
        jnp.asarray(np.concatenate([cosine] * 4, 1), F32),
        jnp.asarray(np.concatenate([-sine, sine] * 2, 1), F32),
    )


def other_halves(values):
    width = values.shape[1]
    lane = lax.broadcasted_iota(jnp.int32, values.shape, 1)
    return jnp.where(
        lane % HD < HD // 2,
        pltpu.roll(values, width - HD // 2, 1),
        pltpu.roll(values, HD // 2, 1),
    )


def widened(table, width):
    copies = width // table.shape[1]
    return table if copies == 1 else jnp.concatenate([table] * copies, 1)


def rotate(values, cosine, sine):
    width = values.shape[1]
    return values * widened(cosine, width) + other_halves(values) * widened(sine, width)


def rotate_back(values, cosine, sine):
    width = values.shape[1]
    return values * widened(cosine, width) - other_halves(values) * widened(sine, width)


def swap(x, axis, k):
    n = lax.axis_size(axis)
    return lax.ppermute(x, axis, [(i, i ^ k) for i in range(n)])


def swap_plane(x, k_dp, k_expert):
    n = lax.axis_size("expert")
    total = n * lax.axis_size("dp")
    return lax.ppermute(x, ("dp", "expert"), [(i, i ^ (k_dp * n + k_expert)) for i in range(total)])


def bits_of(n):
    k, out = n // 2, []
    while k >= 1:
        out.append(k)
        k //= 2
    return out


def gather_sets(x, near=None):
    bits = bits_of(lax.axis_size("expert"))
    sets = []
    for k_dp in range(lax.axis_size("dp")):
        if len(bits) == 2 and k_dp:
            parts = [swap(x, "dp", k_dp), swap_plane(x, k_dp, bits[0])]
            sets.append(parts + [swap(p, "expert", bits[1]) for p in parts])
            continue
        rows = swap(x, "dp", k_dp) if k_dp else x if near is None else near
        for k in bits[:-2]:
            rows = jnp.concatenate([rows, swap(rows, "expert", k)], 0)
        parts = [rows]
        for k in bits[-2:]:
            parts = parts + [swap(p, "expert", k) for p in parts]
        sets.append(parts)
    return sets


def swap_tensor(blocks):
    n = lax.axis_size("tensor")
    return [swap(blocks[k - 1], "tensor", k) for k in range(1, n)]


def gather_tensor(x):
    return [x] + swap_tensor([x] * (lax.axis_size("tensor") - 1))


def rows_at(index, rows):
    return pl.ds(pl.multiple_of(index * rows, rows), rows)


def plain_call(kernel, name, out_shape, scratch, flops, *arrays, after=(), vmem=16):
    def whole(a):
        if a.dtype == jnp.int32 and a.size <= 64:
            return pl.BlockSpec(memory_space=pltpu.SMEM)
        return pl.BlockSpec(a.shape, lambda i: (0,) * a.ndim)

    size = sum(a.size * a.dtype.itemsize for a in list(arrays) + list(out_shape))
    count, extra = len(arrays), len(after)

    def body(*refs):
        kernel(*refs[:count], *refs[count + extra :])

    arrays = list(arrays) + list(after)
    return pl.pallas_call(
        body,
        grid=(1,),
        in_specs=[whole(a) for a in arrays[:count]] + [pl.BlockSpec(memory_space=pl.ANY)] * extra,
        out_specs=[whole(a) for a in out_shape],
        out_shape=out_shape,
        scratch_shapes=scratch,
        compiler_params=pltpu.CompilerParams(vmem_limit_bytes=vmem * 2**20),
        cost_estimate=pl.CostEstimate(flops=flops, bytes_accessed=size, transcendentals=0),
        name=name,
    )(*arrays)


def array(shape, dtype):
    return jax.ShapeDtypeStruct(shape, dtype)


def spread_blocks(me, value_ref, own_ref, sent_refs):
    rows = own_ref.shape[0]
    own_ref[...] = value_ref[rows_at(me, rows), :]
    for k, ref in enumerate(sent_refs, 1):
        ref[...] = value_ref[rows_at(me ^ k, rows), :].astype(ref.dtype)


def block_shapes(block, width, n):
    return [array((block, width), F32)] + [array((block, width), BF16)] * (n - 1)


def unit_rows(values):
    return lax.rsqrt(jnp.mean(values * values, -1, keepdims=True) + EPSILON)


def attend_kernel(heads, group, *refs):
    (meta, lengths, hidden, gain, query_w, key_w, value_w, output_w, cosine, sine) = refs[:10]
    n1_ref, qkv_ref, prob_ref, att_ref, cos_ref, sin_ref = refs[10:16]
    own_ref, *sent_refs = refs[16:-1]
    part_scr = refs[-1]
    x = hidden[...].astype(F32)
    n1 = (x * unit_rows(x) * gain[0:1, :]).astype(BF16)
    n1_ref[...] = n1
    tokens = x.shape[0]
    rows = lax.broadcasted_iota(jnp.int32, (tokens, tokens), 0)
    columns = lax.broadcasted_iota(jnp.int32, (tokens, tokens), 1)
    table_rows = lax.broadcasted_iota(jnp.int32, cosine.shape, 0)
    cos, sin = cosine[...], sine[...]
    row_segment, column_segment = jnp.zeros_like(rows), jnp.zeros_like(rows)
    end = 0
    for i in range(lengths.shape[1] - 1):
        end = end + lengths[0, i]
        row_segment += (rows >= end).astype(jnp.int32)
        column_segment += (columns >= end).astype(jnp.int32)
        cos = jnp.where(table_rows >= end, pltpu.roll(cosine[...], end, 0), cos)
        sin = jnp.where(table_rows >= end, pltpu.roll(sine[...], end, 0), sin)
    cos_ref[...] = cos
    sin_ref[...] = sin
    allowed = (row_segment == column_segment) & (columns <= rows)
    q_width, kv_width = query_w.shape[1], key_w.shape[1]
    keys_at, values_at = q_width, q_width + kv_width
    qkv_ref[:, :q_width] = rotate(dot(n1, query_w[...], ((1,), (0,))), cos, sin).astype(BF16)
    qkv_ref[:, keys_at:values_at] = rotate(dot(n1, key_w[...], ((1,), (0,))), cos, sin).astype(BF16)
    qkv_ref[:, values_at:] = dot(n1, value_w[...], ((1,), (0,))).astype(BF16)
    for h in range(heads):
        g = h // group
        scores = dot(
            qkv_ref[:, h * HD : (h + 1) * HD],
            qkv_ref[:, keys_at + g * HD : keys_at + (g + 1) * HD],
            ((1,), (1,)),
        )
        masked = jnp.where(allowed, scores * HD ** (-0.5), -1e30)
        exponent = jnp.exp(masked - jnp.max(masked, -1, keepdims=True))
        prob = exponent / jnp.sum(exponent, -1, keepdims=True)
        prob_ref[h] = prob
        head_out = dot(
            prob.astype(BF16), qkv_ref[:, values_at + g * HD : values_at + (g + 1) * HD], ((1,), (0,))
        )
        att_ref[:, h * HD : (h + 1) * HD] = head_out.astype(BF16)
    part_scr[...] = dot(att_ref[...], output_w[...], ((1,), (1,)))
    spread_blocks(meta[0], part_scr, own_ref, sent_refs)
    own_ref[...] += hidden[rows_at(meta[0], own_ref.shape[0]), :].astype(F32)


def routes_kernel(routes, dy, out_ref):
    width = dy.shape[1]
    out_ref[:, :width] = dy[...]
    named = routes[...].astype(F32).T
    lane = lax.broadcasted_iota(jnp.int32, (dy.shape[0], EXTRA), 1).astype(F32)
    total = jnp.zeros(lane.shape, F32)
    for j in range(named.shape[1]):
        total += (named[:, j : j + 1] == lane).astype(F32)
    out_ref[:, width:] = total.astype(BF16)


def second_norm_kernel(gain, grad, *refs):
    parts, (residual_ref, n2_ref, grad_ref) = refs[:-3], refs[-3:]
    residual = parts[0][...]
    for part in parts[1:]:
        residual = residual + part[...].astype(F32)
    residual_ref[...] = residual
    n2_ref[...] = (residual * unit_rows(residual) * gain[1:2, :]).astype(BF16)
    grad_ref[...] = grad[...]


def place_kernel(meta, *refs):
    blocks, out_ref = refs[:-1], refs[-1]
    rows = blocks[0].shape[0]
    for k, ref in enumerate(blocks):
        out_ref[rows_at(meta[0] ^ k, rows), :] = ref[...].astype(out_ref.dtype)


def halves_kernel(meta, near, got, last, *refs):
    own_ref, *sent_refs = refs[:-1]
    total_scr = refs[-1]
    rows = last.shape[0]
    total_scr[...] = (
        near[:rows, :].astype(F32) + got[:rows, :].astype(F32) + last[...].astype(F32)
    )
    spread_blocks(meta[0], total_scr, own_ref, sent_refs)


def residual_grad_kernel(experts, tensor_n, meta, residual_ref, n2_ref, dy_ref, router, gain, *refs):
    mixed_near, mixed_got, mixed_last = refs[:3]
    parts, refs = refs[3 : 3 + tensor_n], refs[3 + tensor_n :]
    dh_ref, gain_row_ref, message_ref, mixed_ref, *sent_refs = refs[:-1]
    mixed_scr = refs[-1]
    tokens = dy_ref.shape[0]
    mixed_scr[...] = (
        mixed_near[:tokens, :].astype(F32)
        + mixed_got[:tokens, :].astype(F32)
        + mixed_last[...].astype(F32)
    )
    block, width = residual_ref.shape
    mine = rows_at(meta[0], block)
    arrival = parts[0][...]
    for part in parts[1:]:
        arrival = arrival + part[...].astype(F32)
    logits = dot(n2_ref[...], router[...], ((1,), (1,)))
    routed = dy_ref[mine, width : width + experts].astype(F32) > 0.5
    logits = jnp.where(routed, logits, -1e30)
    gates = jnp.exp(logits - jnp.max(logits, -1, keepdims=True))
    gates = gates / jnp.sum(gates, -1, keepdims=True)
    extra = arrival[:, width:]
    dg = extra[:, :experts] + pltpu.roll(extra, EXTRA - experts, 1)[:, :experts]
    dlog = gates * (dg - jnp.sum(gates * dg, -1, keepdims=True))
    high = dlog.astype(BF16)
    low = (dlog - high.astype(F32)).astype(BF16)
    dn2 = (
        arrival[:, :width]
        + dot(high, router[...], ((1,), (0,)))
        + dot(low, router[...], ((1,), (0,)))
    )
    residual = residual_ref[...]
    scale = unit_rows(residual)
    hat = residual * scale
    gain_row_ref[...] = jnp.zeros_like(gain_row_ref)
    gain_row_ref[0:1, :] = jnp.sum(dn2 * hat, 0, keepdims=True)
    gained = dn2 * gain[1:2, :]
    dh = dy_ref[mine, :width].astype(F32) + scale * (
        gained - hat * jnp.mean(gained * hat, -1, keepdims=True)
    )
    dh_ref[...] = dh
    message_ref[:, :width] = dh.astype(BF16)
    message_ref[:, width:] = jnp.zeros((block, EXTRA), BF16)
    message_ref[:, width : width + experts] = high
    message_ref[:, width + experts : width + 2 * experts] = low
    mixed_ref[...] = mixed_scr[mine, :]
    for k, ref in enumerate(sent_refs, 1):
        ref[:, : width + EXTRA] = message_ref[...]
        ref[:, width + EXTRA :] = mixed_scr[rows_at(meta[0] ^ k, block), :].astype(BF16)


def attend_grad_kernel(heads, group, experts, expert_n, dp_n, tensor_n, *refs):
    (meta, hidden, gain_row, n1_ref, n2_ref, qkv_ref, prob_ref, att_ref, cos_ref, sin_ref) = refs[:10]
    query_w, key_w, value_w, output_w = refs[10:14]
    messages = refs[14 : 14 + tensor_n]
    mixed_own, residual_ref = refs[14 + tensor_n : 16 + tensor_n]
    near_ref, far_ref, layer_ref, own_ref, *sent_refs = refs[16 + tensor_n : -6]
    dh_scr, dqkv_scr, raw_scr, dn1_scr, left_scr, side_scr = refs[-6:]
    block = messages[0].shape[0]
    width = hidden.shape[1]
    for k, ref in enumerate(messages):
        dh_scr[rows_at(meta[0] ^ k, block), :] = ref[:, : width + EXTRA]
    cos, sin = cos_ref[...], sin_ref[...]
    q_width, kv_width = query_w.shape[1], key_w.shape[1]
    keys_at, values_at = q_width, q_width + kv_width
    dob = dh_scr[:, :width]
    da = dot(dob, output_w[...], ((1,), (0,))).astype(BF16)
    scale = HD ** (-0.5)
    for g in range(heads // group):
        key = qkv_ref[:, keys_at + g * HD : keys_at + (g + 1) * HD]
        value = qkv_ref[:, values_at + g * HD : values_at + (g + 1) * HD]
        dk = dv = 0.0
        for h in range(g * group, (g + 1) * group):
            da_h = da[:, h * HD : (h + 1) * HD]
            prob = prob_ref[h]
            dprob = dot(da_h, value, ((1,), (1,)))
            ds = prob * (dprob - jnp.sum(prob * dprob, -1, keepdims=True))
            raw_scr[:, h * HD : (h + 1) * HD] = dot(ds.astype(BF16), key, ((1,), (0,))) * scale
            dk = dk + dot(ds.T.astype(BF16), qkv_ref[:, h * HD : (h + 1) * HD], ((1,), (0,)))
            dv = dv + dot(prob.T.astype(BF16), da_h, ((1,), (0,)))
        raw_scr[:, keys_at + g * HD : keys_at + (g + 1) * HD] = dk * scale
        dqkv_scr[:, values_at + g * HD : values_at + (g + 1) * HD] = dv.astype(BF16)
    dqkv_scr[:, :q_width] = rotate_back(raw_scr[:, :q_width], cos, sin).astype(BF16)
    dqkv_scr[:, keys_at:values_at] = rotate_back(raw_scr[:, keys_at:values_at], cos, sin).astype(BF16)
    dn1 = (
        dot(dqkv_scr[:, :q_width], query_w[...], ((1,), (1,)))
        + dot(dqkv_scr[:, keys_at:values_at], key_w[...], ((1,), (1,)))
        + dot(dqkv_scr[:, values_at:], value_w[...], ((1,), (1,)))
    )
    dn1_scr[...] = dn1
    layer = residual_ref[...] + mixed_own[...]
    for ref in messages[1:]:
        layer = layer + ref[:, width + EXTRA :].astype(F32)
    layer_ref[...] = layer.astype(BF16)
    own_ref[...] = dn1_scr[rows_at(meta[0], block), :]
    for k, ref in enumerate(sent_refs, 1):
        ref[:, :width] = dn1_scr[rows_at(meta[0] ^ k, block), :].astype(BF16)
        ref[:, width:] = layer.astype(BF16)
    x = hidden[...].astype(F32)
    first_row = jnp.sum(dn1 * (x * unit_rows(x)), 0, keepdims=True)
    dlog_t = dh_scr[:, width:].astype(F32).T.astype(BF16)
    router_t = dot(dlog_t, n2_ref[...], ((1,), (0,)))
    router_t = router_t[:experts] + router_t[experts : 2 * experts]
    side = jnp.concatenate(
        [router_t, gain_row[0:1, :], first_row, jnp.zeros((EXTRA - experts - 2, width), F32)], 0
    )
    side_scr[...] = side.T.astype(BF16)
    left_scr[:width, :] = n1_ref[...].T
    left_scr[width:, :] = dob.T
    places = expert_n * dp_n
    rows = width // places
    expert_bits = list(reversed(bits_of(expert_n)))
    qkv_width = values_at + kv_width
    for at in range(places):
        bits = [(at // (places >> (i + 1))) % 2 for i in range(len(expert_bits))]
        e_rel = sum(b * k for b, k in zip(bits, expert_bits))
        index = (meta[2] ^ (at % dp_n)) * expert_n + (meta[1] ^ e_rel)
        out = near_ref if at < places // 2 else far_ref
        to = slice((at % (places // 2)) * rows, (at % (places // 2) + 1) * rows)
        source = rows_at(index, rows)
        out[to, :qkv_width] = dot(left_scr[source, :], dqkv_scr[...], ((1,), (0,))).astype(BF16)
        out[to, qkv_width : qkv_width + EXTRA] = side_scr[source, :]
        below = left_scr[rows_at(index + places, rows), :]
        out[to, qkv_width + EXTRA :] = dot(below, att_ref[...], ((1,), (0,))).astype(BF16)


def input_grad_kernel(meta, hidden, gain, dh_ref, gains_ref, *refs):
    parts, out_ref = refs[:-1], refs[-1]
    block, width = dh_ref.shape
    dn1 = parts[0][...]
    for part in parts[1:]:
        dn1 = dn1 + part[:, :width].astype(F32)
    x = hidden[rows_at(meta[0], block), :].astype(F32)
    scale = unit_rows(x)
    hat = x * scale
    gained = dn1 * gain[0:1, :]
    grad = dh_ref[...] + scale * (gained - hat * jnp.mean(gained * hat, -1, keepdims=True))
    out_ref[:, :width] = grad.astype(BF16)
    rows, columns = gains_ref.shape
    gains = gains_ref[...]
    high = gains.astype(BF16).astype(F32)
    out_ref[:, width:] = jnp.zeros((block, EXTRA), BF16)
    out_ref[: 2 * rows, width : width + columns] = jnp.concatenate(
        [high, gains - high], 0
    ).astype(BF16)


def place_last_kernel(tensor_n, meta, layer_own, *refs):
    layers, blocks = refs[: tensor_n - 1], refs[tensor_n - 1 : -4]
    layer_ref, grad_ref, first_ref, second_ref = refs[-4:]
    rows, width = layer_own.shape
    layer_ref[rows_at(meta[0], rows), :] = layer_own[...]
    for k, ref in enumerate(layers, 1):
        layer_ref[rows_at(meta[0] ^ k, rows), :] = ref[:, width:]
    gains = 0.0
    for k, ref in enumerate(blocks):
        grad_ref[rows_at(meta[0] ^ k, rows), :] = ref[:, :width].astype(F32)
        gains = gains + ref[:16, width:].astype(F32)
    gains = gains[:8] + gains[8:]
    columns = first_ref.shape[1]
    second_ref[...] = gains[0:1, :columns]
    first_ref[...] = gains[1:2, :columns]


def half_kernel(near, got, out_ref):
    half = out_ref.shape[0]
    out_ref[...] = (near[half:, :].astype(F32) + got[half:, :].astype(F32)).astype(BF16)


def add_kernel(near, got, own_ref, *sent_refs):
    rows = own_ref.shape[0]
    for k, ref in enumerate([own_ref] + list(sent_refs)):
        at = slice(k * rows, (k + 1) * rows)
        ref[...] = (near[at, :].astype(F32) + got[at, :].astype(F32)).astype(ref.dtype)


def last_kernel(experts, q_width, kv_width, *refs):
    parts, outs = refs[:-6], refs[-6:]
    total = parts[0][...]
    for part in parts[1:]:
        total = total + part[...].astype(F32)
    at = 0
    for ref, width in zip(outs[:3], (q_width, kv_width, kv_width)):
        ref[...] = total[:, at : at + width]
        at += width
    side = total[:, at : at + EXTRA]
    outs[3][...] = total[:, at + EXTRA :]
    side = side.T
    outs[4][...] = side[:experts]
    outs[5][...] = side[experts : experts + 8]


def pair_of(local_experts):
    return 2 if local_experts % 2 == 0 else 1


def kernel_params(tokens, vmem=28):
    return pltpu.CompilerParams(vmem_limit_bytes=(vmem if tokens <= 512 else 60) * 2**20)


def side_by_side(ref, first, count):
    parts = [ref[first + i] for i in range(count)]
    return parts[0] if count == 1 else jnp.concatenate(parts, 1)


def split_rows(chunk, chunks, value, near_ref, far_ref):
    if chunks == 1:
        half = value.shape[0] // 2
        near_ref[...] = value[:half]
        far_ref[...] = value[half:]
        return
    rows = value.shape[0]

    @pl.when(chunk < chunks // 2)
    def _():
        near_ref[pl.ds(pl.multiple_of(chunk * rows, rows), rows), :] = value

    @pl.when(chunk >= chunks // 2)
    def _():
        at = (chunk - chunks // 2) * rows
        far_ref[pl.ds(pl.multiple_of(at, rows), rows), :] = value


def expert_kernel(own, steps, pair, experts, parts, extra, *refs):
    meta_ref, refs = refs[0], refs[1:]
    x_parts, dy_parts, refs = refs[:parts], refs[parts : 2 * parts], refs[2 * parts :]
    gate_ref, up_ref, down_ref, router_ref = refs[:4]
    refs = refs[extra:]
    both_ref, gated_ref = refs[4:6]
    if own:
        dg_ref, dg_scr = refs[6], refs[-1]
        refs = refs[7:-1]
    else:
        refs = refs[6:]
    gates_scr, x_ref, dy_ref = refs
    step = pl.program_id(1)
    width = x_ref.shape[1]
    lanes = gates_scr.shape[1]

    @pl.when(step == 0)
    def _():
        part_rows = x_parts[0].shape[0]
        for n in range(parts):
            x_ref[n * part_rows : (n + 1) * part_rows, :] = x_parts[n][...]
            dy_ref[n * part_rows : (n + 1) * part_rows, :] = dy_parts[n][...]
        logits = dot(x_ref[...], router_ref[...], ((1,), (1,)))
        routed = dy_ref[:, width : width + experts].astype(F32) > 0.5
        logits = jnp.where(routed, logits, -1e30)
        weights = jnp.exp(logits - jnp.max(logits, -1, keepdims=True))
        gates_scr[...] = jnp.zeros_like(gates_scr)
        gates_scr[:, :experts] = weights / jnp.sum(weights, -1, keepdims=True)
        if own:
            dg_scr[...] = jnp.zeros_like(dg_scr)

    first = meta_ref[1] * (pair * steps) + step * pair
    gates = pltpu.roll(gates_scr[...], lax.rem(lanes - first, lanes), 1)
    raw_all = dot(dy_ref[:, :width], side_by_side(down_ref, 0, pair), ((1,), (0,)))
    units = gate_ref.shape[2]
    column = lax.broadcasted_iota(jnp.int32, gates.shape, 1)
    weight = jnp.concatenate([r[i] for i in range(pair) for r in (gate_ref, up_ref)], 1)
    both_all = dot(x_ref[...], weight, ((1,), (0,)))
    for i in range(pair):
        gate_proj = both_all[:, 2 * i * units : (2 * i + 1) * units]
        up_proj = both_all[:, (2 * i + 1) * units : (2 * i + 2) * units]
        raw = raw_all[:, i * units : (i + 1) * units]
        mine = gates[:, i : i + 1]
        sigmoid_gate = 0.5 * jnp.tanh(0.5 * gate_proj) + 0.5
        activated = gate_proj * sigmoid_gate
        hidden = activated * up_proj
        grad_hidden = raw * mine
        grad_gate = grad_hidden * up_proj * (sigmoid_gate + activated * (1.0 - sigmoid_gate))
        at = 2 * i * units
        both_ref[:, at : at + units] = grad_gate.astype(BF16)
        both_ref[:, at + units : at + 2 * units] = (grad_hidden * activated).astype(BF16)
        gated_ref[:, i * units : (i + 1) * units] = (hidden * mine).astype(BF16)
        if own:
            dg = jnp.sum(raw * hidden, 1, keepdims=True)
            dg_scr[...] += jnp.where(column == first + i, dg, 0.0)
    if own:

        @pl.when(step == steps - 1)
        def _():
            dg = dg_scr[...]
            high = dg.astype(BF16).astype(F32)
            low = pltpu.roll(dg - high, experts, 1)
            dg_ref[...] = (high + low).astype(BF16)


def expert_call(own, meta, xs, dys, gate_weight, up_weight, down_weight, router_weight, after=()):
    part_rows, width = xs[0].shape
    parts = len(xs)
    tokens = part_rows * parts
    if tokens > 512:
        xs, dys, parts = [jnp.concatenate(xs, 0)], [jnp.concatenate(dys, 0)], 1
        part_rows = tokens
    dy_width = dys[0].shape[1]
    local, _, units = gate_weight.shape
    experts = router_weight.shape[0]
    pair = pair_of(local)
    rows = min(tokens, 512)
    chunks, steps = tokens // rows, local // pair
    grid_spec = dict(
        grid=(chunks, steps),
        in_specs=[
            pl.BlockSpec(memory_space=pltpu.SMEM),
        ]
        + [pl.BlockSpec((rows // parts, width), lambda c, s: (c, 0))] * parts
        + [pl.BlockSpec((rows // parts, dy_width), lambda c, s: (c, 0))] * parts
        + [pl.BlockSpec((pair, width, units), lambda c, s: (s, 0, 0))] * 3
        + [pl.BlockSpec(router_weight.shape, lambda c, s: (0, 0))]
        + [pl.BlockSpec(memory_space=pl.ANY)] * len(after),
        out_specs=[
            pl.BlockSpec((rows, pair * 2 * units), lambda c, s: (c, s)),
            pl.BlockSpec((rows, pair * units), lambda c, s: (c, s)),
        ],
        scratch_shapes=[
            pltpu.VMEM((rows, 128), F32),
            pltpu.VMEM((rows, width), BF16),
            pltpu.VMEM((rows, dy_width), BF16),
        ],
    )
    out_shape = [
        jax.ShapeDtypeStruct((tokens, local * 2 * units), BF16),
        jax.ShapeDtypeStruct((tokens, local * units), BF16),
    ]
    if own:
        grid_spec["out_specs"] += [pl.BlockSpec((rows, EXTRA), lambda c, s: (c, 0))]
        out_shape += [jax.ShapeDtypeStruct((tokens, EXTRA), BF16)]
        grid_spec["scratch_shapes"] += [pltpu.VMEM((rows, 128), F32)]
    products = 3
    return pl.pallas_call(
        functools.partial(expert_kernel, own, steps, pair, experts, parts, len(after)),
        out_shape=out_shape,
        compiler_params=kernel_params(tokens),
        cost_estimate=pl.CostEstimate(
            flops=2 * products * tokens * width * local * units,
            bytes_accessed=2 * (3 * local * width * units + 3 * tokens * width),
            transcendentals=tokens * local * units,
        ),
        name="experts_own" if own else "experts_far",
        **grid_spec,
    )(meta, *xs, *dys, gate_weight, up_weight, down_weight, router_weight, *after)


def arrival_kernel(chunks, steps, pair, both_ref, dg_ref, gate_ref, up_ref, *refs):
    near_ref, far_ref, total_scr = refs[-3:]
    chunk, step = pl.program_id(0), pl.program_id(1)

    @pl.when(step == 0)
    def _():
        total_scr[...] = jnp.zeros_like(total_scr)

    weight = jnp.concatenate([r[i] for i in range(pair) for r in (gate_ref, up_ref)], 1)
    total_scr[...] += dot(both_ref[...], weight, ((1,), (1,)))

    @pl.when(step == steps - 1)
    def _():
        message = jnp.concatenate([total_scr[...].astype(BF16), dg_ref[...]], 1)
        split_rows(chunk, chunks, message, near_ref, far_ref)


def arrival_call(both, dg, gate_weight, up_weight, after=()):
    tokens = both.shape[0]
    local, width, units = gate_weight.shape
    pair = pair_of(local)
    rows = min(tokens, 512)
    chunks, steps = tokens // rows, local // pair
    half = (tokens // 2, width + EXTRA)
    return pl.pallas_call(
        functools.partial(arrival_kernel, chunks, steps, pair),
        grid=(chunks, steps),
        in_specs=[
            pl.BlockSpec((rows, pair * 2 * units), lambda c, s: (c, s)),
            pl.BlockSpec((rows, EXTRA), lambda c, s: (c, 0)),
        ]
        + [pl.BlockSpec((pair, width, units), lambda c, s: (s, 0, 0))] * 2
        + [pl.BlockSpec(memory_space=pl.ANY)] * len(after),
        out_specs=[pl.BlockSpec(half, lambda c, s: (0, 0))] * 2,
        out_shape=[jax.ShapeDtypeStruct(half, BF16)] * 2,
        scratch_shapes=[pltpu.VMEM((rows, width), F32)],
        compiler_params=kernel_params(tokens),
        cost_estimate=pl.CostEstimate(
            flops=4 * tokens * width * local * units,
            bytes_accessed=4 * (local * width * units + 2 * tokens * width),
            transcendentals=0,
        ),
        name="experts_arrival",
    )(both, dg, gate_weight, up_weight, *after)


def mixed_kernel(chunks, steps, pair, gated_ref, down_ref, *refs):
    near_ref, far_ref, total_scr = refs[-3:]
    chunk, step = pl.program_id(0), pl.program_id(1)

    @pl.when(step == 0)
    def _():
        total_scr[...] = jnp.zeros_like(total_scr)

    total_scr[...] += dot(gated_ref[...], side_by_side(down_ref, 0, pair), ((1,), (1,)))

    @pl.when(step == steps - 1)
    def _():
        split_rows(chunk, chunks, total_scr[...].astype(BF16), near_ref, far_ref)


def mixed_call(gated, down_weight, after=()):
    tokens = gated.shape[0]
    local, width, units = down_weight.shape
    pair = pair_of(local)
    rows = min(tokens, 512)
    chunks, steps = tokens // rows, local // pair
    half = (tokens // 2, width)
    return pl.pallas_call(
        functools.partial(mixed_kernel, chunks, steps, pair),
        grid=(chunks, steps),
        in_specs=[
            pl.BlockSpec((rows, pair * units), lambda c, s: (c, s)),
            pl.BlockSpec((pair, width, units), lambda c, s: (s, 0, 0)),
        ]
        + [pl.BlockSpec(memory_space=pl.ANY)] * len(after),
        out_specs=[pl.BlockSpec(half, lambda c, s: (0, 0))] * 2,
        out_shape=[jax.ShapeDtypeStruct(half, BF16)] * 2,
        scratch_shapes=[pltpu.VMEM((rows, width), F32)],
        compiler_params=kernel_params(tokens),
        cost_estimate=pl.CostEstimate(
            flops=2 * tokens * width * local * units,
            bytes_accessed=2 * (local * width * units + 2 * tokens * width),
            transcendentals=0,
        ),
        name="experts_mixed",
    )(gated, down_weight, *after)


def weight_grad_kernel(sets, parts, outs, pair, units, place_ref, *refs):
    lefts, rights = refs[: sets * parts], refs[sets * parts : sets * parts + sets]
    grad_refs, left_scr = refs[-1 - outs : -1], refs[-1]

    @pl.when(pl.program_id(0) == 0)
    def _():
        for n in range(sets * parts):
            rows = lefts[n].shape[0]
            left_scr[:, n * rows : (n + 1) * rows] = lefts[n][...].T

    rows = rights[0].shape[0]
    total = None
    for n in range(sets):
        part = dot(left_scr[:, n * rows : (n + 1) * rows], rights[n][...], ((1,), (0,)))
        total = part if total is None else total + part
    for i in range(pair):
        for j in range(outs):
            at = (i * outs + j) * units
            grad_refs[j][i] = total[:, at : at + units]


def weight_grad_call(meta, lefts, rights, local, units, after=()):
    sets, parts = len(lefts), len(lefts[0])
    outs = rights[0].shape[1] // (local * units)
    part_rows = lefts[0][0].shape[0]
    width = lefts[0][0].shape[1] // 128 // sets * 128
    tokens = part_rows * parts
    lefts = sum(lefts, [])
    pair = pair_of(local)
    columns = pl.BlockSpec(
        (part_rows, width), lambda s, meta: (0, meta[2]), pipeline_mode=pl.Buffered(1)
    )
    return pl.pallas_call(
        functools.partial(weight_grad_kernel, sets, parts, outs, pair, units),
        grid_spec=pltpu.PrefetchScalarGridSpec(
            num_scalar_prefetch=1,
            grid=(local // pair,),
            in_specs=[columns] * (sets * parts)
            + [pl.BlockSpec((tokens, pair * outs * units), lambda s, meta: (0, s))] * sets
            + [pl.BlockSpec(memory_space=pl.ANY)] * len(after),
            out_specs=[pl.BlockSpec((pair, width, units), lambda s, meta: (s, 0, 0))] * outs,
            scratch_shapes=[pltpu.VMEM((width, sets * tokens), BF16)],
        ),
        out_shape=[jax.ShapeDtypeStruct((local, width, units), F32)] * outs,
        compiler_params=kernel_params(tokens),
        cost_estimate=pl.CostEstimate(
            flops=2 * sets * tokens * width * outs * local * units,
            bytes_accessed=4 * outs * local * width * units + 4 * sets * tokens * width,
            transcendentals=0,
        ),
        name="experts_weight_grads",
    )(meta, *lefts, *rights, *after)


def reduce_first(near, far, after=()):
    bits = list(reversed(bits_of(lax.axis_size("expert"))))
    for k in bits[:-2]:
        got = swap(far, "expert", k)
        total = (near.astype(F32) + got.astype(F32)).astype(BF16)
        near, far = jnp.split(total, 2, 0)
    got = swap(far, "expert", bits[-2])
    half = near.shape[0] // 2
    if after:
        (sent,) = plain_call(
            half_kernel,
            "half",
            [array((half, near.shape[1]), BF16)],
            [],
            near.size,
            near,
            got,
            after=after,
        )
    else:
        sent = (near[half:].astype(F32) + got[half:].astype(F32)).astype(BF16)
    return near, got, swap(sent, "expert", bits[-1])


def on_device(
    hidden_in,
    seq_lengths,
    expert_routes,
    first_gain,
    query_weight,
    key_weight,
    value_weight,
    output_weight,
    second_gain,
    router_weight,
    gate_weight,
    up_weight,
    down_weight,
    grad_layer_out,
):
    tokens_here, model_width = hidden_in.shape
    q_width, kv_width = query_weight.shape[1], key_weight.shape[1]
    heads, group = q_width // HD, q_width // kv_width
    expert_count = router_weight.shape[1]
    local_experts, _, units = gate_weight.shape
    tensor_n = lax.axis_size("tensor")
    expert_n = lax.axis_size("expert")
    dp_n = lax.axis_size("dp")
    block = tokens_here // tensor_n
    meta = jnp.stack([lax.axis_index(a) for a in ("tensor", "expert", "dp")]).astype(jnp.int32)
    gain_rows = jnp.stack([first_gain, second_gain]).astype(F32)

    (grad_own,) = plain_call(
        routes_kernel,
        "routes",
        [array((tokens_here, model_width + EXTRA), BF16)],
        [],
        tokens_here * model_width,
        expert_routes.T,
        grad_layer_out,
        vmem=60,
    )

    cosine, sine = rope_tables(tokens_here)
    blocks = block_shapes(block, model_width, tensor_n)
    n1, qkv, prob, att, cosine, sine, part, *sent = plain_call(
        functools.partial(attend_kernel, heads, group),
        "attend",
        [
            array((tokens_here, model_width), BF16),
            array((tokens_here, q_width + 2 * kv_width), BF16),
            array((heads, tokens_here, tokens_here), F32),
            array((tokens_here, q_width), BF16),
            array(cosine.shape, F32),
            array(sine.shape, F32),
        ]
        + blocks,
        [pltpu.VMEM((tokens_here, model_width), F32)],
        2 * tokens_here * model_width * 3 * q_width,
        meta,
        seq_lengths,
        hidden_in,
        gain_rows,
        query_weight,
        key_weight,
        value_weight,
        output_weight,
        cosine,
        sine,
        vmem=60,
    )
    far_grads = [swap(grad_own, "dp", k) for k in range(1, dp_n)]
    if expert_n == 4:
        far_grads += [swap_plane(grad_own, k, 2) for k in range(1, dp_n)]
    residual, second_block, grad_near = plain_call(
        second_norm_kernel,
        "second_norm",
        [
            array((block, model_width), F32),
            array((block, model_width), BF16),
            array(grad_own.shape, BF16),
        ],
        [],
        8 * block * model_width,
        gain_rows,
        grad_own,
        part,
        *swap_tensor(sent),
        after=far_grads,
    )
    grad_sets = gather_sets(grad_own, grad_near)
    (second_group,) = plain_call(
        place_kernel,
        "place_second",
        [array((tokens_here, model_width), BF16)],
        [],
        tokens_here * model_width,
        meta,
        *gather_tensor(second_block),
        after=grad_sets[0][1:2],
    )
    second_sets = gather_sets(second_group)

    router_t = router_weight.T
    weights = (gate_weight, up_weight, down_weight, router_t)
    far_grads = [g for x in grad_sets[1:] for g in x[2:]]
    own = expert_call(True, meta, second_sets[0], grad_sets[0], *weights, after=far_grads)
    arrival = arrival_call(
        own[0], own[2], gate_weight, up_weight, after=[x for y in second_sets[1:] for x in y[:2]]
    )
    sides = [own] + [
        expert_call(False, meta, second_sets[i], grad_sets[i], *weights) for i in range(1, dp_n)
    ]
    mixed = mixed_call(own[1], down_weight, after=arrival[:1])
    arrival = plain_call(
        halves_kernel,
        "arrival_blocks",
        block_shapes(block, model_width + EXTRA, tensor_n),
        [pltpu.VMEM((tokens_here, model_width + EXTRA), F32)],
        2 * tokens_here * model_width,
        meta,
        *reduce_first(*arrival),
        after=[mixed[0]] + [x[1] for x in sides[1:]],
    )
    mixed = reduce_first(*mixed, after=arrival[:1])
    arrival = [arrival[0]] + swap_tensor(arrival[1:])
    (grad_down,) = weight_grad_call(
        meta, grad_sets, [x[1] for x in sides], local_experts, units
    )
    grad_gate, grad_upproj = weight_grad_call(
        meta, second_sets, [x[0] for x in sides], local_experts, units
    )

    grad_resid, gain_row, message, mixed_own, *sent = plain_call(
        functools.partial(residual_grad_kernel, expert_count, tensor_n),
        "residual_grad",
        [
            array((block, model_width), F32),
            array((8, model_width), F32),
            array((block, model_width + EXTRA), BF16),
            array((block, model_width), F32),
        ]
        + [array((block, 2 * model_width + EXTRA), BF16)] * (tensor_n - 1),
        [pltpu.VMEM((tokens_here, model_width), F32)],
        20 * block * model_width,
        meta,
        residual,
        second_block,
        grad_own,
        router_t,
        gain_rows,
        *mixed,
        *arrival,
        after=[grad_down],
    )
    places = expert_n * dp_n
    rows = model_width // places
    last_width = 2 * q_width + 2 * kv_width + EXTRA
    near, far, layer_block, *dn1 = plain_call(
        functools.partial(
            attend_grad_kernel, heads, group, expert_count, expert_n, dp_n, tensor_n
        ),
        "attend_grad",
        [array((model_width // 2, last_width), BF16)] * 2
        + [array((block, model_width), BF16), array((block, model_width), F32)]
        + [array((block, 2 * model_width), BF16)] * (tensor_n - 1),
        [
            pltpu.VMEM((tokens_here, model_width + EXTRA), BF16),
            pltpu.VMEM((tokens_here, q_width + 2 * kv_width), BF16),
            pltpu.VMEM((tokens_here, q_width + kv_width), F32),
            pltpu.VMEM((tokens_here, model_width), F32),
            pltpu.VMEM((2 * model_width, tokens_here), BF16),
            pltpu.VMEM((model_width, EXTRA), BF16),
        ],
        2 * tokens_here * model_width * 6 * q_width,
        meta,
        hidden_in,
        gain_row,
        n1,
        second_group,
        qkv,
        prob,
        att,
        cosine,
        sine,
        query_weight,
        key_weight,
        value_weight,
        output_weight,
        message,
        *swap_tensor(sent),
        mixed_own,
        residual,
        after=[grad_gate],
    )

    expert_bits = list(reversed(bits_of(expert_n)))
    for k in expert_bits[:-2]:
        total = near.astype(F32) + swap(far, "expert", k).astype(F32)
        near, far = jnp.split(total.astype(BF16), 2, 0)
    got = swap(far, "expert", expert_bits[-2])
    shapes = [array((rows, last_width), F32)] + [array((rows, last_width), BF16)] * (2 * dp_n - 1)
    own_rows, *sent = plain_call(
        add_kernel, "plane_add", shapes, [], model_width * last_width, near, got
    )
    ways = [(k % dp_n, (k // dp_n) * expert_bits[-1]) for k in range(1, 2 * dp_n)]
    got = [swap_plane(x, *way) for x, way in zip(sent, ways)]
    grad_query, grad_key, grad_value, grad_outproj, grad_router, gains = plain_call(
        functools.partial(last_kernel, expert_count, q_width, kv_width),
        "plane_last",
        [
            array((rows, q_width), F32),
            array((rows, kv_width), F32),
            array((rows, kv_width), F32),
            array((rows, q_width), F32),
            array((expert_count, rows), F32),
            array((8, rows), F32),
        ],
        [],
        4 * rows * last_width,
        own_rows,
        *got,
    )
    dn1 = [dn1[0]] + swap_tensor(dn1[1:])

    (last_block,) = plain_call(
        input_grad_kernel,
        "input_grad",
        [array((block, model_width + EXTRA), BF16)],
        [],
        10 * block * model_width,
        meta,
        hidden_in,
        gain_rows,
        grad_resid,
        gains,
        *dn1,
    )
    layer_out, grad_input, grad_first_out, grad_second_out = plain_call(
        functools.partial(place_last_kernel, tensor_n),
        "place_last",
        [
            array((tokens_here, model_width), BF16),
            array((tokens_here, model_width), F32),
            array((1, rows), F32),
            array((1, rows), F32),
        ],
        [],
        tokens_here * model_width,
        meta,
        layer_block,
        *dn1[1:],
        *gather_tensor(last_block),
    )
    return (
        layer_out,
        grad_input,
        grad_first_out[0],
        grad_query,
        grad_key,
        grad_value,
        grad_outproj,
        grad_second_out[0],
        grad_router.T,
        grad_gate,
        grad_upproj,
        grad_down,
    )


def solution(mesh):
    tokens = P(("dp", "expert"), None)
    columns = P(None, "tensor")
    experts = P("expert", None, "tensor")
    rows = P(("dp", "expert"))
    both = P(("dp", "expert"), "tensor")
    expert_grads = P("expert", "dp", "tensor")
    return jax.shard_map(
        on_device,
        mesh=mesh,
        in_specs=(tokens, tokens, tokens, P())
        + (columns,) * 4
        + (P(), P())
        + (experts,) * 3
        + (tokens,),
        out_specs=(tokens, tokens, rows)
        + (both,) * 4
        + (rows, tokens)
        + (expert_grads,) * 3,
        check_vma=False,
    )
```

time: 187 us -> 137 us (0.73)
  Pallas kernels: 24.3 us -> 44.4 us
  starting transfers between devices: 61.3 us -> 44.3 us
  local copies, waits for them, and re-layouts: 25.9 us -> 9.4 us
  matrix products: 13.3 us -> 0 us
  other arithmetic: 12.8 us -> 1.34 us
  waiting for transfers between devices: 44.5 us -> 36.3 us
  between operations: 4.01 us -> 1.01 us
    ppermute x53 -> x35, starting transfers between devices: 61.3 us -> 37.7 us  [swap(): return lax.ppermute(x, axis, [(i, i ^ k) for i in range(n)])]
    pallas_call x3 -> x17, Pallas kernels: 22 us -> 42.1 us  [the longest x12 15.6 us: plain_call(): pl.pallas_call(body, grid=(1,), in_specs=[whole(a) for a in arrays[:count...]
    ppermute x53 -> x35, waiting for transfers between devices: 44.5 us -> 29 us  [swap(): return lax.ppermute(x, axis, [(i, i ^ k) for i in range(n)])]
    dot_general x20 -> x0, matrix products: 12.3 us -> none  [the longest x15 10.2 us: dot(): lax.dot_general(left, right, (dims, ((), ())), preferred_element_type=F32...]
    ppermute x0 -> x5, waiting for transfers between devices: none -> 7.32 us  [swap_plane(): lax.ppermute(x, ('dp', 'expert'), [(i, i ^ k_dp * n + k_expert) for i in...]
    ppermute x0 -> x5, starting transfers between devices: none -> 6.53 us  [swap_plane(): lax.ppermute(x, ('dp', 'expert'), [(i, i ^ k_dp * n + k_expert) for i in...]
    concatenate x8 -> x0, local copies, waits for them, and re-layouts: 5.37 us -> none  [the longest x3 5.07 us: on_device(): jnp.concatenate([dot(first_normed, grad_query_pre, ((0,), (0,))), dot(fir...]
    squeeze x6 -> x0, local copies, waits for them, and re-layouts: 5.15 us -> none  [the longest x2 3.56 us: reduce_plane(): keep = lax.dynamic_index_in_dim(x, bit, at, keepdims=False)]
  transfers between devices with their start and end apart: 53 -> 40, of which waited for: 17 -> 15; matrix products, arithmetic and copies ran while one was open for 24% -> 2% of each run, Pallas kernels for 13% -> 23%
where the time goes in v3:
time: 137 us
  Pallas kernels  44.4 us (32%)
  starting transfers between devices  44.3 us (32%)
  waiting for transfers between devices  36.3 us (26%)
  local copies, waits for them, and re-layouts  9.4 us (7%)
    ppermute x35, starting transfers between devices, swap(): return lax.ppermute(x, axis, [(i, i ^ k) for i in range(n)])  37.7 us
    ppermute x35, waiting for transfers between devices, swap(): return lax.ppermute(x, axis, [(i, i ^ k) for i in range(n)])  29 us
    pallas_call x12, Pallas kernels, plain_call(): pl.pallas_call(body, grid=(1,), in_specs=[whole(a) for a in arrays[:count...  15.6 us
    pallas_call x2, Pallas kernels, expert_call(): pl.pallas_call(functools.partial(expert_kernel, own, steps, pair, experts...  13.1 us
    pallas_call x2, Pallas kernels, weight_grad_call(): pl.pallas_call(functools.partial(weight_grad_kernel, sets, parts, outs, p...  9.97 us
    unnamed x48, local copies, waits for them, and re-layouts  8.03 us
    ppermute x5, waiting for transfers between devices, swap_plane(): lax.ppermute(x, ('dp', 'expert'), [(i, i ^ k_dp * n + k_expert) for i in...  7.32 us
    ppermute x5, starting transfers between devices, swap_plane(): lax.ppermute(x, ('dp', 'expert'), [(i, i ^ k_dp * n + k_expert) for i in...  6.53 us
  transfers between devices with their start and end apart: 40, of which 15 were waited for; matrix products, arithmetic and copies ran while one was open for 2% of the time, Pallas kernels for 23%

profile of v3, /device:TPU:0, one launch (start us, length us, event | category | flops | bytes accessed | tf_op | source)
XLA Modules:
  0.0 136.7 jit_solution(5040563760530022132)
XLA Ops:
  0.7 2.2 %routes.1.refs_1_.refs_3_ = bf16[128,1152]{1,0:T(8,128)(2,1)} custom-call(s32[8,128]{1,0:T(8,128)} %bitcast.11, bf16[128,1024]{1,0:T(8,128)(2,1)} %refs_1_.4), custom_call_target="tpu_custom_call" | custom-call | flops 131072 | bytes 561152 | tf_op jit(solution)/shard_map/routes/pallas_call | solution.py:121
  2.8 2.9 %collective-permute-start.3 = (bf16[128,1152]{1,0:T(8,128)(2,1)}, bf16[128,1152]{1,0:T(8,128)(2,1)S(1)}, u32[]{:S(2)}, u32[]{:S(2)}) collective-permute-start(bf16[128,1152]{1,0:T(8,128)(2,1)} %routes.1.refs_1_.refs_3_), channel_id=1, source_target_pairs={{0,16},{16,0},{1,17},{17,1},{2,18},{18,2},{3,19},{19,3},{4,20},{20... | collective-permute-start | bytes 884744 | tf_op jit(solution)/shard_map/ppermute | solution.py:60
  9.9 4.2 %attend.1 = (bf16[128,1024]{1,0:T(8,128)(2,1)}, bf16[128,512]{1,0:T(8,128)(2,1)}, f32[4,128,128]{2,1,0:T(8,128)}, bf16[128,256]{1,0:T(8,128)(2,1)}, f32[128,128]...) custom-call(s32[3]{0:T(128)} %pad_add_fusion.refs_0_.place_ref, ...), custom_call_target="tpu_custom_call" | custom-call | flops 201326592 | bytes 3153944 | tf_op jit(solution)/shard_map/attend/pallas_call | solution.py:121
  14.1 1.6 %collective-permute-start = (bf16[32,1024]{1,0:T(8,128)(2,1)}, bf16[32,1024]{1,0:T(8,128)(2,1)S(1)}, u32[]{:S(2)}, u32[]{:S(2)}) collective-permute-start(bf16[32,1024]{1,0:T(8,128)(2,1)} %get-tuple-element.69), channel_id=1, source_target_pairs={{0,1},{1,0},{2,3},{3,2},{4,5},{5,4},{6,7},{7,6},{8,9},{9,8},{10,11... | collective-permute-start | bytes 196616 | tf_op jit(solution)/shard_map/ppermute | solution.py:60
  15.7 2.6 %collective-permute-start.1 = (bf16[32,1024]{1,0:T(8,128)(2,1)}, bf16[32,1024]{1,0:T(8,128)(2,1)S(1)}, u32[]{:S(2)}, u32[]{:S(2)}) collective-permute-start(bf16[32,1024]{1,0:T(8,128)(2,1)} %get-tuple-element.70), channel_id=1, source_target_pairs={{0,2},{1,3},{2,0},{3,1},{4,6},{5,7},{6,4},{7,5},{8,10},{9,11},{10,... | collective-permute-start | bytes 196616 | tf_op jit(solution)/shard_map/ppermute | solution.py:60
  19.3 3.4 %collective-permute-done.1.refs_4_ = bf16[32,1024]{1,0:T(8,128)(2,1)S(1)} collective-permute-done((bf16[32,1024]{1,0:T(8,128)(2,1)}, bf16[32,1024]{1,0:T(8,128)(2,1)S(1)}, u32[]{:S(2)}, u32[]{:S(2)}) %collective-permute-start.1) | collective-permute-done | bytes 65568 | tf_op jit(solution)/shard_map/ppermute | solution.py:60
  22.6 2.0 %collective-permute-done.2.refs_5_ = bf16[32,1024]{1,0:T(8,128)(2,1)S(1)} collective-permute-done((bf16[32,1024]{1,0:T(8,128)(2,1)}, bf16[32,1024]{1,0:T(8,128)(2,1)S(1)}, u32[]{:S(2)}, u32[]{:S(2)}) %collective-permute-start.2) | collective-permute-done | bytes 65568 | tf_op jit(solution)/shard_map/ppermute | solution.py:60
  26.9 1.8 %collective-permute-start.6 = (bf16[32,1024]{1,0:T(8,128)(2,1)S(1)}, bf16[32,1024]{1,0:T(8,128)(2,1)S(1)}, u32[]{:S(2)}, u32[]{:S(2)}) collective-permute-start(bf16[32,1024]{1,0:T(8,128)(2,1)S(1)} %get-tuple-element.73.refs_1_.refs_2_), channel_id=1, source_target_pairs={{0,2},{1,3},{2,0},{3,1},{4,6},{5,7},{6,4},{7,5},{8,10},{9,11},{10,... | collective-permute-start | bytes 196616 | tf_op jit(solution)/shard_map/ppermute | solution.py:60
  28.7 2.6 %collective-permute-start.7 = (bf16[32,1024]{1,0:T(8,128)(2,1)S(1)}, bf16[32,1024]{1,0:T(8,128)(2,1)S(1)}, u32[]{:S(2)}, u32[]{:S(2)}) collective-permute-start(bf16[32,1024]{1,0:T(8,128)(2,1)S(1)} %get-tuple-element.73.refs_1_.refs_2_), channel_id=1, source_target_pairs={{0,3},{1,2},{2,1},{3,0},{4,7},{5,6},{6,5},{7,4},{8,11},{9,10},{10,... | collective-permute-start | bytes 196616 | tf_op jit(solution)/shard_map/ppermute | solution.py:60
  32.6 2.3 %collective-permute-done.7.refs_4_ = bf16[32,1024]{1,0:T(8,128)(2,1)S(1)} collective-permute-done((bf16[32,1024]{1,0:T(8,128)(2,1)S(1)}, bf16[32,1024]{1,0:T(8,128)(2,1)S(1)}, u32[]{:S(2)}, u32[]{:S(2)}) %collective-permute-start.7) | collective-permute-done | bytes 65568 | tf_op jit(solution)/shard_map/ppermute | solution.py:60
  38.1 3.8 %collective-permute-done.9.refs_2_.refs_1_ = bf16[128,1024]{1,0:T(8,128)(2,1)S(1)} collective-permute-done((bf16[128,1024]{1,0:T(8,128)(2,1)S(1)}, bf16[128,1024]{1,0:T(8,128)(2,1)S(1)}, u32[]{:S(2)}, u32[]{:S(2)}) %collective-permute-start.9) | collective-permute-done | bytes 262176 | tf_op jit(solution)/shard_map/ppermute | solution.py:60
  48.1 6.8 %experts_own.1 = (bf16[512,2048]{1,0:T(8,128)(2,1)S(1)}, bf16[512,1024]{1,0:T(8,128)(2,1)S(1)}, bf16[512,128]{1,0:T(8,128)(2,1)S(1)}) custom-call(s32[3]{0:T(128)S(1)} %copy-done.18, bf16[128,1024]{1,0:T(8,128)(2,1)S(1)} %place_second.1.refs_1_.refs_0_.refs_4_, bf16[128,1024]{1,0:T(8,128)(2,1)S(1)} %collective-permute-done.9.refs_2_.refs_1_, ...), custom_call_target="tpu_custom_call" | custom-call | flops 3221225472 | bytes 9437184 | tf_op jit(solution)/shard_map/experts_own/pallas_call | solution.py:570
  54.9 2.3 %collective-permute-done.17.refs_1_.refs_2_.refs_5_ = bf16[128,1024]{1,0:T(8,128)(2,1)S(1)} collective-permute-done((bf16[128,1024]{1,0:T(8,128)(2,1)S(1)}, bf16[128,1024]{1,0:T(8,128)(2,1)S(1)}, u32[]{:S(2)}, u32[]{:S(2)}) %collective-permute-start.17) | collective-permute-done | bytes 262176 | tf_op jit(solution)/shard_map/ppermute | solution.py:66
  57.2 3.4 %experts_arrival.1 = (bf16[256,1152]{1,0:T(8,128)(2,1)S(1)}, bf16[256,1152]{1,0:T(8,128)(2,1)S(1)}) custom-call(bf16[512,2048]{1,0:T(8,128)(2,1)S(1)} %get-tuple-element.76.both_ref.refs_8_, bf16[512,128]{1,0:T(8,128)(2,1)S(1)} %get-tuple-element.77.dg_ref, bf16[8,1024,128]{2,1,0:T(8,128)(2,1)S(1)} %copy-done.19, bf16[8,1024,128]{2,1,0:T(8,128)(2,1)S(1)} %copy-done.20, ...), custom_call_target="tpu_custom_call" | custom-call | flops 2147483648 | bytes 8388608 | tf_op jit(solution)/shard_map/experts_arrival/pallas_call | solution.py:608
  61.3 2.3 %experts_mixed.1 = (bf16[256,1024]{1,0:T(8,128)(2,1)S(1)}, bf16[256,1024]{1,0:T(8,128)(2,1)S(1)}) custom-call(bf16[512,1024]{1,0:T(8,128)(2,1)S(1)} %get-tuple-element.75.gated_ref.refs_8_, bf16[8,1024,128]{2,1,0:T(8,128)(2,1)S(1)} %copy-done.23, bf16[256,1152]{1,0:T(8,128)(2,1)S(1)} %get-tuple-element.78.refs_0_.refs_1_), custom_call_target="tpu_custom_call" | custom-call | flops 1073741824 | bytes 4194304 | tf_op jit(solution)/shard_map/experts_mixed/pallas_call | solution.py:652
  64.8 6.2 %experts_far.1 = (bf16[512,2048]{1,0:T(8,128)(2,1)S(1)}, bf16[512,1024]{1,0:T(8,128)(2,1)S(1)}) custom-call(s32[3]{0:T(128)S(1)} %copy-done.18, bf16[128,1024]{1,0:T(8,128)(2,1)S(1)} %collective-permute-done.16.refs_0_.refs_1_.refs_4_, bf16[128,1024]{1,0:T(8,128)(2,1)S(1)} %collective-permute-done.17.refs_1_.refs_2_.refs_5_, ...), custom_call_target="tpu_custom_call" | custom-call | flops 3221225472 | bytes 9437184 | tf_op jit(solution)/shard_map/experts_far/pallas_call | solution.py:570
  71.1 2.2 %collective-permute-done.20.refs_3_ = bf16[128,1152]{1,0:T(8,128)(2,1)S(1)} collective-permute-done((bf16[128,1152]{1,0:T(8,128)(2,1)S(1)}, bf16[128,1152]{1,0:T(8,128)(2,1)S(1)}, u32[]{:S(2)}, u32[]{:S(2)}) %collective-permute-start.20) | collective-permute-done | bytes 294944 | tf_op jit(solution)/shard_map/ppermute | solution.py:60
  75.3 2.4 %collective-permute-start.25 = (bf16[32,1152]{1,0:T(8,128)(2,1)S(1)}, bf16[32,1152]{1,0:T(8,128)(2,1)S(1)}, u32[]{:S(2)}, u32[]{:S(2)}) collective-permute-start(bf16[32,1152]{1,0:T(8,128)(2,1)S(1)} %get-tuple-element.85), channel_id=1, source_target_pairs={{0,2},{1,3},{2,0},{3,1},{4,6},{5,7},{6,4},{7,5},{8,10},{9,11},{10,... | collective-permute-start | bytes 221192 | tf_op jit(solution)/shard_map/ppermute | solution.py:60
  79.1 4.5 %experts_weight_grads.2.refs_13_ = f32[8,512,128]{2,1,0:T(8,128)} custom-call(s32[3]{0:T(128)S(1)} %copy-done.18, bf16[128,1152]{1,0:T(8,128)(2,1)S(1)} %get-tuple-element.74.refs_5_.refs_0_, bf16[128,1152]{1,0:T(8,128)(2,1)S(1)} %collective-permute-done.8.refs_5_.refs_6_.refs_1_, bf16[128,1152]{1,0:T(8,128)(2,1)S(1)} %collective-permute-done.12.refs_7_.refs_2_, ...), custom_call_target="tpu_custom_call" | custom-call | flops 1073741824 | bytes 4194304 | tf_op jit(solution)/shard_map/experts_weight_grads/pallas_call | solution.py:705
  86.8 2.8 %collective-permute-start.28 = (bf16[32,2176]{1,0:T(8,128)(2,1)S(1)}, bf16[32,2176]{1,0:T(8,128)(2,1)S(1)}, u32[]{:S(2)}, u32[]{:S(2)}) collective-permute-start(bf16[32,2176]{1,0:T(8,128)(2,1)S(1)} %get-tuple-element.96), channel_id=1, source_target_pairs={{0,2},{1,3},{2,0},{3,1},{4,6},{5,7},{6,4},{7,5},{8,10},{9,11},{10,... | collective-permute-start | bytes 417800 | tf_op jit(solution)/shard_map/ppermute | solution.py:60
  89.6 1.6 %collective-permute-start.29 = (bf16[32,2176]{1,0:T(8,128)(2,1)S(1)}, bf16[32,2176]{1,0:T(8,128)(2,1)S(1)}, u32[]{:S(2)}, u32[]{:S(2)}) collective-permute-start(bf16[32,2176]{1,0:T(8,128)(2,1)S(1)} %get-tuple-element.97), channel_id=1, source_target_pairs={{0,3},{1,2},{2,1},{3,0},{4,7},{5,6},{6,5},{7,4},{8,11},{9,10},{10,... | collective-permute-start | bytes 417800 | tf_op jit(solution)/shard_map/ppermute | solution.py:60
  91.3 5.5 %experts_weight_grads.3 = (f32[8,512,128]{2,1,0:T(8,128)}, f32[8,512,128]{2,1,0:T(8,128)}) custom-call(s32[3]{0:T(128)S(1)} %copy-done.18, bf16[128,1024]{1,0:T(8,128)(2,1)S(1)} %place_second.1.refs_1_.refs_0_.refs_4_, bf16[128,1024]{1,0:T(8,128)(2,1)S(1)} %collective-permute-done.9.refs_2_.refs_1_, ...), custom_call_target="tpu_custom_call" | custom-call | flops 2147483648 | bytes 6291456 | tf_op jit(solution)/shard_map/experts_weight_grads/pallas_call | solution.py:705
  96.8 2.1 %collective-permute-done.28.refs_16_ = bf16[32,2176]{1,0:T(8,128)(2,1)S(1)} collective-permute-done((bf16[32,2176]{1,0:T(8,128)(2,1)S(1)}, bf16[32,2176]{1,0:T(8,128)(2,1)S(1)}, u32[]{:S(2)}, u32[]{:S(2)}) %collective-permute-start.28) | collective-permute-done | bytes 139296 | tf_op jit(solution)/shard_map/ppermute | solution.py:60
  100.6 3.2 %attend_grad.1 = (bf16[512,896]{1,0:T(8,128)(2,1)S(1)}, bf16[512,896]{1,0:T(8,128)(2,1)S(1)}, bf16[32,1024]{1,0:T(8,128)(2,1)S(1)}, f32[32,1024]{1,0:T(8,128)S(1...) custom-call(s32[3]{0:T(128)S(1)} %copy-done.18, ...), custom_call_target="tpu_custom_call" | custom-call | flops 402653184 | bytes 6160396 | tf_op jit(solution)/shard_map/attend_grad/pallas_call | solution.py:121
  103.9 2.5 %collective-permute-done.33.refs_1_ = bf16[512,896]{1,0:T(8,128)(2,1)S(1)} collective-permute-done((bf16[512,896]{1,0:T(8,128)(2,1)S(1)}, bf16[512,896]{1,0:T(8,128)(2,1)S(1)}, u32[]{:S(2)}, u32[]{:S(2)}) %collective-permute-start.33) | collective-permute-done | bytes 917536 | tf_op jit(solution)/shard_map/ppermute | solution.py:60
  110.1 2.1 %collective-permute-start.30 = (bf16[32,2048]{1,0:T(8,128)(2,1)S(1)}, bf16[32,2048]{1,0:T(8,128)(2,1)S(1)}, u32[]{:S(2)}, u32[]{:S(2)}) collective-permute-start(bf16[32,2048]{1,0:T(8,128)(2,1)S(1)} %get-tuple-element.102), channel_id=1, source_target_pairs={{0,1},{1,0},{2,3},{3,2},{4,5},{5,4},{6,7},{7,6},{8,9},{9,8},{10,11... | collective-permute-start | bytes 393224 | tf_op jit(solution)/shard_map/ppermute | solution.py:60
  113.0 2.1 %collective-permute-done.34.refs_1_ = bf16[128,896]{1,0:T(8,128)(2,1)S(1)} collective-permute-done((bf16[128,896]{1,0:T(8,128)(2,1)S(1)}, bf16[128,896]{1,0:T(8,128)(2,1)S(1)}, u32[]{:S(2)}, u32[]{:S(2)}) %collective-permute-start.34) | collective-permute-done | bytes 229408 | tf_op jit(solution)/shard_map/ppermute | solution.py:66
  115.1 2.3 %collective-permute-start.32 = (bf16[32,2048]{1,0:T(8,128)(2,1)S(1)}, bf16[32,2048]{1,0:T(8,128)(2,1)S(1)}, u32[]{:S(2)}, u32[]{:S(2)}) collective-permute-start(bf16[32,2048]{1,0:T(8,128)(2,1)S(1)} %get-tuple-element.104), channel_id=1, source_target_pairs={{0,3},{1,2},{2,1},{3,0},{4,7},{5,6},{6,5},{7,4},{8,11},{9,10},{10,... | collective-permute-start | bytes 393224 | tf_op jit(solution)/shard_map/ppermute | solution.py:60
  117.4 3.0 %collective-permute-done.35.refs_2_ = bf16[128,896]{1,0:T(8,128)(2,1)S(1)} collective-permute-done((bf16[128,896]{1,0:T(8,128)(2,1)S(1)}, bf16[128,896]{1,0:T(8,128)(2,1)S(1)}, u32[]{:S(2)}, u32[]{:S(2)}) %collective-permute-start.35) | collective-permute-done | bytes 229408 | tf_op jit(solution)/shard_map/ppermute | solution.py:66
  121.2 2.9 %collective-permute-done.31.refs_7_.refs_3_ = bf16[32,2048]{1,0:T(8,128)(2,1)S(1)} collective-permute-done((bf16[32,2048]{1,0:T(8,128)(2,1)S(1)}, bf16[32,2048]{1,0:T(8,128)(2,1)S(1)}, u32[]{:S(2)}, u32[]{:S(2)}) %collective-permute-start.31) | collective-permute-done | bytes 131104 | tf_op jit(solution)/shard_map/ppermute | solution.py:60
  124.9 2.4 %collective-permute-start.37 = (bf16[32,1152]{1,0:T(8,128)(2,1)S(1)}, bf16[32,1152]{1,0:T(8,128)(2,1)S(1)}, u32[]{:S(2)}, u32[]{:S(2)}) collective-permute-start(bf16[32,1152]{1,0:T(8,128)(2,1)S(1)} %input_grad.1.refs_5_), channel_id=1, source_target_pairs={{0,1},{1,0},{2,3},{3,2},{4,5},{5,4},{6,7},{7,6},{8,9},{9,8},{10,11... | collective-permute-start | bytes 221192 | tf_op jit(solution)/shard_map/ppermute | solution.py:60
  129.8 5.4 %collective-permute-done.38.refs_7_ = bf16[32,1152]{1,0:T(8,128)(2,1)S(1)} collective-permute-done((bf16[32,1152]{1,0:T(8,128)(2,1)S(1)}, bf16[32,1152]{1,0:T(8,128)(2,1)S(1)}, u32[]{:S(2)}, u32[]{:S(2)}) %collective-permute-start.38) | collective-permute-done | bytes 73760 | tf_op jit(solution)/shard_map/ppermute | solution.py:60
  (119 shorter events, 38.2 us)
Async XLA Ops:
  2.8 21.8 %collective-permute-start.3 = (bf16[128,1152]{1,0:T(8,128)(2,1)}, bf16[128,1152]{1,0:T(8,128)(2,1)S(1)}, u32[]{:S(2)}, u32[]{:S(2)}) collective-permute-start(bf16[128,1152]{1,0:T(8,128)(2,1)} %routes.1.refs_1_.refs_3_), channel_id=1, source_target_pairs={{0,16},{16,0},{1,17},{17,1},{2,18},{18,2},{3,19},{19,3},{4,20},{20... | collective-permute-start | bytes 884744 | tf_op jit(solution)/shard_map/ppermute | solution.py:60
  5.8 18.9 %collective-permute-start.4 = (bf16[128,1152]{1,0:T(8,128)(2,1)}, bf16[128,1152]{1,0:T(8,128)(2,1)S(1)}, u32[]{:S(2)}, u32[]{:S(2)}) collective-permute-start(bf16[128,1152]{1,0:T(8,128)(2,1)} %routes.1.refs_1_.refs_3_), channel_id=1, source_target_pairs={{0,24},{4,28},{8,16},{12,20},{16,8},{20,12},{24,0},{28,4},{1,25},{... | collective-permute-start | bytes 884744 | tf_op jit(solution)/shard_map/ppermute | solution.py:66
  15.7 6.9 %collective-permute-start.1 = (bf16[32,1024]{1,0:T(8,128)(2,1)}, bf16[32,1024]{1,0:T(8,128)(2,1)S(1)}, u32[]{:S(2)}, u32[]{:S(2)}) collective-permute-start(bf16[32,1024]{1,0:T(8,128)(2,1)} %get-tuple-element.70), channel_id=1, source_target_pairs={{0,2},{1,3},{2,0},{3,1},{4,6},{5,7},{6,4},{7,5},{8,10},{9,11},{10,... | collective-permute-start | bytes 196616 | tf_op jit(solution)/shard_map/ppermute | solution.py:60
  18.3 6.3 %collective-permute-start.2 = (bf16[32,1024]{1,0:T(8,128)(2,1)}, bf16[32,1024]{1,0:T(8,128)(2,1)S(1)}, u32[]{:S(2)}, u32[]{:S(2)}) collective-permute-start(bf16[32,1024]{1,0:T(8,128)(2,1)} %get-tuple-element.71), channel_id=1, source_target_pairs={{0,3},{1,2},{2,1},{3,0},{4,7},{5,6},{6,5},{7,4},{8,11},{9,10},{10,... | collective-permute-start | bytes 196616 | tf_op jit(solution)/shard_map/ppermute | solution.py:60
  26.4 8.5 %collective-permute-start.8 = (bf16[128,1152]{1,0:T(8,128)(2,1)S(1)}, bf16[128,1152]{1,0:T(8,128)(2,1)S(1)}, u32[]{:S(2)}, u32[]{:S(2)}) collective-permute-start(bf16[128,1152]{1,0:T(8,128)(2,1)S(1)} %get-tuple-element.74.refs_5_.refs_0_), channel_id=1, source_target_pairs={{0,8},{4,12},{8,0},{12,4},{1,9},{5,13},{9,1},{13,5},{2,10},{6,14},... | collective-permute-start | bytes 884744 | tf_op jit(solution)/shard_map/ppermute | solution.py:60
  26.9 5.7 %collective-permute-start.5 = (bf16[32,1024]{1,0:T(8,128)(2,1)S(1)}, bf16[32,1024]{1,0:T(8,128)(2,1)S(1)}, u32[]{:S(2)}, u32[]{:S(2)}) collective-permute-start(bf16[32,1024]{1,0:T(8,128)(2,1)S(1)} %get-tuple-element.73.refs_1_.refs_2_), channel_id=1, source_target_pairs={{0,1},{1,0},{2,3},{3,2},{4,5},{5,4},{6,7},{7,6},{8,9},{9,8},{10,11... | collective-permute-start | bytes 196616 | tf_op jit(solution)/shard_map/ppermute | solution.py:60
  26.9 5.7 %collective-permute-start.6 = (bf16[32,1024]{1,0:T(8,128)(2,1)S(1)}, bf16[32,1024]{1,0:T(8,128)(2,1)S(1)}, u32[]{:S(2)}, u32[]{:S(2)}) collective-permute-start(bf16[32,1024]{1,0:T(8,128)(2,1)S(1)} %get-tuple-element.73.refs_1_.refs_2_), channel_id=1, source_target_pairs={{0,2},{1,3},{2,0},{3,1},{4,6},{5,7},{6,4},{7,5},{8,10},{9,11},{10,... | collective-permute-start | bytes 196616 | tf_op jit(solution)/shard_map/ppermute | solution.py:60
  28.7 6.2 %collective-permute-start.7 = (bf16[32,1024]{1,0:T(8,128)(2,1)S(1)}, bf16[32,1024]{1,0:T(8,128)(2,1)S(1)}, u32[]{:S(2)}, u32[]{:S(2)}) collective-permute-start(bf16[32,1024]{1,0:T(8,128)(2,1)S(1)} %get-tuple-element.73.refs_1_.refs_2_), channel_id=1, source_target_pairs={{0,3},{1,2},{2,1},{3,0},{4,7},{5,6},{6,5},{7,4},{8,11},{9,10},{10,... | collective-permute-start | bytes 196616 | tf_op jit(solution)/shard_map/ppermute | solution.py:60
  31.3 6.3 %collective-permute-start.12 = (bf16[128,1152]{1,0:T(8,128)(2,1)S(1)}, bf16[128,1152]{1,0:T(8,128)(2,1)S(1)}, u32[]{:S(2)}, u32[]{:S(2)}) collective-permute-start(bf16[128,1152]{1,0:T(8,128)(2,1)S(1)} %get-tuple-element.74.refs_5_.refs_0_), channel_id=1, source_target_pairs={{0,4},{4,0},{8,12},{12,8},{1,5},{5,1},{9,13},{13,9},{2,6},{6,2},{1... | collective-permute-start | bytes 884744 | tf_op jit(solution)/shard_map/ppermute | solution.py:60
  35.5 6.4 %collective-permute-start.9 = (bf16[128,1024]{1,0:T(8,128)(2,1)S(1)}, bf16[128,1024]{1,0:T(8,128)(2,1)S(1)}, u32[]{:S(2)}, u32[]{:S(2)}) collective-permute-start(bf16[128,1024]{1,0:T(8,128)(2,1)S(1)} %place_second.1.refs_1_.refs_0_.refs_4_), channel_id=1, source_target_pairs={{0,8},{4,12},{8,0},{12,4},{1,9},{5,13},{9,1},{13,5},{2,10},{6,14},... | collective-permute-start | bytes 786440 | tf_op jit(solution)/shard_map/ppermute | solution.py:60
  37.1 6.4 %collective-permute-start.15 = (bf16[128,1152]{1,0:T(8,128)(2,1)S(1)}, bf16[128,1152]{1,0:T(8,128)(2,1)S(1)}, u32[]{:S(2)}, u32[]{:S(2)}) collective-permute-start(bf16[128,1152]{1,0:T(8,128)(2,1)S(1)} %collective-permute-done.4.refs_7_.refs_6_.refs_5_), channel_id=1, source_target_pairs={{0,4},{4,0},{8,12},{12,8},{1,5},{5,1},{9,13},{13,9},{2,6},{6,2},{1... | collective-permute-start | bytes 884744 | tf_op jit(solution)/shard_map/ppermute | solution.py:60
  37.6 7.3 %collective-permute-start.13 = (bf16[128,1152]{1,0:T(8,128)(2,1)S(1)}, bf16[128,1152]{1,0:T(8,128)(2,1)S(1)}, u32[]{:S(2)}, u32[]{:S(2)}) collective-permute-start(bf16[128,1152]{1,0:T(8,128)(2,1)S(1)} %collective-permute-done.8.refs_5_.refs_6_.refs_1_), channel_id=1, source_target_pairs={{0,4},{4,0},{8,12},{12,8},{1,5},{5,1},{9,13},{13,9},{2,6},{6,2},{1... | collective-permute-start | bytes 884744 | tf_op jit(solution)/shard_map/ppermute | solution.py:60
  37.6 7.3 %collective-permute-start.10 = (bf16[128,1024]{1,0:T(8,128)(2,1)S(1)}, bf16[128,1024]{1,0:T(8,128)(2,1)S(1)}, u32[]{:S(2)}, u32[]{:S(2)}) collective-permute-start(bf16[128,1024]{1,0:T(8,128)(2,1)S(1)} %place_second.1.refs_1_.refs_0_.refs_4_), channel_id=1, source_target_pairs={{0,4},{4,0},{8,12},{12,8},{1,5},{5,1},{9,13},{13,9},{2,6},{6,2},{1... | collective-permute-start | bytes 786440 | tf_op jit(solution)/shard_map/ppermute | solution.py:60
  41.9 13.0 %collective-permute-start.16 = (bf16[128,1024]{1,0:T(8,128)(2,1)S(1)}, bf16[128,1024]{1,0:T(8,128)(2,1)S(1)}, u32[]{:S(2)}, u32[]{:S(2)}) collective-permute-start(bf16[128,1024]{1,0:T(8,128)(2,1)S(1)} %place_second.1.refs_1_.refs_0_.refs_4_), channel_id=1, source_target_pairs={{0,16},{16,0},{1,17},{17,1},{2,18},{18,2},{3,19},{19,3},{4,20},{20... | collective-permute-start | bytes 786440 | tf_op jit(solution)/shard_map/ppermute | solution.py:60
  43.4 13.8 %collective-permute-start.17 = (bf16[128,1024]{1,0:T(8,128)(2,1)S(1)}, bf16[128,1024]{1,0:T(8,128)(2,1)S(1)}, u32[]{:S(2)}, u32[]{:S(2)}) collective-permute-start(bf16[128,1024]{1,0:T(8,128)(2,1)S(1)} %place_second.1.refs_1_.refs_0_.refs_4_), channel_id=1, source_target_pairs={{0,24},{4,28},{8,16},{12,20},{16,8},{20,12},{24,0},{28,4},{1,25},{... | collective-permute-start | bytes 786440 | tf_op jit(solution)/shard_map/ppermute | solution.py:66
  63.7 10.4 %collective-permute-start.18 = (bf16[256,1024]{1,0:T(8,128)(2,1)S(1)}, bf16[256,1024]{1,0:T(8,128)(2,1)S(1)}, u32[]{:S(2)}, u32[]{:S(2)}) collective-permute-start(bf16[256,1024]{1,0:T(8,128)(2,1)S(1)} %get-tuple-element.80), channel_id=1, source_target_pairs={{0,4},{4,0},{8,12},{12,8},{1,5},{5,1},{9,13},{13,9},{2,6},{6,2},{1... | collective-permute-start | bytes 1572872 | tf_op jit(solution)/shard_map/ppermute | solution.py:60
  64.2 9.1 %collective-permute-start.20 = (bf16[128,1152]{1,0:T(8,128)(2,1)S(1)}, bf16[128,1152]{1,0:T(8,128)(2,1)S(1)}, u32[]{:S(2)}, u32[]{:S(2)}) collective-permute-start(bf16[128,1152]{1,0:T(8,128)(2,1)S(1)} %add_convert_fusion), channel_id=1, source_target_pairs={{0,8},{4,12},{8,0},{12,4},{1,9},{5,13},{9,1},{13,5},{2,10},{6,14},... | collective-permute-start | bytes 884744 | tf_op jit(solution)/shard_map/ppermute | solution.py:60
  74.1 9.8 %collective-permute-start.23 = (bf16[128,1024]{1,0:T(8,128)(2,1)S(1)}, bf16[128,1024]{1,0:T(8,128)(2,1)S(1)}, u32[]{:S(2)}, u32[]{:S(2)}) collective-permute-start(bf16[128,1024]{1,0:T(8,128)(2,1)S(1)} %half.1), channel_id=1, source_target_pairs={{0,8},{4,12},{8,0},{12,4},{1,9},{5,13},{9,1},{13,5},{2,10},{6,14},... | collective-permute-start | bytes 786440 | tf_op jit(solution)/shard_map/ppermute | solution.py:60
  74.7 8.9 %collective-permute-start.24 = (bf16[32,1152]{1,0:T(8,128)(2,1)S(1)}, bf16[32,1152]{1,0:T(8,128)(2,1)S(1)}, u32[]{:S(2)}, u32[]{:S(2)}) collective-permute-start(bf16[32,1152]{1,0:T(8,128)(2,1)S(1)} %get-tuple-element.84), channel_id=1, source_target_pairs={{0,1},{1,0},{2,3},{3,2},{4,5},{5,4},{6,7},{7,6},{8,9},{9,8},{10,11... | collective-permute-start | bytes 221192 | tf_op jit(solution)/shard_map/ppermute | solution.py:60
  75.3 8.3 %collective-permute-start.25 = (bf16[32,1152]{1,0:T(8,128)(2,1)S(1)}, bf16[32,1152]{1,0:T(8,128)(2,1)S(1)}, u32[]{:S(2)}, u32[]{:S(2)}) collective-permute-start(bf16[32,1152]{1,0:T(8,128)(2,1)S(1)} %get-tuple-element.85), channel_id=1, source_target_pairs={{0,2},{1,3},{2,0},{3,1},{4,6},{5,7},{6,4},{7,5},{8,10},{9,11},{10,... | collective-permute-start | bytes 221192 | tf_op jit(solution)/shard_map/ppermute | solution.py:60
  77.7 6.2 %collective-permute-start.26 = (bf16[32,1152]{1,0:T(8,128)(2,1)S(1)}, bf16[32,1152]{1,0:T(8,128)(2,1)S(1)}, u32[]{:S(2)}, u32[]{:S(2)}) collective-permute-start(bf16[32,1152]{1,0:T(8,128)(2,1)S(1)} %get-tuple-element.86), channel_id=1, source_target_pairs={{0,3},{1,2},{2,1},{3,0},{4,7},{5,6},{6,5},{7,4},{8,11},{9,10},{10,... | collective-permute-start | bytes 221192 | tf_op jit(solution)/shard_map/ppermute | solution.py:60
  86.8 10.0 %collective-permute-start.27 = (bf16[32,2176]{1,0:T(8,128)(2,1)S(1)}, bf16[32,2176]{1,0:T(8,128)(2,1)S(1)}, u32[]{:S(2)}, u32[]{:S(2)}) collective-permute-start(bf16[32,2176]{1,0:T(8,128)(2,1)S(1)} %get-tuple-element.95), channel_id=1, source_target_pairs={{0,1},{1,0},{2,3},{3,2},{4,5},{5,4},{6,7},{7,6},{8,9},{9,8},{10,11... | collective-permute-start | bytes 417800 | tf_op jit(solution)/shard_map/ppermute | solution.py:60
  86.8 12.1 %collective-permute-start.28 = (bf16[32,2176]{1,0:T(8,128)(2,1)S(1)}, bf16[32,2176]{1,0:T(8,128)(2,1)S(1)}, u32[]{:S(2)}, u32[]{:S(2)}) collective-permute-start(bf16[32,2176]{1,0:T(8,128)(2,1)S(1)} %get-tuple-element.96), channel_id=1, source_target_pairs={{0,2},{1,3},{2,0},{3,1},{4,6},{5,7},{6,4},{7,5},{8,10},{9,11},{10,... | collective-permute-start | bytes 417800 | tf_op jit(solution)/shard_map/ppermute | solution.py:60
  89.6 9.3 %collective-permute-start.29 = (bf16[32,2176]{1,0:T(8,128)(2,1)S(1)}, bf16[32,2176]{1,0:T(8,128)(2,1)S(1)}, u32[]{:S(2)}, u32[]{:S(2)}) collective-permute-start(bf16[32,2176]{1,0:T(8,128)(2,1)S(1)} %get-tuple-element.97), channel_id=1, source_target_pairs={{0,3},{1,2},{2,1},{3,0},{4,7},{5,6},{6,5},{7,4},{8,11},{9,10},{10,... | collective-permute-start | bytes 417800 | tf_op jit(solution)/shard_map/ppermute | solution.py:60
  106.5 8.5 %collective-permute-start.34 = (bf16[128,896]{1,0:T(8,128)(2,1)S(1)}, bf16[128,896]{1,0:T(8,128)(2,1)S(1)}, u32[]{:S(2)}, u32[]{:S(2)}) collective-permute-start(bf16[128,896]{1,0:T(8,128)(2,1)S(1)} %get-tuple-element.109), channel_id=1, source_target_pairs={{0,16},{4,20},{8,24},{12,28},{16,0},{20,4},{24,8},{28,12},{1,17},{... | collective-permute-start | bytes 688136 | tf_op jit(solution)/shard_map/ppermute | solution.py:66
  108.1 12.3 %collective-permute-start.35 = (bf16[128,896]{1,0:T(8,128)(2,1)S(1)}, bf16[128,896]{1,0:T(8,128)(2,1)S(1)}, u32[]{:S(2)}, u32[]{:S(2)}) collective-permute-start(bf16[128,896]{1,0:T(8,128)(2,1)S(1)} %get-tuple-element.110), channel_id=1, source_target_pairs={{0,8},{4,12},{8,0},{12,4},{16,24},{20,28},{24,16},{28,20},{1,9},{5... | collective-permute-start | bytes 688136 | tf_op jit(solution)/shard_map/ppermute | solution.py:66
  109.6 10.8 %collective-permute-start.36 = (bf16[128,896]{1,0:T(8,128)(2,1)S(1)}, bf16[128,896]{1,0:T(8,128)(2,1)S(1)}, u32[]{:S(2)}, u32[]{:S(2)}) collective-permute-start(bf16[128,896]{1,0:T(8,128)(2,1)S(1)} %get-tuple-element.111), channel_id=1, source_target_pairs={{0,24},{4,28},{8,16},{12,20},{16,8},{20,12},{24,0},{28,4},{1,25},{... | collective-permute-start | bytes 688136 | tf_op jit(solution)/shard_map/ppermute | solution.py:66
  110.1 11.1 %collective-permute-start.30 = (bf16[32,2048]{1,0:T(8,128)(2,1)S(1)}, bf16[32,2048]{1,0:T(8,128)(2,1)S(1)}, u32[]{:S(2)}, u32[]{:S(2)}) collective-permute-start(bf16[32,2048]{1,0:T(8,128)(2,1)S(1)} %get-tuple-element.102), channel_id=1, source_target_pairs={{0,1},{1,0},{2,3},{3,2},{4,5},{5,4},{6,7},{7,6},{8,9},{9,8},{10,11... | collective-permute-start | bytes 393224 | tf_op jit(solution)/shard_map/ppermute | solution.py:60
  112.2 12.0 %collective-permute-start.31 = (bf16[32,2048]{1,0:T(8,128)(2,1)S(1)}, bf16[32,2048]{1,0:T(8,128)(2,1)S(1)}, u32[]{:S(2)}, u32[]{:S(2)}) collective-permute-start(bf16[32,2048]{1,0:T(8,128)(2,1)S(1)} %get-tuple-element.103), channel_id=1, source_target_pairs={{0,2},{1,3},{2,0},{3,1},{4,6},{5,7},{6,4},{7,5},{8,10},{9,11},{10,... | collective-permute-start | bytes 393224 | tf_op jit(solution)/shard_map/ppermute | solution.py:60
  115.1 9.1 %collective-permute-start.32 = (bf16[32,2048]{1,0:T(8,128)(2,1)S(1)}, bf16[32,2048]{1,0:T(8,128)(2,1)S(1)}, u32[]{:S(2)}, u32[]{:S(2)}) collective-permute-start(bf16[32,2048]{1,0:T(8,128)(2,1)S(1)} %get-tuple-element.104), channel_id=1, source_target_pairs={{0,3},{1,2},{2,1},{3,0},{4,7},{5,6},{6,5},{7,4},{8,11},{9,10},{10,... | collective-permute-start | bytes 393224 | tf_op jit(solution)/shard_map/ppermute | solution.py:60
  127.3 7.8 %collective-permute-start.38 = (bf16[32,1152]{1,0:T(8,128)(2,1)S(1)}, bf16[32,1152]{1,0:T(8,128)(2,1)S(1)}, u32[]{:S(2)}, u32[]{:S(2)}) collective-permute-start(bf16[32,1152]{1,0:T(8,128)(2,1)S(1)} %input_grad.1.refs_5_), channel_id=1, source_target_pairs={{0,2},{1,3},{2,0},{3,1},{4,6},{5,7},{6,4},{7,5},{8,10},{9,11},{10,... | collective-permute-start | bytes 221192 | tf_op jit(solution)/shard_map/ppermute | solution.py:60
  128.2 7.0 %collective-permute-start.39 = (bf16[32,1152]{1,0:T(8,128)(2,1)S(1)}, bf16[32,1152]{1,0:T(8,128)(2,1)S(1)}, u32[]{:S(2)}, u32[]{:S(2)}) collective-permute-start(bf16[32,1152]{1,0:T(8,128)(2,1)S(1)} %input_grad.1.refs_5_), channel_id=1, source_target_pairs={{0,3},{1,2},{2,1},{3,0},{4,7},{5,6},{6,5},{7,4},{8,11},{9,10},{10,... | collective-permute-start | bytes 221192 | tf_op jit(solution)/shard_map/ppermute | solution.py:60
  (32 other events, 271.8 us)

commit v4 on v3

--- a/solution.py
+++ b/solution.py
@@ -105,8 +105,10 @@
     return pl.ds(pl.multiple_of(index * rows, rows), rows)
 
 
-def plain_call(kernel, name, out_shape, scratch, flops, *arrays, after=(), vmem=16):
-    def whole(a):
+def plain_call(kernel, name, out_shape, scratch, flops, *arrays, after=(), hbm=(), vmem=16):
+    def whole(a, far=False):
+        if far:
+            return pl.BlockSpec(memory_space=pltpu.HBM)
         if a.dtype == jnp.int32 and a.size <= 64:
             return pl.BlockSpec(memory_space=pltpu.SMEM)
         return pl.BlockSpec(a.shape, lambda i: (0,) * a.ndim)
@@ -121,7 +123,7 @@
     return pl.pallas_call(
         body,
         grid=(1,),
-        in_specs=[whole(a) for a in arrays[:count]] + [pl.BlockSpec(memory_space=pl.ANY)] * extra,
+        in_specs=[whole(a, i in hbm) for i, a in enumerate(arrays[:count])] + [pl.BlockSpec(memory_space=pl.ANY)] * extra,
         out_specs=[whole(a) for a in out_shape],
         out_shape=out_shape,
         scratch_shapes=scratch,
@@ -150,13 +152,27 @@
     return lax.rsqrt(jnp.mean(values * values, -1, keepdims=True) + EPSILON)
 
 
+def gain_row(ref):
+    values = ref[...].astype(F32)
+    return jnp.concatenate([values[i : i + 1, :] for i in range(values.shape[0])], 1)
+
+
 def attend_kernel(heads, group, *refs):
-    (meta, lengths, hidden, gain, query_w, key_w, value_w, output_w, cosine, sine) = refs[:10]
-    n1_ref, qkv_ref, prob_ref, att_ref, cos_ref, sin_ref = refs[10:16]
-    own_ref, *sent_refs = refs[16:-1]
-    part_scr = refs[-1]
+    (meta, lengths, gain, cosine, sine) = refs[:5]
+    far_refs, refs = refs[5:10], refs[10:]
+    n1_ref, qkv_ref, prob_ref, att_ref, cos_ref, sin_ref = refs[:6]
+    own_ref, *sent_refs = refs[6:-7]
+    part_scr, hidden, query_w, key_w, value_w, output_w, sems = refs[-7:]
+    near_refs = [hidden, query_w, key_w, value_w, output_w]
+    copies = [
+        pltpu.make_async_copy(far, near, sems.at[i])
+        for i, (far, near) in enumerate(zip(far_refs, near_refs))
+    ]
+    for copy in copies:
+        copy.start()
+    copies[0].wait()
     x = hidden[...].astype(F32)
-    n1 = (x * unit_rows(x) * gain[0:1, :]).astype(BF16)
+    n1 = (x * unit_rows(x) * gain_row(gain)).astype(BF16)
     n1_ref[...] = n1
     tokens = x.shape[0]
     rows = lax.broadcasted_iota(jnp.int32, (tokens, tokens), 0)
@@ -176,6 +192,8 @@
     allowed = (row_segment == column_segment) & (columns <= rows)
     q_width, kv_width = query_w.shape[1], key_w.shape[1]
     keys_at, values_at = q_width, q_width + kv_width
+    for copy in copies[1:4]:
+        copy.wait()
     qkv_ref[:, :q_width] = rotate(dot(n1, query_w[...], ((1,), (0,))), cos, sin).astype(BF16)
     qkv_ref[:, keys_at:values_at] = rotate(dot(n1, key_w[...], ((1,), (0,))), cos, sin).astype(BF16)
     qkv_ref[:, values_at:] = dot(n1, value_w[...], ((1,), (0,))).astype(BF16)
@@ -194,16 +212,17 @@
             prob.astype(BF16), qkv_ref[:, values_at + g * HD : values_at + (g + 1) * HD], ((1,), (0,))
         )
         att_ref[:, h * HD : (h + 1) * HD] = head_out.astype(BF16)
+    for copy in copies[4:]:
+        copy.wait()
     part_scr[...] = dot(att_ref[...], output_w[...], ((1,), (1,)))
     spread_blocks(meta[0], part_scr, own_ref, sent_refs)
     own_ref[...] += hidden[rows_at(meta[0], own_ref.shape[0]), :].astype(F32)
 
 
-def routes_kernel(routes, dy, out_ref):
-    width = dy.shape[1]
-    out_ref[:, :width] = dy[...]
+def fill_routes(routes, out_ref):
+    width = out_ref.shape[1] - EXTRA
     named = routes[...].astype(F32).T
-    lane = lax.broadcasted_iota(jnp.int32, (dy.shape[0], EXTRA), 1).astype(F32)
+    lane = lax.broadcasted_iota(jnp.int32, (out_ref.shape[0], EXTRA), 1).astype(F32)
     total = jnp.zeros(lane.shape, F32)
     for j in range(named.shape[1]):
         total += (named[:, j : j + 1] == lane).astype(F32)
@@ -212,19 +231,20 @@
 
 def second_norm_kernel(gain, grad, *refs):
     parts, (residual_ref, n2_ref, grad_ref) = refs[:-3], refs[-3:]
+    grad_ref[...] = grad[...]
     residual = parts[0][...]
     for part in parts[1:]:
         residual = residual + part[...].astype(F32)
     residual_ref[...] = residual
-    n2_ref[...] = (residual * unit_rows(residual) * gain[1:2, :]).astype(BF16)
-    grad_ref[...] = grad[...]
-
-
-def place_kernel(meta, *refs):
+    n2_ref[...] = (residual * unit_rows(residual) * gain_row(gain)).astype(BF16)
+
+
+def place_second_kernel(meta, routes, *refs):
     blocks, out_ref = refs[:-1], refs[-1]
-    rows = blocks[0].shape[0]
+    rows, width = blocks[0].shape
     for k, ref in enumerate(blocks):
-        out_ref[rows_at(meta[0] ^ k, rows), :] = ref[...].astype(out_ref.dtype)
+        out_ref[rows_at(meta[0] ^ k, rows), :width] = ref[...]
+    fill_routes(routes, out_ref)
 
 
 def halves_kernel(meta, near, got, last, *refs):
@@ -253,8 +273,8 @@
     arrival = parts[0][...]
     for part in parts[1:]:
         arrival = arrival + part[...].astype(F32)
-    logits = dot(n2_ref[...], router[...], ((1,), (1,)))
-    routed = dy_ref[mine, width : width + experts].astype(F32) > 0.5
+    logits = dot(n2_ref[mine, :width], router[...], ((1,), (1,)))
+    routed = n2_ref[mine, width : width + experts].astype(F32) > 0.5
     logits = jnp.where(routed, logits, -1e30)
     gates = jnp.exp(logits - jnp.max(logits, -1, keepdims=True))
     gates = gates / jnp.sum(gates, -1, keepdims=True)
@@ -273,8 +293,8 @@
     hat = residual * scale
     gain_row_ref[...] = jnp.zeros_like(gain_row_ref)
     gain_row_ref[0:1, :] = jnp.sum(dn2 * hat, 0, keepdims=True)
-    gained = dn2 * gain[1:2, :]
-    dh = dy_ref[mine, :width].astype(F32) + scale * (
+    gained = dn2 * gain_row(gain)
+    dh = dy_ref[mine, :].astype(F32) + scale * (
         gained - hat * jnp.mean(gained * hat, -1, keepdims=True)
     )
     dh_ref[...] = dh
@@ -338,7 +358,7 @@
     x = hidden[...].astype(F32)
     first_row = jnp.sum(dn1 * (x * unit_rows(x)), 0, keepdims=True)
     dlog_t = dh_scr[:, width:].astype(F32).T.astype(BF16)
-    router_t = dot(dlog_t, n2_ref[...], ((1,), (0,)))
+    router_t = dot(dlog_t, n2_ref[:, :width], ((1,), (0,)))
     router_t = router_t[:experts] + router_t[experts : 2 * experts]
     side = jnp.concatenate(
         [router_t, gain_row[0:1, :], first_row, jnp.zeros((EXTRA - experts - 2, width), F32)], 0
@@ -372,7 +392,7 @@
     x = hidden[rows_at(meta[0], block), :].astype(F32)
     scale = unit_rows(x)
     hat = x * scale
-    gained = dn1 * gain[0:1, :]
+    gained = dn1 * gain_row(gain)
     grad = dh_ref[...] + scale * (gained - hat * jnp.mean(gained * hat, -1, keepdims=True))
     out_ref[:, :width] = grad.astype(BF16)
     rows, columns = gains_ref.shape
@@ -473,7 +493,7 @@
         refs = refs[6:]
     gates_scr, x_ref, dy_ref = refs
     step = pl.program_id(1)
-    width = x_ref.shape[1]
+    width = dy_ref.shape[1]
     lanes = gates_scr.shape[1]
 
     @pl.when(step == 0)
@@ -482,8 +502,8 @@
         for n in range(parts):
             x_ref[n * part_rows : (n + 1) * part_rows, :] = x_parts[n][...]
             dy_ref[n * part_rows : (n + 1) * part_rows, :] = dy_parts[n][...]
-        logits = dot(x_ref[...], router_ref[...], ((1,), (1,)))
-        routed = dy_ref[:, width : width + experts].astype(F32) > 0.5
+        logits = dot(x_ref[:, :width], router_ref[...], ((1,), (1,)))
+        routed = x_ref[:, width : width + experts].astype(F32) > 0.5
         logits = jnp.where(routed, logits, -1e30)
         weights = jnp.exp(logits - jnp.max(logits, -1, keepdims=True))
         gates_scr[...] = jnp.zeros_like(gates_scr)
@@ -493,11 +513,11 @@
 
     first = meta_ref[1] * (pair * steps) + step * pair
     gates = pltpu.roll(gates_scr[...], lax.rem(lanes - first, lanes), 1)
-    raw_all = dot(dy_ref[:, :width], side_by_side(down_ref, 0, pair), ((1,), (0,)))
+    raw_all = dot(dy_ref[...], side_by_side(down_ref, 0, pair), ((1,), (0,)))
     units = gate_ref.shape[2]
     column = lax.broadcasted_iota(jnp.int32, gates.shape, 1)
     weight = jnp.concatenate([r[i] for i in range(pair) for r in (gate_ref, up_ref)], 1)
-    both_all = dot(x_ref[...], weight, ((1,), (0,)))
+    both_all = dot(x_ref[:, :width], weight, ((1,), (0,)))
     for i in range(pair):
         gate_proj = both_all[:, 2 * i * units : (2 * i + 1) * units]
         up_proj = both_all[:, (2 * i + 1) * units : (2 * i + 2) * units]
@@ -526,13 +546,13 @@
 
 
 def expert_call(own, meta, xs, dys, gate_weight, up_weight, down_weight, router_weight, after=()):
-    part_rows, width = xs[0].shape
+    part_rows, width = dys[0].shape
     parts = len(xs)
     tokens = part_rows * parts
     if tokens > 512:
         xs, dys, parts = [jnp.concatenate(xs, 0)], [jnp.concatenate(dys, 0)], 1
         part_rows = tokens
-    dy_width = dys[0].shape[1]
+    x_width = xs[0].shape[1]
     local, _, units = gate_weight.shape
     experts = router_weight.shape[0]
     pair = pair_of(local)
@@ -543,8 +563,8 @@
         in_specs=[
             pl.BlockSpec(memory_space=pltpu.SMEM),
         ]
+        + [pl.BlockSpec((rows // parts, x_width), lambda c, s: (c, 0))] * parts
         + [pl.BlockSpec((rows // parts, width), lambda c, s: (c, 0))] * parts
-        + [pl.BlockSpec((rows // parts, dy_width), lambda c, s: (c, 0))] * parts
         + [pl.BlockSpec((pair, width, units), lambda c, s: (s, 0, 0))] * 3
         + [pl.BlockSpec(router_weight.shape, lambda c, s: (0, 0))]
         + [pl.BlockSpec(memory_space=pl.ANY)] * len(after),
@@ -554,8 +574,8 @@
         ],
         scratch_shapes=[
             pltpu.VMEM((rows, 128), F32),
+            pltpu.VMEM((rows, x_width), BF16),
             pltpu.VMEM((rows, width), BF16),
-            pltpu.VMEM((rows, dy_width), BF16),
         ],
     )
     out_shape = [
@@ -672,7 +692,19 @@
 
 def weight_grad_kernel(sets, parts, outs, pair, units, place_ref, *refs):
     lefts, rights = refs[: sets * parts], refs[sets * parts : sets * parts + sets]
-    grad_refs, left_scr = refs[-1 - outs : -1], refs[-1]
+    grad_refs, token_ref = refs[-4 - outs : -4], refs[-4]
+    left_scr, out_scr, sems = refs[-3:]
+    token_ref[...] = jnp.zeros_like(token_ref)
+    step, steps = pl.program_id(0), pl.num_programs(0)
+    slot = lax.rem(step, 2)
+
+    def copies(at, which):
+        return [
+            pltpu.make_async_copy(
+                out_scr.at[which, j], grad_refs[j].at[pl.ds(at * pair, pair)], sems.at[which, j]
+            )
+            for j in range(outs)
+        ]
 
     @pl.when(pl.program_id(0) == 0)
     def _():
@@ -685,10 +717,28 @@
     for n in range(sets):
         part = dot(left_scr[:, n * rows : (n + 1) * rows], rights[n][...], ((1,), (0,)))
         total = part if total is None else total + part
+
+    @pl.when(step >= 2)
+    def _():
+        for copy in copies(step - 2, slot):
+            copy.wait()
+
     for i in range(pair):
         for j in range(outs):
             at = (i * outs + j) * units
-            grad_refs[j][i] = total[:, at : at + units]
+            out_scr[slot, j, i] = total[:, at : at + units]
+    for copy in copies(step, slot):
+        copy.start()
+
+    @pl.when(step == steps - 1)
+    def _():
+        for copy in copies(step, slot):
+            copy.wait()
+
+    @pl.when((step == steps - 1) & (step >= 1))
+    def _():
+        for copy in copies(step - 1, 1 - slot):
+            copy.wait()
 
 
 def weight_grad_call(meta, lefts, rights, local, units, after=()):
@@ -710,10 +760,15 @@
             in_specs=[columns] * (sets * parts)
             + [pl.BlockSpec((tokens, pair * outs * units), lambda s, meta: (0, s))] * sets
             + [pl.BlockSpec(memory_space=pl.ANY)] * len(after),
-            out_specs=[pl.BlockSpec((pair, width, units), lambda s, meta: (s, 0, 0))] * outs,
-            scratch_shapes=[pltpu.VMEM((width, sets * tokens), BF16)],
+            out_specs=[pl.BlockSpec(memory_space=pltpu.HBM)] * outs
+            + [pl.BlockSpec((8, 128), lambda s, meta: (0, 0))],
+            scratch_shapes=[
+                pltpu.VMEM((width, sets * tokens), BF16),
+                pltpu.VMEM((2, outs, pair, width, units), F32),
+                pltpu.SemaphoreType.DMA((2, outs)),
+            ],
         ),
-        out_shape=[jax.ShapeDtypeStruct((local, width, units), F32)] * outs,
+        out_shape=[array((local, width, units), F32)] * outs + [array((8, 128), F32)],
         compiler_params=kernel_params(tokens),
         cost_estimate=pl.CostEstimate(
             flops=2 * sets * tokens * width * outs * local * units,
@@ -774,22 +829,11 @@
     dp_n = lax.axis_size("dp")
     block = tokens_here // tensor_n
     meta = jnp.stack([lax.axis_index(a) for a in ("tensor", "expert", "dp")]).astype(jnp.int32)
-    gain_rows = jnp.stack([first_gain, second_gain]).astype(F32)
-
-    (grad_own,) = plain_call(
-        routes_kernel,
-        "routes",
-        [array((tokens_here, model_width + EXTRA), BF16)],
-        [],
-        tokens_here * model_width,
-        expert_routes.T,
-        grad_layer_out,
-        vmem=60,
-    )
+    first_tile, second_tile = first_gain.reshape(-1, 128), second_gain.reshape(-1, 128)
 
     cosine, sine = rope_tables(tokens_here)
     blocks = block_shapes(block, model_width, tensor_n)
-    n1, qkv, prob, att, cosine, sine, part, *sent = plain_call(
+    outs = plain_call(
         functools.partial(attend_kernel, heads, group),
         "attend",
         [
@@ -801,47 +845,58 @@
             array(sine.shape, F32),
         ]
         + blocks,
-        [pltpu.VMEM((tokens_here, model_width), F32)],
+        [
+            pltpu.VMEM((tokens_here, model_width), F32),
+            pltpu.VMEM(hidden_in.shape, BF16),
+            pltpu.VMEM(query_weight.shape, BF16),
+            pltpu.VMEM(key_weight.shape, BF16),
+            pltpu.VMEM(value_weight.shape, BF16),
+            pltpu.VMEM(output_weight.shape, BF16),
+            pltpu.SemaphoreType.DMA((5,)),
+        ],
         2 * tokens_here * model_width * 3 * q_width,
         meta,
         seq_lengths,
+        first_tile,
+        cosine,
+        sine,
         hidden_in,
-        gain_rows,
         query_weight,
         key_weight,
         value_weight,
         output_weight,
-        cosine,
-        sine,
+        hbm=range(5, 10),
         vmem=60,
     )
-    far_grads = [swap(grad_own, "dp", k) for k in range(1, dp_n)]
+    n1, qkv, prob, att, cosine, sine, part, *sent = outs
+    far_grads = [swap(grad_layer_out, "dp", k) for k in range(1, dp_n)]
     if expert_n == 4:
-        far_grads += [swap_plane(grad_own, k, 2) for k in range(1, dp_n)]
+        far_grads += [swap_plane(grad_layer_out, k, 2) for k in range(1, dp_n)]
     residual, second_block, grad_near = plain_call(
         second_norm_kernel,
         "second_norm",
         [
             array((block, model_width), F32),
             array((block, model_width), BF16),
-            array(grad_own.shape, BF16),
+            array(grad_layer_out.shape, BF16),
         ],
         [],
         8 * block * model_width,
-        gain_rows,
-        grad_own,
+        second_tile,
+        grad_layer_out,
         part,
         *swap_tensor(sent),
         after=far_grads,
     )
-    grad_sets = gather_sets(grad_own, grad_near)
+    grad_sets = gather_sets(grad_layer_out, grad_near)
     (second_group,) = plain_call(
-        place_kernel,
+        place_second_kernel,
         "place_second",
-        [array((tokens_here, model_width), BF16)],
+        [array((tokens_here, model_width + EXTRA), BF16)],
         [],
         tokens_here * model_width,
         meta,
+        expert_routes.T,
         *gather_tensor(second_block),
         after=grad_sets[0][1:2],
     )
@@ -849,7 +904,7 @@
 
     router_t = router_weight.T
     weights = (gate_weight, up_weight, down_weight, router_t)
-    far_grads = [g for x in grad_sets[1:] for g in x[2:]]
+    far_grads = [g for x in grad_sets[1:] for g in x[:2]]
     own = expert_call(True, meta, second_sets[0], grad_sets[0], *weights, after=far_grads)
     arrival = arrival_call(
         own[0], own[2], gate_weight, up_weight, after=[x for y in second_sets[1:] for x in y[:2]]
@@ -870,10 +925,10 @@
     )
     mixed = reduce_first(*mixed, after=arrival[:1])
     arrival = [arrival[0]] + swap_tensor(arrival[1:])
-    (grad_down,) = weight_grad_call(
+    grad_down, down_done = weight_grad_call(
         meta, grad_sets, [x[1] for x in sides], local_experts, units
     )
-    grad_gate, grad_upproj = weight_grad_call(
+    grad_gate, grad_upproj, gate_done = weight_grad_call(
         meta, second_sets, [x[0] for x in sides], local_experts, units
     )
 
@@ -891,13 +946,13 @@
         20 * block * model_width,
         meta,
         residual,
-        second_block,
-        grad_own,
+        second_group,
+        grad_layer_out,
         router_t,
-        gain_rows,
+        second_tile,
         *mixed,
         *arrival,
-        after=[grad_down],
+        after=[down_done],
     )
     places = expert_n * dp_n
     rows = model_width // places
@@ -937,7 +992,7 @@
         *swap_tensor(sent),
         mixed_own,
         residual,
-        after=[grad_gate],
+        after=[gate_done],
     )
 
     expert_bits = list(reversed(bits_of(expert_n)))
@@ -977,7 +1032,7 @@
         10 * block * model_width,
         meta,
         hidden_in,
-        gain_rows,
+        first_tile,
         grad_resid,
         gains,
         *dn1,

time: 137 us -> 134 us (0.978)
  local copies, waits for them, and re-layouts: 9.4 us -> 6.44 us
    unnamed x48 -> x50, local copies, waits for them, and re-layouts: 8.03 us -> 6.44 us
    another operation x2 -> x0, local copies, waits for them, and re-layouts: 1.37 us -> none  [on_device(): gain_rows = jnp.stack([first_gain, second_gain]).astype(F32)]
    pallas_call x12 -> x11, Pallas kernels: 15.6 us -> 14.5 us  [plain_call(): pl.pallas_call(body, grid=(1,), in_specs=[whole(a, i in hbm) for i, a in...]
  transfers between devices with their start and end apart: 40 -> 40, of which waited for: 15 -> 15; matrix products, arithmetic and copies ran while one was open for 2% -> 0% of each run, Pallas kernels for 23% -> 24%
where the time goes in v4:
time: 134 us; the launch traced here: 133 us
  starting transfers between devices  44.8 us (33%)
  Pallas kernels  43.7 us (33%)
  waiting for transfers between devices  36.6 us (27%)
  local copies, waits for them, and re-layouts  6.44 us (5%)
    ppermute x35, starting transfers between devices, swap(): return lax.ppermute(x, axis, [(i, i ^ k) for i in range(n)])  37.4 us
    ppermute x35, waiting for transfers between devices, swap(): return lax.ppermute(x, axis, [(i, i ^ k) for i in range(n)])  30 us
    pallas_call x11, Pallas kernels, plain_call(): pl.pallas_call(body, grid=(1,), in_specs=[whole(a, i in hbm) for i, a in...  14.5 us
    pallas_call x2, Pallas kernels, expert_call(): pl.pallas_call(functools.partial(expert_kernel, own, steps, pair, experts...  13.1 us
    pallas_call x2, Pallas kernels, weight_grad_call(): pl.pallas_call(functools.partial(weight_grad_kernel, sets, parts, outs, p...  10.2 us
    ppermute x5, starting transfers between devices, swap_plane(): lax.ppermute(x, ('dp', 'expert'), [(i, i ^ k_dp * n + k_expert) for i in...  7.44 us
    ppermute x5, waiting for transfers between devices, swap_plane(): lax.ppermute(x, ('dp', 'expert'), [(i, i ^ k_dp * n + k_expert) for i in...  6.54 us
    unnamed x50, local copies, waits for them, and re-layouts  6.44 us
  transfers between devices with their start and end apart: 40, of which 15 were waited for; matrix products, arithmetic and copies ran while one was open for 0% of the time, Pallas kernels for 24%

profile of v4, /device:TPU:0, one launch (start us, length us, event | category | flops | bytes accessed | tf_op | source)
XLA Modules:
  0.0 133.3 jit_solution(12350686232854419223)
XLA Ops:
  0.7 3.0 %collective-permute-start.3 = (bf16[128,1024]{1,0:T(8,128)(2,1)}, bf16[128,1024]{1,0:T(8,128)(2,1)S(1)}, u32[]{:S(2)}, u32[]{:S(2)}) collective-permute-start(bf16[128,1024]{1,0:T(8,128)(2,1)} %refs_3_.2), channel_id=1, source_target_pairs={{0,16},{16,0},{1,17},{17,1},{2,18},{18,2},{3,19},{19,3},{4,20},{20... | collective-permute-start | bytes 786440 | tf_op jit(solution)/shard_map/ppermute | solution.py:60
  5.8 4.9 %attend.1 = (bf16[128,1024]{1,0:T(8,128)(2,1)}, bf16[128,512]{1,0:T(8,128)(2,1)}, f32[4,128,128]{2,1,0:T(8,128)}, bf16[128,256]{1,0:T(8,128)(2,1)}, f32[128,128]...) custom-call(s32[3]{0:T(128)} %pad_add_fusion.refs_0_.place_ref, ...), custom_call_target="tpu_custom_call" | custom-call | flops 201326592 | bytes 3147800 | tf_op jit(solution)/shard_map/attend/pallas_call | solution.py:123
  10.6 1.6 %collective-permute-start = (bf16[32,1024]{1,0:T(8,128)(2,1)}, bf16[32,1024]{1,0:T(8,128)(2,1)S(1)}, u32[]{:S(2)}, u32[]{:S(2)}) collective-permute-start(bf16[32,1024]{1,0:T(8,128)(2,1)} %get-tuple-element.72), channel_id=1, source_target_pairs={{0,1},{1,0},{2,3},{3,2},{4,5},{5,4},{6,7},{7,6},{8,9},{9,8},{10,11... | collective-permute-start | bytes 196616 | tf_op jit(solution)/shard_map/ppermute | solution.py:60
  12.3 2.6 %collective-permute-start.1 = (bf16[32,1024]{1,0:T(8,128)(2,1)}, bf16[32,1024]{1,0:T(8,128)(2,1)S(1)}, u32[]{:S(2)}, u32[]{:S(2)}) collective-permute-start(bf16[32,1024]{1,0:T(8,128)(2,1)} %get-tuple-element.73), channel_id=1, source_target_pairs={{0,2},{1,3},{2,0},{3,1},{4,6},{5,7},{6,4},{7,5},{8,10},{9,11},{10,... | collective-permute-start | bytes 196616 | tf_op jit(solution)/shard_map/ppermute | solution.py:60
  15.8 3.4 %collective-permute-done.1.refs_4_ = bf16[32,1024]{1,0:T(8,128)(2,1)S(1)} collective-permute-done((bf16[32,1024]{1,0:T(8,128)(2,1)}, bf16[32,1024]{1,0:T(8,128)(2,1)S(1)}, u32[]{:S(2)}, u32[]{:S(2)}) %collective-permute-start.1) | collective-permute-done | bytes 65568 | tf_op jit(solution)/shard_map/ppermute | solution.py:60
  19.2 1.9 %collective-permute-done.2.refs_5_ = bf16[32,1024]{1,0:T(8,128)(2,1)S(1)} collective-permute-done((bf16[32,1024]{1,0:T(8,128)(2,1)}, bf16[32,1024]{1,0:T(8,128)(2,1)S(1)}, u32[]{:S(2)}, u32[]{:S(2)}) %collective-permute-start.2) | collective-permute-done | bytes 65568 | tf_op jit(solution)/shard_map/ppermute | solution.py:60
  23.5 1.8 %collective-permute-start.6 = (bf16[32,1024]{1,0:T(8,128)(2,1)S(1)}, bf16[32,1024]{1,0:T(8,128)(2,1)S(1)}, u32[]{:S(2)}, u32[]{:S(2)}) collective-permute-start(bf16[32,1024]{1,0:T(8,128)(2,1)S(1)} %get-tuple-element.76.refs_2_), channel_id=1, source_target_pairs={{0,2},{1,3},{2,0},{3,1},{4,6},{5,7},{6,4},{7,5},{8,10},{9,11},{10,... | collective-permute-start | bytes 196616 | tf_op jit(solution)/shard_map/ppermute | solution.py:60
  25.3 2.6 %collective-permute-start.7 = (bf16[32,1024]{1,0:T(8,128)(2,1)S(1)}, bf16[32,1024]{1,0:T(8,128)(2,1)S(1)}, u32[]{:S(2)}, u32[]{:S(2)}) collective-permute-start(bf16[32,1024]{1,0:T(8,128)(2,1)S(1)} %get-tuple-element.76.refs_2_), channel_id=1, source_target_pairs={{0,3},{1,2},{2,1},{3,0},{4,7},{5,6},{6,5},{7,4},{8,11},{9,10},{10,... | collective-permute-start | bytes 196616 | tf_op jit(solution)/shard_map/ppermute | solution.py:60
  29.0 2.4 %collective-permute-done.7.refs_5_ = bf16[32,1024]{1,0:T(8,128)(2,1)S(1)} collective-permute-done((bf16[32,1024]{1,0:T(8,128)(2,1)S(1)}, bf16[32,1024]{1,0:T(8,128)(2,1)S(1)}, u32[]{:S(2)}, u32[]{:S(2)}) %collective-permute-start.7) | collective-permute-done | bytes 65568 | tf_op jit(solution)/shard_map/ppermute | solution.py:60
  32.3 1.6 %collective-permute-start.9 = (bf16[128,1152]{1,0:T(8,128)(2,1)S(1)}, bf16[128,1152]{1,0:T(8,128)(2,1)S(1)}, u32[]{:S(2)}, u32[]{:S(2)}) collective-permute-start(bf16[128,1152]{1,0:T(8,128)(2,1)S(1)} %place_second.1.refs_1_.refs_2_.refs_0_.refs_4_), channel_id=1, source_target_pairs={{0,8},{4,12},{8,0},{12,4},{1,9},{5,13},{9,1},{13,5},{2,10},{6,14},... | collective-permute-start | bytes 884744 | tf_op jit(solution)/shard_map/ppermute | solution.py:60
  33.9 5.2 %collective-permute-done.9.refs_2_.refs_1_ = bf16[128,1152]{1,0:T(8,128)(2,1)S(1)} collective-permute-done((bf16[128,1152]{1,0:T(8,128)(2,1)S(1)}, bf16[128,1152]{1,0:T(8,128)(2,1)S(1)}, u32[]{:S(2)}, u32[]{:S(2)}) %collective-permute-start.9) | collective-permute-done | bytes 294944 | tf_op jit(solution)/shard_map/ppermute | solution.py:60
  41.1 2.4 %collective-permute-start.15 = (bf16[128,1152]{1,0:T(8,128)(2,1)S(1)}, bf16[128,1152]{1,0:T(8,128)(2,1)S(1)}, u32[]{:S(2)}, u32[]{:S(2)}) collective-permute-start(bf16[128,1152]{1,0:T(8,128)(2,1)S(1)} %place_second.1.refs_1_.refs_2_.refs_0_.refs_4_), channel_id=1, source_target_pairs={{0,24},{4,28},{8,16},{12,20},{16,8},{20,12},{24,0},{28,4},{1,25},{... | collective-permute-start | bytes 884744 | tf_op jit(solution)/shard_map/ppermute | solution.py:66
  48.3 6.9 %experts_own.1 = (bf16[512,2048]{1,0:T(8,128)(2,1)S(1)}, bf16[512,1024]{1,0:T(8,128)(2,1)S(1)}, bf16[512,128]{1,0:T(8,128)(2,1)S(1)}) custom-call(s32[3]{0:T(128)S(1)} %copy-done.14, bf16[128,1152]{1,0:T(8,128)(2,1)S(1)} %place_second.1.refs_1_.refs_2_.refs_0_.refs_4_, bf16[128,1152]{1,0:T(8,128)(2,1)S(1)} %collective-permute-done.9.refs_2_.refs_1_, ...), custom_call_target="tpu_custom_call" | custom-call | flops 3221225472 | bytes 9437184 | tf_op jit(solution)/shard_map/experts_own/pallas_call | solution.py:590
  56.3 3.5 %experts_arrival.1 = (bf16[256,1152]{1,0:T(8,128)(2,1)S(1)}, bf16[256,1152]{1,0:T(8,128)(2,1)S(1)}) custom-call(bf16[512,2048]{1,0:T(8,128)(2,1)S(1)} %get-tuple-element.79.both_ref.refs_8_, bf16[512,128]{1,0:T(8,128)(2,1)S(1)} %get-tuple-element.80.dg_ref, bf16[8,1024,128]{2,1,0:T(8,128)(2,1)S(1)} %copy-done.20, bf16[8,1024,128]{2,1,0:T(8,128)(2,1)S(1)} %copy-done.22, ...), custom_call_target="tpu_custom_call" | custom-call | flops 2147483648 | bytes 8388608 | tf_op jit(solution)/shard_map/experts_arrival/pallas_call | solution.py:628
  61.0 2.3 %experts_mixed.1 = (bf16[256,1024]{1,0:T(8,128)(2,1)S(1)}, bf16[256,1024]{1,0:T(8,128)(2,1)S(1)}) custom-call(bf16[512,1024]{1,0:T(8,128)(2,1)S(1)} %get-tuple-element.78.gated_ref.refs_8_, bf16[8,1024,128]{2,1,0:T(8,128)(2,1)S(1)} %copy-done.24, bf16[256,1152]{1,0:T(8,128)(2,1)S(1)} %get-tuple-element.81.refs_0_.refs_1_), custom_call_target="tpu_custom_call" | custom-call | flops 1073741824 | bytes 4194304 | tf_op jit(solution)/shard_map/experts_mixed/pallas_call | solution.py:672
  64.5 6.3 %experts_far.1 = (bf16[512,2048]{1,0:T(8,128)(2,1)S(1)}, bf16[512,1024]{1,0:T(8,128)(2,1)S(1)}) custom-call(s32[3]{0:T(128)S(1)} %copy-done.14, bf16[128,1152]{1,0:T(8,128)(2,1)S(1)} %collective-permute-done.14.refs_0_.refs_1_.refs_4_, bf16[128,1152]{1,0:T(8,128)(2,1)S(1)} %collective-permute-done.15.refs_1_.refs_2_.refs_5_, ...), custom_call_target="tpu_custom_call" | custom-call | flops 3221225472 | bytes 9437184 | tf_op jit(solution)/shard_map/experts_far/pallas_call | solution.py:590
  70.8 2.2 %collective-permute-done.18.refs_3_ = bf16[128,1152]{1,0:T(8,128)(2,1)S(1)} collective-permute-done((bf16[128,1152]{1,0:T(8,128)(2,1)S(1)}, bf16[128,1152]{1,0:T(8,128)(2,1)S(1)}, u32[]{:S(2)}, u32[]{:S(2)}) %collective-permute-start.18) | collective-permute-done | bytes 294944 | tf_op jit(solution)/shard_map/ppermute | solution.py:60
  75.0 2.4 %collective-permute-start.25 = (bf16[32,1152]{1,0:T(8,128)(2,1)S(1)}, bf16[32,1152]{1,0:T(8,128)(2,1)S(1)}, u32[]{:S(2)}, u32[]{:S(2)}) collective-permute-start(bf16[32,1152]{1,0:T(8,128)(2,1)S(1)} %get-tuple-element.88), channel_id=1, source_target_pairs={{0,2},{1,3},{2,0},{3,1},{4,6},{5,7},{6,4},{7,5},{8,10},{9,11},{10,... | collective-permute-start | bytes 221192 | tf_op jit(solution)/shard_map/ppermute | solution.py:60
  78.8 4.3 %experts_weight_grads.2 = (f32[8,512,128]{2,1,0:T(8,128)}, f32[8,128]{1,0:T(8,128)S(1)}) custom-call(s32[3]{0:T(128)S(1)} %copy-done.14, bf16[128,1024]{1,0:T(8,128)(2,1)S(1)} %get-tuple-element.77.refs_5_.refs_0_, bf16[128,1024]{1,0:T(8,128)(2,1)S(1)} %collective-permute-done.8.refs_6_.refs_1_, ...), custom_call_target="tpu_custom_call" | custom-call | flops 1073741824 | bytes 4194304 | tf_op jit(solution)/shard_map/experts_weight_grads/pallas_call | solution.py:755
  85.1 2.6 %collective-permute-start.28 = (bf16[32,2176]{1,0:T(8,128)(2,1)S(1)}, bf16[32,2176]{1,0:T(8,128)(2,1)S(1)}, u32[]{:S(2)}, u32[]{:S(2)}) collective-permute-start(bf16[32,2176]{1,0:T(8,128)(2,1)S(1)} %get-tuple-element.100), channel_id=1, source_target_pairs={{0,2},{1,3},{2,0},{3,1},{4,6},{5,7},{6,4},{7,5},{8,10},{9,11},{10,... | collective-permute-start | bytes 417800 | tf_op jit(solution)/shard_map/ppermute | solution.py:60
  87.6 1.8 %collective-permute-start.29 = (bf16[32,2176]{1,0:T(8,128)(2,1)S(1)}, bf16[32,2176]{1,0:T(8,128)(2,1)S(1)}, u32[]{:S(2)}, u32[]{:S(2)}) collective-permute-start(bf16[32,2176]{1,0:T(8,128)(2,1)S(1)} %get-tuple-element.101), channel_id=1, source_target_pairs={{0,3},{1,2},{2,1},{3,0},{4,7},{5,6},{6,5},{7,4},{8,11},{9,10},{10,... | collective-permute-start | bytes 417800 | tf_op jit(solution)/shard_map/ppermute | solution.py:60
  89.5 6.0 %experts_weight_grads.3 = (f32[8,512,128]{2,1,0:T(8,128)}, f32[8,512,128]{2,1,0:T(8,128)}, f32[8,128]{1,0:T(8,128)S(1)}) custom-call(s32[3]{0:T(128)S(1)} %copy-done.14, bf16[128,1152]{1,0:T(8,128)(2,1)S(1)} %place_second.1.refs_1_.refs_2_.refs_0_.refs_4_, bf16[128,1152]{1,0:T(8,128)(2,1)S(1)} %collective-permute-done.9.refs_2_.refs_1_, ...), custom_call_target="tpu_custom_call" | custom-call | flops 2147483648 | bytes 6291456 | tf_op jit(solution)/shard_map/experts_weight_grads/pallas_call | solution.py:755
  97.2 3.2 %attend_grad.1 = (bf16[512,896]{1,0:T(8,128)(2,1)S(1)}, bf16[512,896]{1,0:T(8,128)(2,1)S(1)}, bf16[32,1024]{1,0:T(8,128)(2,1)S(1)}, f32[32,1024]{1,0:T(8,128)S(1...) custom-call(s32[3]{0:T(128)S(1)} %copy-done.14, ...), custom_call_target="tpu_custom_call" | custom-call | flops 402653184 | bytes 6193164 | tf_op jit(solution)/shard_map/attend_grad/pallas_call | solution.py:123
  100.5 2.5 %collective-permute-done.33.refs_1_ = bf16[512,896]{1,0:T(8,128)(2,1)S(1)} collective-permute-done((bf16[512,896]{1,0:T(8,128)(2,1)S(1)}, bf16[512,896]{1,0:T(8,128)(2,1)S(1)}, u32[]{:S(2)}, u32[]{:S(2)}) %collective-permute-start.33) | collective-permute-done | bytes 917536 | tf_op jit(solution)/shard_map/ppermute | solution.py:60
  106.8 2.1 %collective-permute-start.30 = (bf16[32,2048]{1,0:T(8,128)(2,1)S(1)}, bf16[32,2048]{1,0:T(8,128)(2,1)S(1)}, u32[]{:S(2)}, u32[]{:S(2)}) collective-permute-start(bf16[32,2048]{1,0:T(8,128)(2,1)S(1)} %get-tuple-element.106), channel_id=1, source_target_pairs={{0,1},{1,0},{2,3},{3,2},{4,5},{5,4},{6,7},{7,6},{8,9},{9,8},{10,11... | collective-permute-start | bytes 393224 | tf_op jit(solution)/shard_map/ppermute | solution.py:60
  109.5 2.2 %collective-permute-done.34.refs_1_ = bf16[128,896]{1,0:T(8,128)(2,1)S(1)} collective-permute-done((bf16[128,896]{1,0:T(8,128)(2,1)S(1)}, bf16[128,896]{1,0:T(8,128)(2,1)S(1)}, u32[]{:S(2)}, u32[]{:S(2)}) %collective-permute-start.34) | collective-permute-done | bytes 229408 | tf_op jit(solution)/shard_map/ppermute | solution.py:66
  111.7 2.1 %collective-permute-start.32 = (bf16[32,2048]{1,0:T(8,128)(2,1)S(1)}, bf16[32,2048]{1,0:T(8,128)(2,1)S(1)}, u32[]{:S(2)}, u32[]{:S(2)}) collective-permute-start(bf16[32,2048]{1,0:T(8,128)(2,1)S(1)} %get-tuple-element.108), channel_id=1, source_target_pairs={{0,3},{1,2},{2,1},{3,0},{4,7},{5,6},{6,5},{7,4},{8,11},{9,10},{10,... | collective-permute-start | bytes 393224 | tf_op jit(solution)/shard_map/ppermute | solution.py:60
  113.8 3.2 %collective-permute-done.35.refs_2_ = bf16[128,896]{1,0:T(8,128)(2,1)S(1)} collective-permute-done((bf16[128,896]{1,0:T(8,128)(2,1)S(1)}, bf16[128,896]{1,0:T(8,128)(2,1)S(1)}, u32[]{:S(2)}, u32[]{:S(2)}) %collective-permute-start.35) | collective-permute-done | bytes 229408 | tf_op jit(solution)/shard_map/ppermute | solution.py:66
  117.9 3.0 %collective-permute-done.31.refs_7_.refs_3_ = bf16[32,2048]{1,0:T(8,128)(2,1)S(1)} collective-permute-done((bf16[32,2048]{1,0:T(8,128)(2,1)S(1)}, bf16[32,2048]{1,0:T(8,128)(2,1)S(1)}, u32[]{:S(2)}, u32[]{:S(2)}) %collective-permute-start.31) | collective-permute-done | bytes 131104 | tf_op jit(solution)/shard_map/ppermute | solution.py:60
  121.6 2.4 %collective-permute-start.37 = (bf16[32,1152]{1,0:T(8,128)(2,1)S(1)}, bf16[32,1152]{1,0:T(8,128)(2,1)S(1)}, u32[]{:S(2)}, u32[]{:S(2)}) collective-permute-start(bf16[32,1152]{1,0:T(8,128)(2,1)S(1)} %input_grad.1.refs_5_), channel_id=1, source_target_pairs={{0,1},{1,0},{2,3},{3,2},{4,5},{5,4},{6,7},{7,6},{8,9},{9,8},{10,11... | collective-permute-start | bytes 221192 | tf_op jit(solution)/shard_map/ppermute | solution.py:60
  124.7 1.8 %collective-permute-start.39 = (bf16[32,1152]{1,0:T(8,128)(2,1)S(1)}, bf16[32,1152]{1,0:T(8,128)(2,1)S(1)}, u32[]{:S(2)}, u32[]{:S(2)}) collective-permute-start(bf16[32,1152]{1,0:T(8,128)(2,1)S(1)} %input_grad.1.refs_5_), channel_id=1, source_target_pairs={{0,3},{1,2},{2,1},{3,0},{4,7},{5,6},{6,5},{7,4},{8,11},{9,10},{10,... | collective-permute-start | bytes 221192 | tf_op jit(solution)/shard_map/ppermute | solution.py:60
  126.4 5.3 %collective-permute-done.38.refs_7_ = bf16[32,1152]{1,0:T(8,128)(2,1)S(1)} collective-permute-done((bf16[32,1152]{1,0:T(8,128)(2,1)S(1)}, bf16[32,1152]{1,0:T(8,128)(2,1)S(1)}, u32[]{:S(2)}, u32[]{:S(2)}) %collective-permute-start.38) | collective-permute-done | bytes 73760 | tf_op jit(solution)/shard_map/ppermute | solution.py:60
  (117 shorter events, 32.7 us)
Async XLA Ops:
  0.7 20.5 %collective-permute-start.3 = (bf16[128,1024]{1,0:T(8,128)(2,1)}, bf16[128,1024]{1,0:T(8,128)(2,1)S(1)}, u32[]{:S(2)}, u32[]{:S(2)}) collective-permute-start(bf16[128,1024]{1,0:T(8,128)(2,1)} %refs_3_.2), channel_id=1, source_target_pairs={{0,16},{16,0},{1,17},{17,1},{2,18},{18,2},{3,19},{19,3},{4,20},{20... | collective-permute-start | bytes 786440 | tf_op jit(solution)/shard_map/ppermute | solution.py:60
  3.7 17.5 %collective-permute-start.4 = (bf16[128,1024]{1,0:T(8,128)(2,1)}, bf16[128,1024]{1,0:T(8,128)(2,1)S(1)}, u32[]{:S(2)}, u32[]{:S(2)}) collective-permute-start(bf16[128,1024]{1,0:T(8,128)(2,1)} %refs_3_.2), channel_id=1, source_target_pairs={{0,24},{4,28},{8,16},{12,20},{16,8},{20,12},{24,0},{28,4},{1,25},{... | collective-permute-start | bytes 786440 | tf_op jit(solution)/shard_map/ppermute | solution.py:66
  10.6 5.2 %collective-permute-start = (bf16[32,1024]{1,0:T(8,128)(2,1)}, bf16[32,1024]{1,0:T(8,128)(2,1)S(1)}, u32[]{:S(2)}, u32[]{:S(2)}) collective-permute-start(bf16[32,1024]{1,0:T(8,128)(2,1)} %get-tuple-element.72), channel_id=1, source_target_pairs={{0,1},{1,0},{2,3},{3,2},{4,5},{5,4},{6,7},{7,6},{8,9},{9,8},{10,11... | collective-permute-start | bytes 196616 | tf_op jit(solution)/shard_map/ppermute | solution.py:60
  12.3 6.9 %collective-permute-start.1 = (bf16[32,1024]{1,0:T(8,128)(2,1)}, bf16[32,1024]{1,0:T(8,128)(2,1)S(1)}, u32[]{:S(2)}, u32[]{:S(2)}) collective-permute-start(bf16[32,1024]{1,0:T(8,128)(2,1)} %get-tuple-element.73), channel_id=1, source_target_pairs={{0,2},{1,3},{2,0},{3,1},{4,6},{5,7},{6,4},{7,5},{8,10},{9,11},{10,... | collective-permute-start | bytes 196616 | tf_op jit(solution)/shard_map/ppermute | solution.py:60
  14.9 6.3 %collective-permute-start.2 = (bf16[32,1024]{1,0:T(8,128)(2,1)}, bf16[32,1024]{1,0:T(8,128)(2,1)S(1)}, u32[]{:S(2)}, u32[]{:S(2)}) collective-permute-start(bf16[32,1024]{1,0:T(8,128)(2,1)} %get-tuple-element.74), channel_id=1, source_target_pairs={{0,3},{1,2},{2,1},{3,0},{4,7},{5,6},{6,5},{7,4},{8,11},{9,10},{10,... | collective-permute-start | bytes 196616 | tf_op jit(solution)/shard_map/ppermute | solution.py:60
  22.9 8.5 %collective-permute-start.8 = (bf16[128,1024]{1,0:T(8,128)(2,1)S(1)}, bf16[128,1024]{1,0:T(8,128)(2,1)S(1)}, u32[]{:S(2)}, u32[]{:S(2)}) collective-permute-start(bf16[128,1024]{1,0:T(8,128)(2,1)S(1)} %get-tuple-element.77.refs_5_.refs_0_), channel_id=1, source_target_pairs={{0,8},{4,12},{8,0},{12,4},{1,9},{5,13},{9,1},{13,5},{2,10},{6,14},... | collective-permute-start | bytes 786440 | tf_op jit(solution)/shard_map/ppermute | solution.py:60
  23.5 5.5 %collective-permute-start.5 = (bf16[32,1024]{1,0:T(8,128)(2,1)S(1)}, bf16[32,1024]{1,0:T(8,128)(2,1)S(1)}, u32[]{:S(2)}, u32[]{:S(2)}) collective-permute-start(bf16[32,1024]{1,0:T(8,128)(2,1)S(1)} %get-tuple-element.76.refs_2_), channel_id=1, source_target_pairs={{0,1},{1,0},{2,3},{3,2},{4,5},{5,4},{6,7},{7,6},{8,9},{9,8},{10,11... | collective-permute-start | bytes 196616 | tf_op jit(solution)/shard_map/ppermute | solution.py:60
  23.5 5.5 %collective-permute-start.6 = (bf16[32,1024]{1,0:T(8,128)(2,1)S(1)}, bf16[32,1024]{1,0:T(8,128)(2,1)S(1)}, u32[]{:S(2)}, u32[]{:S(2)}) collective-permute-start(bf16[32,1024]{1,0:T(8,128)(2,1)S(1)} %get-tuple-element.76.refs_2_), channel_id=1, source_target_pairs={{0,2},{1,3},{2,0},{3,1},{4,6},{5,7},{6,4},{7,5},{8,10},{9,11},{10,... | collective-permute-start | bytes 196616 | tf_op jit(solution)/shard_map/ppermute | solution.py:60
  25.3 6.2 %collective-permute-start.7 = (bf16[32,1024]{1,0:T(8,128)(2,1)S(1)}, bf16[32,1024]{1,0:T(8,128)(2,1)S(1)}, u32[]{:S(2)}, u32[]{:S(2)}) collective-permute-start(bf16[32,1024]{1,0:T(8,128)(2,1)S(1)} %get-tuple-element.76.refs_2_), channel_id=1, source_target_pairs={{0,3},{1,2},{2,1},{3,0},{4,7},{5,6},{6,5},{7,4},{8,11},{9,10},{10,... | collective-permute-start | bytes 196616 | tf_op jit(solution)/shard_map/ppermute | solution.py:60
  32.3 6.8 %collective-permute-start.9 = (bf16[128,1152]{1,0:T(8,128)(2,1)S(1)}, bf16[128,1152]{1,0:T(8,128)(2,1)S(1)}, u32[]{:S(2)}, u32[]{:S(2)}) collective-permute-start(bf16[128,1152]{1,0:T(8,128)(2,1)S(1)} %place_second.1.refs_1_.refs_2_.refs_0_.refs_4_), channel_id=1, source_target_pairs={{0,8},{4,12},{8,0},{12,4},{1,9},{5,13},{9,1},{13,5},{2,10},{6,14},... | collective-permute-start | bytes 884744 | tf_op jit(solution)/shard_map/ppermute | solution.py:60
  33.9 9.6 %collective-permute-start.10 = (bf16[128,1152]{1,0:T(8,128)(2,1)S(1)}, bf16[128,1152]{1,0:T(8,128)(2,1)S(1)}, u32[]{:S(2)}, u32[]{:S(2)}) collective-permute-start(bf16[128,1152]{1,0:T(8,128)(2,1)S(1)} %place_second.1.refs_1_.refs_2_.refs_0_.refs_4_), channel_id=1, source_target_pairs={{0,4},{4,0},{8,12},{12,8},{1,5},{5,1},{9,13},{13,9},{2,6},{6,2},{1... | collective-permute-start | bytes 884744 | tf_op jit(solution)/shard_map/ppermute | solution.py:60
  39.1 4.4 %collective-permute-start.11 = (bf16[128,1152]{1,0:T(8,128)(2,1)S(1)}, bf16[128,1152]{1,0:T(8,128)(2,1)S(1)}, u32[]{:S(2)}, u32[]{:S(2)}) collective-permute-start(bf16[128,1152]{1,0:T(8,128)(2,1)S(1)} %collective-permute-done.9.refs_2_.refs_1_), channel_id=1, source_target_pairs={{0,4},{4,0},{8,12},{12,8},{1,5},{5,1},{9,13},{13,9},{2,6},{6,2},{1... | collective-permute-start | bytes 884744 | tf_op jit(solution)/shard_map/ppermute | solution.py:60
  39.6 15.6 %collective-permute-start.14 = (bf16[128,1152]{1,0:T(8,128)(2,1)S(1)}, bf16[128,1152]{1,0:T(8,128)(2,1)S(1)}, u32[]{:S(2)}, u32[]{:S(2)}) collective-permute-start(bf16[128,1152]{1,0:T(8,128)(2,1)S(1)} %place_second.1.refs_1_.refs_2_.refs_0_.refs_4_), channel_id=1, source_target_pairs={{0,16},{16,0},{1,17},{17,1},{2,18},{18,2},{3,19},{19,3},{4,20},{20... | collective-permute-start | bytes 884744 | tf_op jit(solution)/shard_map/ppermute | solution.py:60
  41.1 15.2 %collective-permute-start.15 = (bf16[128,1152]{1,0:T(8,128)(2,1)S(1)}, bf16[128,1152]{1,0:T(8,128)(2,1)S(1)}, u32[]{:S(2)}, u32[]{:S(2)}) collective-permute-start(bf16[128,1152]{1,0:T(8,128)(2,1)S(1)} %place_second.1.refs_1_.refs_2_.refs_0_.refs_4_), channel_id=1, source_target_pairs={{0,24},{4,28},{8,16},{12,20},{16,8},{20,12},{24,0},{28,4},{1,25},{... | collective-permute-start | bytes 884744 | tf_op jit(solution)/shard_map/ppermute | solution.py:66
  63.4 10.4 %collective-permute-start.16 = (bf16[256,1024]{1,0:T(8,128)(2,1)S(1)}, bf16[256,1024]{1,0:T(8,128)(2,1)S(1)}, u32[]{:S(2)}, u32[]{:S(2)}) collective-permute-start(bf16[256,1024]{1,0:T(8,128)(2,1)S(1)} %get-tuple-element.83), channel_id=1, source_target_pairs={{0,4},{4,0},{8,12},{12,8},{1,5},{5,1},{9,13},{13,9},{2,6},{6,2},{1... | collective-permute-start | bytes 1572872 | tf_op jit(solution)/shard_map/ppermute | solution.py:60
  64.0 9.1 %collective-permute-start.18 = (bf16[128,1152]{1,0:T(8,128)(2,1)S(1)}, bf16[128,1152]{1,0:T(8,128)(2,1)S(1)}, u32[]{:S(2)}, u32[]{:S(2)}) collective-permute-start(bf16[128,1152]{1,0:T(8,128)(2,1)S(1)} %add_convert_fusion), channel_id=1, source_target_pairs={{0,8},{4,12},{8,0},{12,4},{1,9},{5,13},{9,1},{13,5},{2,10},{6,14},... | collective-permute-start | bytes 884744 | tf_op jit(solution)/shard_map/ppermute | solution.py:60
  73.8 9.8 %collective-permute-start.23 = (bf16[128,1024]{1,0:T(8,128)(2,1)S(1)}, bf16[128,1024]{1,0:T(8,128)(2,1)S(1)}, u32[]{:S(2)}, u32[]{:S(2)}) collective-permute-start(bf16[128,1024]{1,0:T(8,128)(2,1)S(1)} %half.1), channel_id=1, source_target_pairs={{0,8},{4,12},{8,0},{12,4},{1,9},{5,13},{9,1},{13,5},{2,10},{6,14},... | collective-permute-start | bytes 786440 | tf_op jit(solution)/shard_map/ppermute | solution.py:60
  74.4 8.7 %collective-permute-start.24 = (bf16[32,1152]{1,0:T(8,128)(2,1)S(1)}, bf16[32,1152]{1,0:T(8,128)(2,1)S(1)}, u32[]{:S(2)}, u32[]{:S(2)}) collective-permute-start(bf16[32,1152]{1,0:T(8,128)(2,1)S(1)} %get-tuple-element.87), channel_id=1, source_target_pairs={{0,1},{1,0},{2,3},{3,2},{4,5},{5,4},{6,7},{7,6},{8,9},{9,8},{10,11... | collective-permute-start | bytes 221192 | tf_op jit(solution)/shard_map/ppermute | solution.py:60
  75.0 8.1 %collective-permute-start.25 = (bf16[32,1152]{1,0:T(8,128)(2,1)S(1)}, bf16[32,1152]{1,0:T(8,128)(2,1)S(1)}, u32[]{:S(2)}, u32[]{:S(2)}) collective-permute-start(bf16[32,1152]{1,0:T(8,128)(2,1)S(1)} %get-tuple-element.88), channel_id=1, source_target_pairs={{0,2},{1,3},{2,0},{3,1},{4,6},{5,7},{6,4},{7,5},{8,10},{9,11},{10,... | collective-permute-start | bytes 221192 | tf_op jit(solution)/shard_map/ppermute | solution.py:60
  77.4 6.2 %collective-permute-start.26 = (bf16[32,1152]{1,0:T(8,128)(2,1)S(1)}, bf16[32,1152]{1,0:T(8,128)(2,1)S(1)}, u32[]{:S(2)}, u32[]{:S(2)}) collective-permute-start(bf16[32,1152]{1,0:T(8,128)(2,1)S(1)} %get-tuple-element.89), channel_id=1, source_target_pairs={{0,3},{1,2},{2,1},{3,0},{4,7},{5,6},{6,5},{7,4},{8,11},{9,10},{10,... | collective-permute-start | bytes 221192 | tf_op jit(solution)/shard_map/ppermute | solution.py:60
  85.0 10.5 %collective-permute-start.27 = (bf16[32,2176]{1,0:T(8,128)(2,1)S(1)}, bf16[32,2176]{1,0:T(8,128)(2,1)S(1)}, u32[]{:S(2)}, u32[]{:S(2)}) collective-permute-start(bf16[32,2176]{1,0:T(8,128)(2,1)S(1)} %get-tuple-element.99), channel_id=1, source_target_pairs={{0,1},{1,0},{2,3},{3,2},{4,5},{5,4},{6,7},{7,6},{8,9},{9,8},{10,11... | collective-permute-start | bytes 417800 | tf_op jit(solution)/shard_map/ppermute | solution.py:60
  85.1 12.0 %collective-permute-start.28 = (bf16[32,2176]{1,0:T(8,128)(2,1)S(1)}, bf16[32,2176]{1,0:T(8,128)(2,1)S(1)}, u32[]{:S(2)}, u32[]{:S(2)}) collective-permute-start(bf16[32,2176]{1,0:T(8,128)(2,1)S(1)} %get-tuple-element.100), channel_id=1, source_target_pairs={{0,2},{1,3},{2,0},{3,1},{4,6},{5,7},{6,4},{7,5},{8,10},{9,11},{10,... | collective-permute-start | bytes 417800 | tf_op jit(solution)/shard_map/ppermute | solution.py:60
  87.6 9.5 %collective-permute-start.29 = (bf16[32,2176]{1,0:T(8,128)(2,1)S(1)}, bf16[32,2176]{1,0:T(8,128)(2,1)S(1)}, u32[]{:S(2)}, u32[]{:S(2)}) collective-permute-start(bf16[32,2176]{1,0:T(8,128)(2,1)S(1)} %get-tuple-element.101), channel_id=1, source_target_pairs={{0,3},{1,2},{2,1},{3,0},{4,7},{5,6},{6,5},{7,4},{8,11},{9,10},{10,... | collective-permute-start | bytes 417800 | tf_op jit(solution)/shard_map/ppermute | solution.py:60
  103.2 8.5 %collective-permute-start.34 = (bf16[128,896]{1,0:T(8,128)(2,1)S(1)}, bf16[128,896]{1,0:T(8,128)(2,1)S(1)}, u32[]{:S(2)}, u32[]{:S(2)}) collective-permute-start(bf16[128,896]{1,0:T(8,128)(2,1)S(1)} %get-tuple-element.113), channel_id=1, source_target_pairs={{0,16},{4,20},{8,24},{12,28},{16,0},{20,4},{24,8},{28,12},{1,17},{... | collective-permute-start | bytes 688136 | tf_op jit(solution)/shard_map/ppermute | solution.py:66
  104.7 12.3 %collective-permute-start.35 = (bf16[128,896]{1,0:T(8,128)(2,1)S(1)}, bf16[128,896]{1,0:T(8,128)(2,1)S(1)}, u32[]{:S(2)}, u32[]{:S(2)}) collective-permute-start(bf16[128,896]{1,0:T(8,128)(2,1)S(1)} %get-tuple-element.114), channel_id=1, source_target_pairs={{0,8},{4,12},{8,0},{12,4},{16,24},{20,28},{24,16},{28,20},{1,9},{5... | collective-permute-start | bytes 688136 | tf_op jit(solution)/shard_map/ppermute | solution.py:66
  106.3 10.8 %collective-permute-start.36 = (bf16[128,896]{1,0:T(8,128)(2,1)S(1)}, bf16[128,896]{1,0:T(8,128)(2,1)S(1)}, u32[]{:S(2)}, u32[]{:S(2)}) collective-permute-start(bf16[128,896]{1,0:T(8,128)(2,1)S(1)} %get-tuple-element.115), channel_id=1, source_target_pairs={{0,24},{4,28},{8,16},{12,20},{16,8},{20,12},{24,0},{28,4},{1,25},{... | collective-permute-start | bytes 688136 | tf_op jit(solution)/shard_map/ppermute | solution.py:66
  106.8 11.1 %collective-permute-start.30 = (bf16[32,2048]{1,0:T(8,128)(2,1)S(1)}, bf16[32,2048]{1,0:T(8,128)(2,1)S(1)}, u32[]{:S(2)}, u32[]{:S(2)}) collective-permute-start(bf16[32,2048]{1,0:T(8,128)(2,1)S(1)} %get-tuple-element.106), channel_id=1, source_target_pairs={{0,1},{1,0},{2,3},{3,2},{4,5},{5,4},{6,7},{7,6},{8,9},{9,8},{10,11... | collective-permute-start | bytes 393224 | tf_op jit(solution)/shard_map/ppermute | solution.py:60
  108.9 12.0 %collective-permute-start.31 = (bf16[32,2048]{1,0:T(8,128)(2,1)S(1)}, bf16[32,2048]{1,0:T(8,128)(2,1)S(1)}, u32[]{:S(2)}, u32[]{:S(2)}) collective-permute-start(bf16[32,2048]{1,0:T(8,128)(2,1)S(1)} %get-tuple-element.107), channel_id=1, source_target_pairs={{0,2},{1,3},{2,0},{3,1},{4,6},{5,7},{6,4},{7,5},{8,10},{9,11},{10,... | collective-permute-start | bytes 393224 | tf_op jit(solution)/shard_map/ppermute | solution.py:60
  111.7 9.2 %collective-permute-start.32 = (bf16[32,2048]{1,0:T(8,128)(2,1)S(1)}, bf16[32,2048]{1,0:T(8,128)(2,1)S(1)}, u32[]{:S(2)}, u32[]{:S(2)}) collective-permute-start(bf16[32,2048]{1,0:T(8,128)(2,1)S(1)} %get-tuple-element.108), channel_id=1, source_target_pairs={{0,3},{1,2},{2,1},{3,0},{4,7},{5,6},{6,5},{7,4},{8,11},{9,10},{10,... | collective-permute-start | bytes 393224 | tf_op jit(solution)/shard_map/ppermute | solution.py:60
  121.6 4.8 %collective-permute-start.37 = (bf16[32,1152]{1,0:T(8,128)(2,1)S(1)}, bf16[32,1152]{1,0:T(8,128)(2,1)S(1)}, u32[]{:S(2)}, u32[]{:S(2)}) collective-permute-start(bf16[32,1152]{1,0:T(8,128)(2,1)S(1)} %input_grad.1.refs_5_), channel_id=1, source_target_pairs={{0,1},{1,0},{2,3},{3,2},{4,5},{5,4},{6,7},{7,6},{8,9},{9,8},{10,11... | collective-permute-start | bytes 221192 | tf_op jit(solution)/shard_map/ppermute | solution.py:60
  124.0 7.8 %collective-permute-start.38 = (bf16[32,1152]{1,0:T(8,128)(2,1)S(1)}, bf16[32,1152]{1,0:T(8,128)(2,1)S(1)}, u32[]{:S(2)}, u32[]{:S(2)}) collective-permute-start(bf16[32,1152]{1,0:T(8,128)(2,1)S(1)} %input_grad.1.refs_5_), channel_id=1, source_target_pairs={{0,2},{1,3},{2,0},{3,1},{4,6},{5,7},{6,4},{7,5},{8,10},{9,11},{10,... | collective-permute-start | bytes 221192 | tf_op jit(solution)/shard_map/ppermute | solution.py:60
  124.7 7.1 %collective-permute-start.39 = (bf16[32,1152]{1,0:T(8,128)(2,1)S(1)}, bf16[32,1152]{1,0:T(8,128)(2,1)S(1)}, u32[]{:S(2)}, u32[]{:S(2)}) collective-permute-start(bf16[32,1152]{1,0:T(8,128)(2,1)S(1)} %input_grad.1.refs_5_), channel_id=1, source_target_pairs={{0,3},{1,2},{2,1},{3,0},{4,7},{5,6},{6,5},{7,4},{8,11},{9,10},{10,... | collective-permute-start | bytes 221192 | tf_op jit(solution)/shard_map/ppermute | solution.py:60
  (33 other events, 285.8 us)

commit v5 on v4

--- a/solution.py
+++ b/solution.py
@@ -995,6 +995,8 @@
         after=[gate_done],
     )
 
+    dn1 = [dn1[0]] + swap_tensor(dn1[1:])
+
     expert_bits = list(reversed(bits_of(expert_n)))
     for k in expert_bits[:-2]:
         total = near.astype(F32) + swap(far, "expert", k).astype(F32)
@@ -1021,9 +1023,8 @@
         4 * rows * last_width,
         own_rows,
         *got,
-    )
-    dn1 = [dn1[0]] + swap_tensor(dn1[1:])
-
+        after=dn1[1:],
+    )
     (last_block,) = plain_call(
         input_grad_kernel,
         "input_grad",

time: 134 us -> 132 us (0.985)
  waiting for transfers between devices: 36.6 us -> 33.3 us
  starting transfers between devices: 44.8 us -> 46.2 us
    ppermute x5, waiting for transfers between devices: 6.54 us -> 1.13 us  [swap_plane(): lax.ppermute(x, ('dp', 'expert'), [(i, i ^ k_dp * n + k_expert) for i in...]
    ppermute x35, waiting for transfers between devices: 30 us -> 32.2 us  [swap(): return lax.ppermute(x, axis, [(i, i ^ k) for i in range(n)])]
    ppermute x35, starting transfers between devices: 37.4 us -> 38.8 us  [swap(): return lax.ppermute(x, axis, [(i, i ^ k) for i in range(n)])]
  transfers between devices with their start and end apart: 40 -> 40, of which waited for: 15 -> 15; matrix products, arithmetic and copies ran while one was open for 0% -> 1% of each run, Pallas kernels for 24% -> 24%
where the time goes in v5:
time: 132 us; the launch traced here: 131 us
  starting transfers between devices  46.2 us (35%)
  Pallas kernels  43.7 us (33%)
  waiting for transfers between devices  33.3 us (25%)
  local copies, waits for them, and re-layouts  6.44 us (5%)
    ppermute x35, starting transfers between devices, swap(): return lax.ppermute(x, axis, [(i, i ^ k) for i in range(n)])  38.8 us
    ppermute x35, waiting for transfers between devices, swap(): return lax.ppermute(x, axis, [(i, i ^ k) for i in range(n)])  32.2 us
    pallas_call x11, Pallas kernels, plain_call(): pl.pallas_call(body, grid=(1,), in_specs=[whole(a, i in hbm) for i, a in...  14.5 us
    pallas_call x2, Pallas kernels, expert_call(): pl.pallas_call(functools.partial(expert_kernel, own, steps, pair, experts...  13.1 us
    pallas_call x2, Pallas kernels, weight_grad_call(): pl.pallas_call(functools.partial(weight_grad_kernel, sets, parts, outs, p...  10.2 us
    ppermute x5, starting transfers between devices, swap_plane(): lax.ppermute(x, ('dp', 'expert'), [(i, i ^ k_dp * n + k_expert) for i in...  7.44 us
    unnamed x50, local copies, waits for them, and re-layouts  6.44 us
    pallas_call x1, Pallas kernels, arrival_call(): pl.pallas_call(functools.partial(arrival_kernel, chunks, steps, pair), gr...  3.52 us
  transfers between devices with their start and end apart: 40, of which 15 were waited for; matrix products, arithmetic and copies ran while one was open for 1% of the time, Pallas kernels for 24%

profile of v5, /device:TPU:0, one launch (start us, length us, event | category | flops | bytes accessed | tf_op | source)
XLA Modules:
  0.0 131.5 jit_solution(15975474134786013418)
XLA Ops:
  0.7 3.0 %collective-permute-start.3 = (bf16[128,1024]{1,0:T(8,128)(2,1)}, bf16[128,1024]{1,0:T(8,128)(2,1)S(1)}, u32[]{:S(2)}, u32[]{:S(2)}) collective-permute-start(bf16[128,1024]{1,0:T(8,128)(2,1)} %refs_3_.2), channel_id=1, source_target_pairs={{0,16},{16,0},{1,17},{17,1},{2,18},{18,2},{3,19},{19,3},{4,20},{20... | collective-permute-start | bytes 786440 | tf_op jit(solution)/shard_map/ppermute | solution.py:60
  5.8 4.9 %attend.1 = (bf16[128,1024]{1,0:T(8,128)(2,1)}, bf16[128,512]{1,0:T(8,128)(2,1)}, f32[4,128,128]{2,1,0:T(8,128)}, bf16[128,256]{1,0:T(8,128)(2,1)}, f32[128,128]...) custom-call(s32[3]{0:T(128)} %pad_add_fusion.refs_0_.place_ref, ...), custom_call_target="tpu_custom_call" | custom-call | flops 201326592 | bytes 3147800 | tf_op jit(solution)/shard_map/attend/pallas_call | solution.py:123
  10.6 1.6 %collective-permute-start = (bf16[32,1024]{1,0:T(8,128)(2,1)}, bf16[32,1024]{1,0:T(8,128)(2,1)S(1)}, u32[]{:S(2)}, u32[]{:S(2)}) collective-permute-start(bf16[32,1024]{1,0:T(8,128)(2,1)} %get-tuple-element.72), channel_id=1, source_target_pairs={{0,1},{1,0},{2,3},{3,2},{4,5},{5,4},{6,7},{7,6},{8,9},{9,8},{10,11... | collective-permute-start | bytes 196616 | tf_op jit(solution)/shard_map/ppermute | solution.py:60
  12.3 2.6 %collective-permute-start.1 = (bf16[32,1024]{1,0:T(8,128)(2,1)}, bf16[32,1024]{1,0:T(8,128)(2,1)S(1)}, u32[]{:S(2)}, u32[]{:S(2)}) collective-permute-start(bf16[32,1024]{1,0:T(8,128)(2,1)} %get-tuple-element.73), channel_id=1, source_target_pairs={{0,2},{1,3},{2,0},{3,1},{4,6},{5,7},{6,4},{7,5},{8,10},{9,11},{10,... | collective-permute-start | bytes 196616 | tf_op jit(solution)/shard_map/ppermute | solution.py:60
  15.8 3.4 %collective-permute-done.1.refs_4_ = bf16[32,1024]{1,0:T(8,128)(2,1)S(1)} collective-permute-done((bf16[32,1024]{1,0:T(8,128)(2,1)}, bf16[32,1024]{1,0:T(8,128)(2,1)S(1)}, u32[]{:S(2)}, u32[]{:S(2)}) %collective-permute-start.1) | collective-permute-done | bytes 65568 | tf_op jit(solution)/shard_map/ppermute | solution.py:60
  19.2 1.9 %collective-permute-done.2.refs_5_ = bf16[32,1024]{1,0:T(8,128)(2,1)S(1)} collective-permute-done((bf16[32,1024]{1,0:T(8,128)(2,1)}, bf16[32,1024]{1,0:T(8,128)(2,1)S(1)}, u32[]{:S(2)}, u32[]{:S(2)}) %collective-permute-start.2) | collective-permute-done | bytes 65568 | tf_op jit(solution)/shard_map/ppermute | solution.py:60
  23.5 1.8 %collective-permute-start.6 = (bf16[32,1024]{1,0:T(8,128)(2,1)S(1)}, bf16[32,1024]{1,0:T(8,128)(2,1)S(1)}, u32[]{:S(2)}, u32[]{:S(2)}) collective-permute-start(bf16[32,1024]{1,0:T(8,128)(2,1)S(1)} %get-tuple-element.76.refs_2_), channel_id=1, source_target_pairs={{0,2},{1,3},{2,0},{3,1},{4,6},{5,7},{6,4},{7,5},{8,10},{9,11},{10,... | collective-permute-start | bytes 196616 | tf_op jit(solution)/shard_map/ppermute | solution.py:60
  25.3 2.6 %collective-permute-start.7 = (bf16[32,1024]{1,0:T(8,128)(2,1)S(1)}, bf16[32,1024]{1,0:T(8,128)(2,1)S(1)}, u32[]{:S(2)}, u32[]{:S(2)}) collective-permute-start(bf16[32,1024]{1,0:T(8,128)(2,1)S(1)} %get-tuple-element.76.refs_2_), channel_id=1, source_target_pairs={{0,3},{1,2},{2,1},{3,0},{4,7},{5,6},{6,5},{7,4},{8,11},{9,10},{10,... | collective-permute-start | bytes 196616 | tf_op jit(solution)/shard_map/ppermute | solution.py:60
  29.0 2.4 %collective-permute-done.7.refs_5_ = bf16[32,1024]{1,0:T(8,128)(2,1)S(1)} collective-permute-done((bf16[32,1024]{1,0:T(8,128)(2,1)S(1)}, bf16[32,1024]{1,0:T(8,128)(2,1)S(1)}, u32[]{:S(2)}, u32[]{:S(2)}) %collective-permute-start.7) | collective-permute-done | bytes 65568 | tf_op jit(solution)/shard_map/ppermute | solution.py:60
  32.3 1.6 %collective-permute-start.9 = (bf16[128,1152]{1,0:T(8,128)(2,1)S(1)}, bf16[128,1152]{1,0:T(8,128)(2,1)S(1)}, u32[]{:S(2)}, u32[]{:S(2)}) collective-permute-start(bf16[128,1152]{1,0:T(8,128)(2,1)S(1)} %place_second.1.refs_1_.refs_2_.refs_0_.refs_4_), channel_id=1, source_target_pairs={{0,8},{4,12},{8,0},{12,4},{1,9},{5,13},{9,1},{13,5},{2,10},{6,14},... | collective-permute-start | bytes 884744 | tf_op jit(solution)/shard_map/ppermute | solution.py:60
  33.9 5.2 %collective-permute-done.9.refs_2_.refs_1_ = bf16[128,1152]{1,0:T(8,128)(2,1)S(1)} collective-permute-done((bf16[128,1152]{1,0:T(8,128)(2,1)S(1)}, bf16[128,1152]{1,0:T(8,128)(2,1)S(1)}, u32[]{:S(2)}, u32[]{:S(2)}) %collective-permute-start.9) | collective-permute-done | bytes 294944 | tf_op jit(solution)/shard_map/ppermute | solution.py:60
  41.1 2.4 %collective-permute-start.15 = (bf16[128,1152]{1,0:T(8,128)(2,1)S(1)}, bf16[128,1152]{1,0:T(8,128)(2,1)S(1)}, u32[]{:S(2)}, u32[]{:S(2)}) collective-permute-start(bf16[128,1152]{1,0:T(8,128)(2,1)S(1)} %place_second.1.refs_1_.refs_2_.refs_0_.refs_4_), channel_id=1, source_target_pairs={{0,24},{4,28},{8,16},{12,20},{16,8},{20,12},{24,0},{28,4},{1,25},{... | collective-permute-start | bytes 884744 | tf_op jit(solution)/shard_map/ppermute | solution.py:66
  45.1 1.6 %copy-done.21 = bf16[8,1024,128]{2,1,0:T(8,128)(2,1)S(1)} copy-done((bf16[8,1024,128]{2,1,0:T(8,128)(2,1)S(1)}, bf16[8,1024,128]{2,1,0:T(8,128)(2,1)}, u32[]{:S(2)}) %copy-start.21) | copy-done | bytes 2097176
  48.3 6.9 %experts_own.1 = (bf16[512,2048]{1,0:T(8,128)(2,1)S(1)}, bf16[512,1024]{1,0:T(8,128)(2,1)S(1)}, bf16[512,128]{1,0:T(8,128)(2,1)S(1)}) custom-call(s32[3]{0:T(128)S(1)} %copy-done.14, bf16[128,1152]{1,0:T(8,128)(2,1)S(1)} %place_second.1.refs_1_.refs_2_.refs_0_.refs_4_, bf16[128,1152]{1,0:T(8,128)(2,1)S(1)} %collective-permute-done.9.refs_2_.refs_1_, ...), custom_call_target="tpu_custom_call" | custom-call | flops 3221225472 | bytes 9437184 | tf_op jit(solution)/shard_map/experts_own/pallas_call | solution.py:590
  56.3 3.5 %experts_arrival.1 = (bf16[256,1152]{1,0:T(8,128)(2,1)S(1)}, bf16[256,1152]{1,0:T(8,128)(2,1)S(1)}) custom-call(bf16[512,2048]{1,0:T(8,128)(2,1)S(1)} %get-tuple-element.79.both_ref.refs_8_, bf16[512,128]{1,0:T(8,128)(2,1)S(1)} %get-tuple-element.80.dg_ref, bf16[8,1024,128]{2,1,0:T(8,128)(2,1)S(1)} %copy-done.20, bf16[8,1024,128]{2,1,0:T(8,128)(2,1)S(1)} %copy-done.22, ...), custom_call_target="tpu_custom_call" | custom-call | flops 2147483648 | bytes 8388608 | tf_op jit(solution)/shard_map/experts_arrival/pallas_call | solution.py:628
  61.0 2.3 %experts_mixed.1 = (bf16[256,1024]{1,0:T(8,128)(2,1)S(1)}, bf16[256,1024]{1,0:T(8,128)(2,1)S(1)}) custom-call(bf16[512,1024]{1,0:T(8,128)(2,1)S(1)} %get-tuple-element.78.gated_ref.refs_8_, bf16[8,1024,128]{2,1,0:T(8,128)(2,1)S(1)} %copy-done.24, bf16[256,1152]{1,0:T(8,128)(2,1)S(1)} %get-tuple-element.81.refs_0_.refs_1_), custom_call_target="tpu_custom_call" | custom-call | flops 1073741824 | bytes 4194304 | tf_op jit(solution)/shard_map/experts_mixed/pallas_call | solution.py:672
  64.5 6.3 %experts_far.1 = (bf16[512,2048]{1,0:T(8,128)(2,1)S(1)}, bf16[512,1024]{1,0:T(8,128)(2,1)S(1)}) custom-call(s32[3]{0:T(128)S(1)} %copy-done.14, bf16[128,1152]{1,0:T(8,128)(2,1)S(1)} %collective-permute-done.14.refs_0_.refs_1_.refs_4_, bf16[128,1152]{1,0:T(8,128)(2,1)S(1)} %collective-permute-done.15.refs_1_.refs_2_.refs_5_, ...), custom_call_target="tpu_custom_call" | custom-call | flops 3221225472 | bytes 9437184 | tf_op jit(solution)/shard_map/experts_far/pallas_call | solution.py:590
  70.8 2.2 %collective-permute-done.18.refs_3_ = bf16[128,1152]{1,0:T(8,128)(2,1)S(1)} collective-permute-done((bf16[128,1152]{1,0:T(8,128)(2,1)S(1)}, bf16[128,1152]{1,0:T(8,128)(2,1)S(1)}, u32[]{:S(2)}, u32[]{:S(2)}) %collective-permute-start.18) | collective-permute-done | bytes 294944 | tf_op jit(solution)/shard_map/ppermute | solution.py:60
  75.0 2.4 %collective-permute-start.25 = (bf16[32,1152]{1,0:T(8,128)(2,1)S(1)}, bf16[32,1152]{1,0:T(8,128)(2,1)S(1)}, u32[]{:S(2)}, u32[]{:S(2)}) collective-permute-start(bf16[32,1152]{1,0:T(8,128)(2,1)S(1)} %get-tuple-element.88), channel_id=1, source_target_pairs={{0,2},{1,3},{2,0},{3,1},{4,6},{5,7},{6,4},{7,5},{8,10},{9,11},{10,... | collective-permute-start | bytes 221192 | tf_op jit(solution)/shard_map/ppermute | solution.py:60
  78.8 4.3 %experts_weight_grads.2 = (f32[8,512,128]{2,1,0:T(8,128)}, f32[8,128]{1,0:T(8,128)S(1)}) custom-call(s32[3]{0:T(128)S(1)} %copy-done.14, bf16[128,1024]{1,0:T(8,128)(2,1)S(1)} %get-tuple-element.77.refs_5_.refs_0_, bf16[128,1024]{1,0:T(8,128)(2,1)S(1)} %collective-permute-done.8.refs_6_.refs_1_, ...), custom_call_target="tpu_custom_call" | custom-call | flops 1073741824 | bytes 4194304 | tf_op jit(solution)/shard_map/experts_weight_grads/pallas_call | solution.py:755
  85.1 2.6 %collective-permute-start.28 = (bf16[32,2176]{1,0:T(8,128)(2,1)S(1)}, bf16[32,2176]{1,0:T(8,128)(2,1)S(1)}, u32[]{:S(2)}, u32[]{:S(2)}) collective-permute-start(bf16[32,2176]{1,0:T(8,128)(2,1)S(1)} %get-tuple-element.100), channel_id=1, source_target_pairs={{0,2},{1,3},{2,0},{3,1},{4,6},{5,7},{6,4},{7,5},{8,10},{9,11},{10,... | collective-permute-start | bytes 417800 | tf_op jit(solution)/shard_map/ppermute | solution.py:60
  87.6 1.8 %collective-permute-start.29 = (bf16[32,2176]{1,0:T(8,128)(2,1)S(1)}, bf16[32,2176]{1,0:T(8,128)(2,1)S(1)}, u32[]{:S(2)}, u32[]{:S(2)}) collective-permute-start(bf16[32,2176]{1,0:T(8,128)(2,1)S(1)} %get-tuple-element.101), channel_id=1, source_target_pairs={{0,3},{1,2},{2,1},{3,0},{4,7},{5,6},{6,5},{7,4},{8,11},{9,10},{10,... | collective-permute-start | bytes 417800 | tf_op jit(solution)/shard_map/ppermute | solution.py:60
  89.5 6.0 %experts_weight_grads.3 = (f32[8,512,128]{2,1,0:T(8,128)}, f32[8,512,128]{2,1,0:T(8,128)}, f32[8,128]{1,0:T(8,128)S(1)}) custom-call(s32[3]{0:T(128)S(1)} %copy-done.14, bf16[128,1152]{1,0:T(8,128)(2,1)S(1)} %place_second.1.refs_1_.refs_2_.refs_0_.refs_4_, bf16[128,1152]{1,0:T(8,128)(2,1)S(1)} %collective-permute-done.9.refs_2_.refs_1_, ...), custom_call_target="tpu_custom_call" | custom-call | flops 2147483648 | bytes 6291456 | tf_op jit(solution)/shard_map/experts_weight_grads/pallas_call | solution.py:755
  95.5 1.6 %collective-permute-done.28.refs_16_ = bf16[32,2176]{1,0:T(8,128)(2,1)S(1)} collective-permute-done((bf16[32,2176]{1,0:T(8,128)(2,1)S(1)}, bf16[32,2176]{1,0:T(8,128)(2,1)S(1)}, u32[]{:S(2)}, u32[]{:S(2)}) %collective-permute-start.28) | collective-permute-done | bytes 139296 | tf_op jit(solution)/shard_map/ppermute | solution.py:60
  97.2 3.2 %attend_grad.1 = (bf16[512,896]{1,0:T(8,128)(2,1)S(1)}, bf16[512,896]{1,0:T(8,128)(2,1)S(1)}, bf16[32,1024]{1,0:T(8,128)(2,1)S(1)}, f32[32,1024]{1,0:T(8,128)S(1...) custom-call(s32[3]{0:T(128)S(1)} %copy-done.14, ...), custom_call_target="tpu_custom_call" | custom-call | flops 402653184 | bytes 6193164 | tf_op jit(solution)/shard_map/attend_grad/pallas_call | solution.py:123
  100.5 2.2 %collective-permute-start.30 = (bf16[32,2048]{1,0:T(8,128)(2,1)S(1)}, bf16[32,2048]{1,0:T(8,128)(2,1)S(1)}, u32[]{:S(2)}, u32[]{:S(2)}) collective-permute-start(bf16[32,2048]{1,0:T(8,128)(2,1)S(1)} %get-tuple-element.106), channel_id=1, source_target_pairs={{0,1},{1,0},{2,3},{3,2},{4,5},{5,4},{6,7},{7,6},{8,9},{9,8},{10,11... | collective-permute-start | bytes 393224 | tf_op jit(solution)/shard_map/ppermute | solution.py:60
  106.8 2.7 %collective-permute-start.31 = (bf16[32,2048]{1,0:T(8,128)(2,1)S(1)}, bf16[32,2048]{1,0:T(8,128)(2,1)S(1)}, u32[]{:S(2)}, u32[]{:S(2)}) collective-permute-start(bf16[32,2048]{1,0:T(8,128)(2,1)S(1)} %get-tuple-element.107), channel_id=1, source_target_pairs={{0,2},{1,3},{2,0},{3,1},{4,6},{5,7},{6,4},{7,5},{8,10},{9,11},{10,... | collective-permute-start | bytes 393224 | tf_op jit(solution)/shard_map/ppermute | solution.py:60
  109.5 1.8 %collective-permute-start.32 = (bf16[32,2048]{1,0:T(8,128)(2,1)S(1)}, bf16[32,2048]{1,0:T(8,128)(2,1)S(1)}, u32[]{:S(2)}, u32[]{:S(2)}) collective-permute-start(bf16[32,2048]{1,0:T(8,128)(2,1)S(1)} %get-tuple-element.108), channel_id=1, source_target_pairs={{0,3},{1,2},{2,1},{3,0},{4,7},{5,6},{6,5},{7,4},{8,11},{9,10},{10,... | collective-permute-start | bytes 393224 | tf_op jit(solution)/shard_map/ppermute | solution.py:60
  111.2 8.2 %collective-permute-done.31.refs_5_.refs_7_.refs_3_ = bf16[32,2048]{1,0:T(8,128)(2,1)S(1)} collective-permute-done((bf16[32,2048]{1,0:T(8,128)(2,1)S(1)}, bf16[32,2048]{1,0:T(8,128)(2,1)S(1)}, u32[]{:S(2)}, u32[]{:S(2)}) %collective-permute-start.31) | collective-permute-done | bytes 131104 | tf_op jit(solution)/shard_map/ppermute | solution.py:60
  121.0 2.0 %collective-permute-start.37 = (bf16[32,1152]{1,0:T(8,128)(2,1)S(1)}, bf16[32,1152]{1,0:T(8,128)(2,1)S(1)}, u32[]{:S(2)}, u32[]{:S(2)}) collective-permute-start(bf16[32,1152]{1,0:T(8,128)(2,1)S(1)} %input_grad.1.refs_5_), channel_id=1, source_target_pairs={{0,1},{1,0},{2,3},{3,2},{4,5},{5,4},{6,7},{7,6},{8,9},{9,8},{10,11... | collective-permute-start | bytes 221192 | tf_op jit(solution)/shard_map/ppermute | solution.py:60
  123.7 1.8 %collective-permute-start.39 = (bf16[32,1152]{1,0:T(8,128)(2,1)S(1)}, bf16[32,1152]{1,0:T(8,128)(2,1)S(1)}, u32[]{:S(2)}, u32[]{:S(2)}) collective-permute-start(bf16[32,1152]{1,0:T(8,128)(2,1)S(1)} %input_grad.1.refs_5_), channel_id=1, source_target_pairs={{0,3},{1,2},{2,1},{3,0},{4,7},{5,6},{6,5},{7,4},{8,11},{9,10},{10,... | collective-permute-start | bytes 221192 | tf_op jit(solution)/shard_map/ppermute | solution.py:60
  125.6 3.6 %collective-permute-done.38.refs_7_ = bf16[32,1152]{1,0:T(8,128)(2,1)S(1)} collective-permute-done((bf16[32,1152]{1,0:T(8,128)(2,1)S(1)}, bf16[32,1152]{1,0:T(8,128)(2,1)S(1)}, u32[]{:S(2)}, u32[]{:S(2)}) %collective-permute-start.38) | collective-permute-done | bytes 73760 | tf_op jit(solution)/shard_map/ppermute | solution.py:60
  (117 shorter events, 30.0 us)
Async XLA Ops:
  0.7 20.5 %collective-permute-start.3 = (bf16[128,1024]{1,0:T(8,128)(2,1)}, bf16[128,1024]{1,0:T(8,128)(2,1)S(1)}, u32[]{:S(2)}, u32[]{:S(2)}) collective-permute-start(bf16[128,1024]{1,0:T(8,128)(2,1)} %refs_3_.2), channel_id=1, source_target_pairs={{0,16},{16,0},{1,17},{17,1},{2,18},{18,2},{3,19},{19,3},{4,20},{20... | collective-permute-start | bytes 786440 | tf_op jit(solution)/shard_map/ppermute | solution.py:60
  3.7 17.5 %collective-permute-start.4 = (bf16[128,1024]{1,0:T(8,128)(2,1)}, bf16[128,1024]{1,0:T(8,128)(2,1)S(1)}, u32[]{:S(2)}, u32[]{:S(2)}) collective-permute-start(bf16[128,1024]{1,0:T(8,128)(2,1)} %refs_3_.2), channel_id=1, source_target_pairs={{0,24},{4,28},{8,16},{12,20},{16,8},{20,12},{24,0},{28,4},{1,25},{... | collective-permute-start | bytes 786440 | tf_op jit(solution)/shard_map/ppermute | solution.py:66
  10.6 5.2 %collective-permute-start = (bf16[32,1024]{1,0:T(8,128)(2,1)}, bf16[32,1024]{1,0:T(8,128)(2,1)S(1)}, u32[]{:S(2)}, u32[]{:S(2)}) collective-permute-start(bf16[32,1024]{1,0:T(8,128)(2,1)} %get-tuple-element.72), channel_id=1, source_target_pairs={{0,1},{1,0},{2,3},{3,2},{4,5},{5,4},{6,7},{7,6},{8,9},{9,8},{10,11... | collective-permute-start | bytes 196616 | tf_op jit(solution)/shard_map/ppermute | solution.py:60
  12.3 6.9 %collective-permute-start.1 = (bf16[32,1024]{1,0:T(8,128)(2,1)}, bf16[32,1024]{1,0:T(8,128)(2,1)S(1)}, u32[]{:S(2)}, u32[]{:S(2)}) collective-permute-start(bf16[32,1024]{1,0:T(8,128)(2,1)} %get-tuple-element.73), channel_id=1, source_target_pairs={{0,2},{1,3},{2,0},{3,1},{4,6},{5,7},{6,4},{7,5},{8,10},{9,11},{10,... | collective-permute-start | bytes 196616 | tf_op jit(solution)/shard_map/ppermute | solution.py:60
  14.9 6.3 %collective-permute-start.2 = (bf16[32,1024]{1,0:T(8,128)(2,1)}, bf16[32,1024]{1,0:T(8,128)(2,1)S(1)}, u32[]{:S(2)}, u32[]{:S(2)}) collective-permute-start(bf16[32,1024]{1,0:T(8,128)(2,1)} %get-tuple-element.74), channel_id=1, source_target_pairs={{0,3},{1,2},{2,1},{3,0},{4,7},{5,6},{6,5},{7,4},{8,11},{9,10},{10,... | collective-permute-start | bytes 196616 | tf_op jit(solution)/shard_map/ppermute | solution.py:60
  22.9 8.5 %collective-permute-start.8 = (bf16[128,1024]{1,0:T(8,128)(2,1)S(1)}, bf16[128,1024]{1,0:T(8,128)(2,1)S(1)}, u32[]{:S(2)}, u32[]{:S(2)}) collective-permute-start(bf16[128,1024]{1,0:T(8,128)(2,1)S(1)} %get-tuple-element.77.refs_5_.refs_0_), channel_id=1, source_target_pairs={{0,8},{4,12},{8,0},{12,4},{1,9},{5,13},{9,1},{13,5},{2,10},{6,14},... | collective-permute-start | bytes 786440 | tf_op jit(solution)/shard_map/ppermute | solution.py:60
  23.5 5.5 %collective-permute-start.5 = (bf16[32,1024]{1,0:T(8,128)(2,1)S(1)}, bf16[32,1024]{1,0:T(8,128)(2,1)S(1)}, u32[]{:S(2)}, u32[]{:S(2)}) collective-permute-start(bf16[32,1024]{1,0:T(8,128)(2,1)S(1)} %get-tuple-element.76.refs_2_), channel_id=1, source_target_pairs={{0,1},{1,0},{2,3},{3,2},{4,5},{5,4},{6,7},{7,6},{8,9},{9,8},{10,11... | collective-permute-start | bytes 196616 | tf_op jit(solution)/shard_map/ppermute | solution.py:60
  23.5 5.5 %collective-permute-start.6 = (bf16[32,1024]{1,0:T(8,128)(2,1)S(1)}, bf16[32,1024]{1,0:T(8,128)(2,1)S(1)}, u32[]{:S(2)}, u32[]{:S(2)}) collective-permute-start(bf16[32,1024]{1,0:T(8,128)(2,1)S(1)} %get-tuple-element.76.refs_2_), channel_id=1, source_target_pairs={{0,2},{1,3},{2,0},{3,1},{4,6},{5,7},{6,4},{7,5},{8,10},{9,11},{10,... | collective-permute-start | bytes 196616 | tf_op jit(solution)/shard_map/ppermute | solution.py:60
  25.3 6.2 %collective-permute-start.7 = (bf16[32,1024]{1,0:T(8,128)(2,1)S(1)}, bf16[32,1024]{1,0:T(8,128)(2,1)S(1)}, u32[]{:S(2)}, u32[]{:S(2)}) collective-permute-start(bf16[32,1024]{1,0:T(8,128)(2,1)S(1)} %get-tuple-element.76.refs_2_), channel_id=1, source_target_pairs={{0,3},{1,2},{2,1},{3,0},{4,7},{5,6},{6,5},{7,4},{8,11},{9,10},{10,... | collective-permute-start | bytes 196616 | tf_op jit(solution)/shard_map/ppermute | solution.py:60
  32.3 6.8 %collective-permute-start.9 = (bf16[128,1152]{1,0:T(8,128)(2,1)S(1)}, bf16[128,1152]{1,0:T(8,128)(2,1)S(1)}, u32[]{:S(2)}, u32[]{:S(2)}) collective-permute-start(bf16[128,1152]{1,0:T(8,128)(2,1)S(1)} %place_second.1.refs_1_.refs_2_.refs_0_.refs_4_), channel_id=1, source_target_pairs={{0,8},{4,12},{8,0},{12,4},{1,9},{5,13},{9,1},{13,5},{2,10},{6,14},... | collective-permute-start | bytes 884744 | tf_op jit(solution)/shard_map/ppermute | solution.py:60
  33.9 9.6 %collective-permute-start.10 = (bf16[128,1152]{1,0:T(8,128)(2,1)S(1)}, bf16[128,1152]{1,0:T(8,128)(2,1)S(1)}, u32[]{:S(2)}, u32[]{:S(2)}) collective-permute-start(bf16[128,1152]{1,0:T(8,128)(2,1)S(1)} %place_second.1.refs_1_.refs_2_.refs_0_.refs_4_), channel_id=1, source_target_pairs={{0,4},{4,0},{8,12},{12,8},{1,5},{5,1},{9,13},{13,9},{2,6},{6,2},{1... | collective-permute-start | bytes 884744 | tf_op jit(solution)/shard_map/ppermute | solution.py:60
  39.1 4.4 %collective-permute-start.11 = (bf16[128,1152]{1,0:T(8,128)(2,1)S(1)}, bf16[128,1152]{1,0:T(8,128)(2,1)S(1)}, u32[]{:S(2)}, u32[]{:S(2)}) collective-permute-start(bf16[128,1152]{1,0:T(8,128)(2,1)S(1)} %collective-permute-done.9.refs_2_.refs_1_), channel_id=1, source_target_pairs={{0,4},{4,0},{8,12},{12,8},{1,5},{5,1},{9,13},{13,9},{2,6},{6,2},{1... | collective-permute-start | bytes 884744 | tf_op jit(solution)/shard_map/ppermute | solution.py:60
  39.6 15.6 %collective-permute-start.14 = (bf16[128,1152]{1,0:T(8,128)(2,1)S(1)}, bf16[128,1152]{1,0:T(8,128)(2,1)S(1)}, u32[]{:S(2)}, u32[]{:S(2)}) collective-permute-start(bf16[128,1152]{1,0:T(8,128)(2,1)S(1)} %place_second.1.refs_1_.refs_2_.refs_0_.refs_4_), channel_id=1, source_target_pairs={{0,16},{16,0},{1,17},{17,1},{2,18},{18,2},{3,19},{19,3},{4,20},{20... | collective-permute-start | bytes 884744 | tf_op jit(solution)/shard_map/ppermute | solution.py:60
  41.1 15.2 %collective-permute-start.15 = (bf16[128,1152]{1,0:T(8,128)(2,1)S(1)}, bf16[128,1152]{1,0:T(8,128)(2,1)S(1)}, u32[]{:S(2)}, u32[]{:S(2)}) collective-permute-start(bf16[128,1152]{1,0:T(8,128)(2,1)S(1)} %place_second.1.refs_1_.refs_2_.refs_0_.refs_4_), channel_id=1, source_target_pairs={{0,24},{4,28},{8,16},{12,20},{16,8},{20,12},{24,0},{28,4},{1,25},{... | collective-permute-start | bytes 884744 | tf_op jit(solution)/shard_map/ppermute | solution.py:66
  63.4 10.4 %collective-permute-start.16 = (bf16[256,1024]{1,0:T(8,128)(2,1)S(1)}, bf16[256,1024]{1,0:T(8,128)(2,1)S(1)}, u32[]{:S(2)}, u32[]{:S(2)}) collective-permute-start(bf16[256,1024]{1,0:T(8,128)(2,1)S(1)} %get-tuple-element.83), channel_id=1, source_target_pairs={{0,4},{4,0},{8,12},{12,8},{1,5},{5,1},{9,13},{13,9},{2,6},{6,2},{1... | collective-permute-start | bytes 1572872 | tf_op jit(solution)/shard_map/ppermute | solution.py:60
  64.0 9.1 %collective-permute-start.18 = (bf16[128,1152]{1,0:T(8,128)(2,1)S(1)}, bf16[128,1152]{1,0:T(8,128)(2,1)S(1)}, u32[]{:S(2)}, u32[]{:S(2)}) collective-permute-start(bf16[128,1152]{1,0:T(8,128)(2,1)S(1)} %add_convert_fusion), channel_id=1, source_target_pairs={{0,8},{4,12},{8,0},{12,4},{1,9},{5,13},{9,1},{13,5},{2,10},{6,14},... | collective-permute-start | bytes 884744 | tf_op jit(solution)/shard_map/ppermute | solution.py:60
  73.8 9.8 %collective-permute-start.23 = (bf16[128,1024]{1,0:T(8,128)(2,1)S(1)}, bf16[128,1024]{1,0:T(8,128)(2,1)S(1)}, u32[]{:S(2)}, u32[]{:S(2)}) collective-permute-start(bf16[128,1024]{1,0:T(8,128)(2,1)S(1)} %half.1), channel_id=1, source_target_pairs={{0,8},{4,12},{8,0},{12,4},{1,9},{5,13},{9,1},{13,5},{2,10},{6,14},... | collective-permute-start | bytes 786440 | tf_op jit(solution)/shard_map/ppermute | solution.py:60
  74.4 8.7 %collective-permute-start.24 = (bf16[32,1152]{1,0:T(8,128)(2,1)S(1)}, bf16[32,1152]{1,0:T(8,128)(2,1)S(1)}, u32[]{:S(2)}, u32[]{:S(2)}) collective-permute-start(bf16[32,1152]{1,0:T(8,128)(2,1)S(1)} %get-tuple-element.87), channel_id=1, source_target_pairs={{0,1},{1,0},{2,3},{3,2},{4,5},{5,4},{6,7},{7,6},{8,9},{9,8},{10,11... | collective-permute-start | bytes 221192 | tf_op jit(solution)/shard_map/ppermute | solution.py:60
  75.0 8.1 %collective-permute-start.25 = (bf16[32,1152]{1,0:T(8,128)(2,1)S(1)}, bf16[32,1152]{1,0:T(8,128)(2,1)S(1)}, u32[]{:S(2)}, u32[]{:S(2)}) collective-permute-start(bf16[32,1152]{1,0:T(8,128)(2,1)S(1)} %get-tuple-element.88), channel_id=1, source_target_pairs={{0,2},{1,3},{2,0},{3,1},{4,6},{5,7},{6,4},{7,5},{8,10},{9,11},{10,... | collective-permute-start | bytes 221192 | tf_op jit(solution)/shard_map/ppermute | solution.py:60
  77.4 6.2 %collective-permute-start.26 = (bf16[32,1152]{1,0:T(8,128)(2,1)S(1)}, bf16[32,1152]{1,0:T(8,128)(2,1)S(1)}, u32[]{:S(2)}, u32[]{:S(2)}) collective-permute-start(bf16[32,1152]{1,0:T(8,128)(2,1)S(1)} %get-tuple-element.89), channel_id=1, source_target_pairs={{0,3},{1,2},{2,1},{3,0},{4,7},{5,6},{6,5},{7,4},{8,11},{9,10},{10,... | collective-permute-start | bytes 221192 | tf_op jit(solution)/shard_map/ppermute | solution.py:60
  85.0 10.5 %collective-permute-start.27 = (bf16[32,2176]{1,0:T(8,128)(2,1)S(1)}, bf16[32,2176]{1,0:T(8,128)(2,1)S(1)}, u32[]{:S(2)}, u32[]{:S(2)}) collective-permute-start(bf16[32,2176]{1,0:T(8,128)(2,1)S(1)} %get-tuple-element.99), channel_id=1, source_target_pairs={{0,1},{1,0},{2,3},{3,2},{4,5},{5,4},{6,7},{7,6},{8,9},{9,8},{10,11... | collective-permute-start | bytes 417800 | tf_op jit(solution)/shard_map/ppermute | solution.py:60
  85.1 12.0 %collective-permute-start.28 = (bf16[32,2176]{1,0:T(8,128)(2,1)S(1)}, bf16[32,2176]{1,0:T(8,128)(2,1)S(1)}, u32[]{:S(2)}, u32[]{:S(2)}) collective-permute-start(bf16[32,2176]{1,0:T(8,128)(2,1)S(1)} %get-tuple-element.100), channel_id=1, source_target_pairs={{0,2},{1,3},{2,0},{3,1},{4,6},{5,7},{6,4},{7,5},{8,10},{9,11},{10,... | collective-permute-start | bytes 417800 | tf_op jit(solution)/shard_map/ppermute | solution.py:60
  87.6 9.5 %collective-permute-start.29 = (bf16[32,2176]{1,0:T(8,128)(2,1)S(1)}, bf16[32,2176]{1,0:T(8,128)(2,1)S(1)}, u32[]{:S(2)}, u32[]{:S(2)}) collective-permute-start(bf16[32,2176]{1,0:T(8,128)(2,1)S(1)} %get-tuple-element.101), channel_id=1, source_target_pairs={{0,3},{1,2},{2,1},{3,0},{4,7},{5,6},{6,5},{7,4},{8,11},{9,10},{10,... | collective-permute-start | bytes 417800 | tf_op jit(solution)/shard_map/ppermute | solution.py:60
  100.5 9.0 %collective-permute-start.30 = (bf16[32,2048]{1,0:T(8,128)(2,1)S(1)}, bf16[32,2048]{1,0:T(8,128)(2,1)S(1)}, u32[]{:S(2)}, u32[]{:S(2)}) collective-permute-start(bf16[32,2048]{1,0:T(8,128)(2,1)S(1)} %get-tuple-element.106), channel_id=1, source_target_pairs={{0,1},{1,0},{2,3},{3,2},{4,5},{5,4},{6,7},{7,6},{8,9},{9,8},{10,11... | collective-permute-start | bytes 393224 | tf_op jit(solution)/shard_map/ppermute | solution.py:60
  103.2 16.3 %collective-permute-start.34 = (bf16[128,896]{1,0:T(8,128)(2,1)S(1)}, bf16[128,896]{1,0:T(8,128)(2,1)S(1)}, u32[]{:S(2)}, u32[]{:S(2)}) collective-permute-start(bf16[128,896]{1,0:T(8,128)(2,1)S(1)} %get-tuple-element.113), channel_id=1, source_target_pairs={{0,16},{4,20},{8,24},{12,28},{16,0},{20,4},{24,8},{28,12},{1,17},{... | collective-permute-start | bytes 688136 | tf_op jit(solution)/shard_map/ppermute | solution.py:66
  104.7 14.7 %collective-permute-start.35 = (bf16[128,896]{1,0:T(8,128)(2,1)S(1)}, bf16[128,896]{1,0:T(8,128)(2,1)S(1)}, u32[]{:S(2)}, u32[]{:S(2)}) collective-permute-start(bf16[128,896]{1,0:T(8,128)(2,1)S(1)} %get-tuple-element.114), channel_id=1, source_target_pairs={{0,8},{4,12},{8,0},{12,4},{16,24},{20,28},{24,16},{28,20},{1,9},{5... | collective-permute-start | bytes 688136 | tf_op jit(solution)/shard_map/ppermute | solution.py:66
  106.3 13.2 %collective-permute-start.36 = (bf16[128,896]{1,0:T(8,128)(2,1)S(1)}, bf16[128,896]{1,0:T(8,128)(2,1)S(1)}, u32[]{:S(2)}, u32[]{:S(2)}) collective-permute-start(bf16[128,896]{1,0:T(8,128)(2,1)S(1)} %get-tuple-element.115), channel_id=1, source_target_pairs={{0,24},{4,28},{8,16},{12,20},{16,8},{20,12},{24,0},{28,4},{1,25},{... | collective-permute-start | bytes 688136 | tf_op jit(solution)/shard_map/ppermute | solution.py:66
  106.8 12.7 %collective-permute-start.31 = (bf16[32,2048]{1,0:T(8,128)(2,1)S(1)}, bf16[32,2048]{1,0:T(8,128)(2,1)S(1)}, u32[]{:S(2)}, u32[]{:S(2)}) collective-permute-start(bf16[32,2048]{1,0:T(8,128)(2,1)S(1)} %get-tuple-element.107), channel_id=1, source_target_pairs={{0,2},{1,3},{2,0},{3,1},{4,6},{5,7},{6,4},{7,5},{8,10},{9,11},{10,... | collective-permute-start | bytes 393224 | tf_op jit(solution)/shard_map/ppermute | solution.py:60
  109.5 10.0 %collective-permute-start.32 = (bf16[32,2048]{1,0:T(8,128)(2,1)S(1)}, bf16[32,2048]{1,0:T(8,128)(2,1)S(1)}, u32[]{:S(2)}, u32[]{:S(2)}) collective-permute-start(bf16[32,2048]{1,0:T(8,128)(2,1)S(1)} %get-tuple-element.108), channel_id=1, source_target_pairs={{0,3},{1,2},{2,1},{3,0},{4,7},{5,6},{6,5},{7,4},{8,11},{9,10},{10,... | collective-permute-start | bytes 393224 | tf_op jit(solution)/shard_map/ppermute | solution.py:60
  121.0 4.5 %collective-permute-start.37 = (bf16[32,1152]{1,0:T(8,128)(2,1)S(1)}, bf16[32,1152]{1,0:T(8,128)(2,1)S(1)}, u32[]{:S(2)}, u32[]{:S(2)}) collective-permute-start(bf16[32,1152]{1,0:T(8,128)(2,1)S(1)} %input_grad.1.refs_5_), channel_id=1, source_target_pairs={{0,1},{1,0},{2,3},{3,2},{4,5},{5,4},{6,7},{7,6},{8,9},{9,8},{10,11... | collective-permute-start | bytes 221192 | tf_op jit(solution)/shard_map/ppermute | solution.py:60
  123.1 6.1 %collective-permute-start.38 = (bf16[32,1152]{1,0:T(8,128)(2,1)S(1)}, bf16[32,1152]{1,0:T(8,128)(2,1)S(1)}, u32[]{:S(2)}, u32[]{:S(2)}) collective-permute-start(bf16[32,1152]{1,0:T(8,128)(2,1)S(1)} %input_grad.1.refs_5_), channel_id=1, source_target_pairs={{0,2},{1,3},{2,0},{3,1},{4,6},{5,7},{6,4},{7,5},{8,10},{9,11},{10,... | collective-permute-start | bytes 221192 | tf_op jit(solution)/shard_map/ppermute | solution.py:60
  123.7 6.3 %collective-permute-start.39 = (bf16[32,1152]{1,0:T(8,128)(2,1)S(1)}, bf16[32,1152]{1,0:T(8,128)(2,1)S(1)}, u32[]{:S(2)}, u32[]{:S(2)}) collective-permute-start(bf16[32,1152]{1,0:T(8,128)(2,1)S(1)} %input_grad.1.refs_5_), channel_id=1, source_target_pairs={{0,3},{1,2},{2,1},{3,0},{4,7},{5,6},{6,5},{7,4},{8,11},{9,10},{10,... | collective-permute-start | bytes 221192 | tf_op jit(solution)/shard_map/ppermute | solution.py:60
  (33 other events, 285.2 us)
